TPU v7x, 128 devices: a whole 4x4x4 slice. The times are simulated.
128 devices in a mesh: pipe: 2 (over x_lo), patch: 32 (over z, y, core), head: 2 (over x_hi).
Axes of the slice: x: 4 (x_hi: 2, x_lo: 2; x = x_hi * 2 + x_lo), y: 4, z: 4, core: 2. Of those that a mesh axis runs over, the one named last changes fastest.
Arguments:
- queries: bfloat16 [2, 6144, 2560], P('pipe', ('patch', 'head')), may hold values from -40 to 40
- fresh_keys: bfloat16 [2, 6144, 2560], P('pipe', ('patch', 'head')), may hold values from -6 to 6
- fresh_values: bfloat16 [2, 6144, 2560], P('pipe', ('patch', 'head')), may hold values from -6 to 6
- stale_keys: bfloat16 [2, 6144, 2560], P('pipe', 'patch', 'head'), may hold values from -40 to 40
- stale_values: bfloat16 [2, 6144, 2560], P('pipe', 'patch', 'head'), may hold values from -6 to 6
- out_weight: bfloat16 [2, 2560, 5120], P('pipe', 'head'), may hold values from -0.5 to 0.5
- out_gate: float32 [2, 5120], P('pipe'), may hold values from 0.5 to 2
Outputs:
- new_keys: bfloat16 [2, 6144, 2560], P('pipe', 'patch', 'head')
- new_values: bfloat16 [2, 6144, 2560], P('pipe', 'patch', 'head')
- onward: bfloat16 [2, 6144, 5120], P('pipe', ('patch', 'head'))
All inputs are finite; a program needn't handle non-finite values.
Results may differ from a plain program's by a relative error of at most 0.014.
Values may be sent and summed in bfloat16 or wider, within the bound.
No kernel may reach another device: no remote copies, remote signals or barrier semaphores. Data moves between devices by JAX's collectives and lax.ppermute only.
A program may use at most 192 MiB of HBM per device.

v0:
```python
import jax
import jax.numpy as jnp
from jax import lax
from jax.sharding import PartitionSpec as P

HEAD_DIM = 128


def passed_along(value, axis, steps):
    count = lax.axis_size(axis)
    pairs = [(source, (source + steps) % count) for source in range(count)]
    return lax.ppermute(value, axis, pairs)


def per_device(queries, fresh_keys, fresh_values, stale_keys, stale_values, out_weight, out_gate):
    score_scale = HEAD_DIM ** (-0.5)
    query_local, key_local, value_local = (
        lax.all_to_all(queries[0], "head", split_axis=1, concat_axis=0, tiled=True),
        lax.all_to_all(fresh_keys[0], "head", split_axis=1, concat_axis=0, tiled=True),
        lax.all_to_all(fresh_values[0], "head", split_axis=1, concat_axis=0, tiled=True),
    )
    patch_rows = query_local.shape[0]
    local_heads = query_local.shape[1] // HEAD_DIM
    query_heads = query_local.reshape(patch_rows, local_heads, HEAD_DIM)
    own_start = lax.axis_index("patch") * patch_rows
    stale_all = (
        lax.all_gather(stale_keys[0], "patch", axis=0, tiled=True),
        lax.all_gather(stale_values[0], "patch", axis=0, tiled=True),
    )
    keys_used = lax.dynamic_update_slice_in_dim(stale_all[0], key_local, own_start, 0)
    values_used = lax.dynamic_update_slice_in_dim(stale_all[1], value_local, own_start, 0)
    key_heads = keys_used.reshape(keys_used.shape[0], local_heads, HEAD_DIM)
    scores = (
        jnp.einsum("qhd,khd->hqk", query_heads, key_heads, preferred_element_type=jnp.float32)
        * score_scale
    )
    row_top = jnp.max(scores, axis=-1)
    weights = jnp.exp(scores - row_top[:, :, None])
    row_total = jnp.sum(weights, axis=-1)
    value_heads = values_used.reshape(values_used.shape[0], local_heads, HEAD_DIM)
    numerator = jnp.einsum(
        "hqk,khd->qhd",
        weights.astype(jnp.bfloat16),
        value_heads,
        preferred_element_type=jnp.float32,
    )
    attended = (numerator / jnp.transpose(row_total)[:, :, None]).reshape(
        patch_rows, local_heads * HEAD_DIM
    )
    attended = attended.astype(jnp.bfloat16)
    weight_local = out_weight[0]
    summed = lax.psum_scatter(
        jnp.dot(attended, weight_local, preferred_element_type=jnp.float32).astype(jnp.bfloat16),
        "head",
        scatter_dimension=0,
        tiled=True,
    ).astype(jnp.float32)
    result = (summed * out_gate[0][None, :]).astype(jnp.bfloat16)
    handed = passed_along(result, "pipe", 1)
    return (key_local[None], value_local[None], handed[None])


def solution(mesh):
    in_specs = (
        P("pipe", ("patch", "head"), None),
        P("pipe", ("patch", "head"), None),
        P("pipe", ("patch", "head"), None),
        P("pipe", "patch", "head"),
        P("pipe", "patch", "head"),
        P("pipe", "head", None),
        P("pipe", None),
    )
    out_specs = (
        P("pipe", "patch", "head"),
        P("pipe", "patch", "head"),
        P("pipe", ("patch", "head"), None),
    )
    return jax.shard_map(
        per_device, mesh=mesh, in_specs=in_specs, out_specs=out_specs, check_vma=False
    )
```

profile of v0, /device:TPU:0, one launch (start us, length us, event | category | flops | bytes accessed | tf_op | source)
XLA Modules:
  0.0 281.8 jit_solution(16977289024115810617)
XLA Ops:
  7.2 0.0 all-gather.7.cloned.1.call-start
  7.2 0.7 all-gather.7.cloned.1.call-update
  7.9 0.0 all-gather.5.cloned.1.call-start
  7.9 0.7 all-gather.5.cloned.1.call-update
  8.6 1.1 all_to_all.40
  9.8 0.8 copy.58
  10.6 4.4 %all-to-all-start = ((bf16[96,2,1280]{2,0,1:T(8,128)(2,1)}), bf16[96,2,1280]{2,0,1:T(8,128)(2,1)S(1)}, u32[]{:S(2)}, u32[]{:S(2)}) async-start(bf16[96,2,1280]{2,0,1:T(8,128)(2,1)} %copy.58), calls=%async_computation | async-start | bytes 983040 | tf_op jit(solution)/shard_map/all_to_all | solution.py:19
  15.0 1.1 all_to_all.48
  16.1 0.8 copy.64
  17.0 7.2 %all-to-all-done = bf16[96,2,1280]{2,0,1:T(8,128)(2,1)S(1)} async-done(((bf16[96,2,1280]{2,0,1:T(8,128)(2,1)}), bf16[96,2,1280]{2,0,1:T(8,128)(2,1)S(1)}, u32[]{:S(2)}, u32[]{:S(2)}) %all-to-all-start) | async-done | bytes 491552 | tf_op jit(solution)/shard_map/all_to_all | solution.py:19
  24.1 3.5 %all-to-all-start.2 = ((bf16[96,2,1280]{2,0,1:T(8,128)(2,1)}), bf16[96,2,1280]{2,0,1:T(8,128)(2,1)S(1)}, u32[]{:S(2)}, u32[]{:S(2)}) async-start(bf16[96,2,1280]{2,0,1:T(8,128)(2,1)} %copy.64), calls=%async_computation.2 | async-start | bytes 983040 | tf_op jit(solution)/shard_map/all_to_all | solution.py:18
  27.6 1.1 all_to_all.43
  28.8 0.8 copy.59
  29.6 6.2 %all-to-all-done.2 = bf16[96,2,1280]{2,0,1:T(8,128)(2,1)S(1)} async-done(((bf16[96,2,1280]{2,0,1:T(8,128)(2,1)}), bf16[96,2,1280]{2,0,1:T(8,128)(2,1)S(1)}, u32[]{:S(2)}, u32[]{:S(2)}) %all-to-all-start.2) | async-done | bytes 491552 | tf_op jit(solution)/shard_map/all_to_all | solution.py:18
  35.8 3.5 %all-to-all-start.1 = ((bf16[96,2,1280]{2,0,1:T(8,128)(2,1)}), bf16[96,2,1280]{2,0,1:T(8,128)(2,1)S(1)}, u32[]{:S(2)}, u32[]{:S(2)}) async-start(bf16[96,2,1280]{2,0,1:T(8,128)(2,1)} %copy.59), calls=%async_computation.1 | async-start | bytes 983040 | tf_op jit(solution)/shard_map/all_to_all | solution.py:20
  39.3 0.0 reduce-scatter.2.cloned.1.call-start
  39.4 0.2 copy.63
  39.6 0.3 reshape.36
  39.9 7.3 %all-to-all-done.1 = bf16[96,2,1280]{2,0,1:T(8,128)(2,1)S(1)} async-done(((bf16[96,2,1280]{2,0,1:T(8,128)(2,1)}), bf16[96,2,1280]{2,0,1:T(8,128)(2,1)S(1)}, u32[]{:S(2)}, u32[]{:S(2)}) %all-to-all-start.1) | async-done | bytes 491552 | tf_op jit(solution)/shard_map/all_to_all | solution.py:20
  47.2 0.2 copy.61
  47.4 35.6 %all-gather.7.cloned.1.call-done = bf16[1,6144,1280]{2,1,0:T(8,128)(2,1)} async-done(((bf16[1,192,1280]{2,1,0:T(8,128)(2,1)}), bf16[1,6144,1280]{2,1,0:T(8,128)(2,1)}) %all-gather.7.cloned.1.call-update) | async-done | bytes 15728656 | tf_op jit(solution)/shard_map/all_gather | solution.py:27
  83.1 20.5 %copy.62 = bf16[1,6144,1280]{1,2,0:T(8,128)(2,1)} copy(bf16[1,6144,1280]{2,1,0:T(8,128)(2,1)} %all-gather.7.cloned.1.call-done) | data formatting | bytes 31457280 | tf_op jit(solution)/shard_map/all_gather | solution.py:27
  103.6 6.8 %dynamic_update_slice.7 = bf16[6144,1280]{0,1:T(8,128)(2,1)} dynamic-update-slice(bf16[6144,1280]{0,1:T(8,128)(2,1)} %bitcast.49, bf16[192,1280]{0,1:T(8,128)(2,1)S(1)} %copy.63, s32[]{:T(128)S(6)} %select_n.4, s32[]{:T(128)} %constant.5.clone.1) | dynamic-update-slice | bytes 983044 | tf_op jit(solution)/shard_map/dynamic_update_slice | solution.py:30
  110.4 22.7 %bitcast_reduce_fusion = (f32[10,192]{1,0:T(8,128)S(1)}, f32[10,6144,192]{1,2,0:T(8,128)}) fusion(bf16[6144,10,128]{0,2,1:T(8,128)(2,1)} %bitcast.50, bf16[192,10,128]{2,1,0:T(8,128)(2,1)S(1)} %reshape.36), kind=kOutput, calls=%fused_computation.1 | convolution fusion | flops 3043489792 | bytes 63413760 | tf_op jit(solution)/shard_map/qhd,khd->hqk/dot_general | solution.py:34
  133.1 21.1 %fusion.1 = f32[10,192]{1,0:T(8,128)S(1)} fusion(f32[10,6144,192]{1,2,0:T(8,128)} %get-tuple-element.4, f32[10,192]{1,0:T(8,128)S(1)} %get-tuple-element.3), kind=kLoop, calls=%fused_computation.3 | loop fusion | flops 35387520 | bytes 47201280 | tf_op jit(solution)/shard_map/reduce_sum | solution.py:39
  154.2 0.9 all-gather.5.cloned.1.call-done
  155.1 20.5 %copy.60 = bf16[1,6144,1280]{1,2,0:T(8,128)(2,1)} copy(bf16[1,6144,1280]{2,1,0:T(8,128)(2,1)} %all-gather.5.cloned.1.call-done) | data formatting | bytes 31457280 | tf_op jit(solution)/shard_map/all_gather | solution.py:28
  175.6 6.8 %dynamic_update_slice.6 = bf16[6144,1280]{0,1:T(8,128)(2,1)} dynamic-update-slice(bf16[6144,1280]{0,1:T(8,128)(2,1)} %bitcast.51, bf16[192,1280]{0,1:T(8,128)(2,1)S(1)} %copy.61, s32[]{:T(128)S(6)} %select_n.4, s32[]{:T(128)} %constant.5.clone.1) | dynamic-update-slice | bytes 983044 | tf_op jit(solution)/shard_map/dynamic_update_slice | solution.py:31
  182.4 21.6 %fusion.18 = bf16[192,10,128]{2,0,1:T(8,128)(2,1)S(1)} fusion(bf16[6144,10,128]{0,2,1:T(8,128)(2,1)} %bitcast.52, f32[10,6144,192]{1,2,0:T(8,128)} %get-tuple-element.4, f32[10,192]{1,0:T(8,128)S(1)} %get-tuple-element.3, f32[192,10]{0,1:T(8,128)S(1)} %bitcast.61), kind=kOutput, calls=%fused_computation.14 | convolution fusion | flops 3055779840 | bytes 63421440 | tf_op jit(solution)/shard_map/hqk,khd->qhd/dot_general | solution.py:41
  204.0 0.0 copy-start
  204.0 0.2 copy.68
  204.2 8.8 %fusion.9 = bf16[192,5120]{1,0:T(8,128)(2,1)} fusion(bf16[192,1280]{0,1:T(8,128)(2,1)S(1)} %bitcast.57, bf16[1,1280,5120]{2,1,0:T(8,128)(2,1)} %param.12), kind=kOutput, calls=%fused_computation.10 | convolution fusion | flops 2517565440 | bytes 15564800 | tf_op jit(solution)/shard_map/dot_general | solution.py:53
  213.0 0.0 reduce-scatter.2.cloned.1.call-update
  213.1 34.7 %reduce-scatter.2.cloned.1.call-done = bf16[96,5120]{1,0:T(8,128)(2,1)} async-done(((bf16[192,5120]{1,0:T(8,128)(2,1)}), bf16[96,5120]{1,0:T(8,128)(2,1)}) %reduce-scatter.2.cloned.1.call-update) | async-done | bytes 983056 | tf_op jit(solution)/shard_map/reduce_scatter | solution.py:52
  247.8 0.0 copy-done
  247.8 1.4 multiply_convert_fusion
  249.2 0.6 collective-permute-start
  249.8 22.9 %collective-permute-done = bf16[96,5120]{1,0:T(8,128)(2,1)S(1)} collective-permute-done((bf16[96,5120]{1,0:T(8,128)(2,1)S(1)}, bf16[96,5120]{1,0:T(8,128)(2,1)S(1)}, u32[]{:S(2)}, u32[]{:S(2)}) %collective-permute-start) | collective-permute-done | bytes 983072 | tf_op jit(solution)/shard_map/ppermute | solution.py:12
  272.8 0.8 copy.80
  273.5 0.8 copy.81
  274.3 0.9 copy.82
Async XLA Ops:
  7.2 75.9 %all-gather.7.cloned.1.call-start = ((), (), s32[]{:S(2)}) async-start(), calls=%async_computation.6 | async-start | bytes 16220160 | tf_op jit(solution)/shard_map/all_gather | solution.py:27
  7.9 147.2 %all-gather.5.cloned.1.call-start = ((), (), s32[]{:S(2)}) async-start(), calls=%async_computation.5 | async-start | bytes 16220160 | tf_op jit(solution)/shard_map/all_gather | solution.py:28
  10.6 13.5 %all-to-all-start = ((bf16[96,2,1280]{2,0,1:T(8,128)(2,1)}), bf16[96,2,1280]{2,0,1:T(8,128)(2,1)S(1)}, u32[]{:S(2)}, u32[]{:S(2)}) async-start(bf16[96,2,1280]{2,0,1:T(8,128)(2,1)} %copy.58), calls=%async_computation | async-start | bytes 983040 | tf_op jit(solution)/shard_map/all_to_all | solution.py:19
  24.1 11.7 %all-to-all-start.2 = ((bf16[96,2,1280]{2,0,1:T(8,128)(2,1)}), bf16[96,2,1280]{2,0,1:T(8,128)(2,1)S(1)}, u32[]{:S(2)}, u32[]{:S(2)}) async-start(bf16[96,2,1280]{2,0,1:T(8,128)(2,1)} %copy.64), calls=%async_computation.2 | async-start | bytes 983040 | tf_op jit(solution)/shard_map/all_to_all | solution.py:18
  35.8 11.4 %all-to-all-start.1 = ((bf16[96,2,1280]{2,0,1:T(8,128)(2,1)}), bf16[96,2,1280]{2,0,1:T(8,128)(2,1)S(1)}, u32[]{:S(2)}, u32[]{:S(2)}) async-start(bf16[96,2,1280]{2,0,1:T(8,128)(2,1)} %copy.59), calls=%async_computation.1 | async-start | bytes 983040 | tf_op jit(solution)/shard_map/all_to_all | solution.py:20
  39.3 208.5 %reduce-scatter.2.cloned.1.call-start = ((), (), s32[]{:S(2)}) async-start(), calls=%async_computation.4 | async-start | bytes 2949120 | tf_op jit(solution)/shard_map/reduce_scatter | solution.py:52
  204.0 43.8 %copy-start = (f32[1,5120]{1,0:T(1,128)S(1)}, f32[1,5120]{1,0:T(1,128)}, u32[]{:S(2)}) copy-start(f32[1,5120]{1,0:T(1,128)} %param.13) | copy-start | bytes 61444
  249.2 23.6 %collective-permute-start = (bf16[96,5120]{1,0:T(8,128)(2,1)S(1)}, bf16[96,5120]{1,0:T(8,128)(2,1)S(1)}, u32[]{:S(2)}, u32[]{:S(2)}) collective-permute-start(bf16[96,5120]{1,0:T(8,128)(2,1)S(1)} %multiply_convert_fusion), channel_id=1, source_target_pairs={{0,64},{64,0},{1,65},{65,1},{2,66},{66,2},{3,67},{67,3},{4,68},{68... | collective-permute-start | bytes 2949128 | tf_op jit(solution)/shard_map/ppermute | solution.py:12
Sparse Core Ops, SparseCore 0:
  10.3 72.7 all-gather.6
  85.3 69.7 all-gather.4
  213.2 34.5 reduce-scatter.1
where the time goes:
time: 284 us; the launch traced here: 282 us
  waiting for transfers between devices  116 us (41%)
  local copies, waits for them, and re-layouts  64.1 us (23%)
  matrix products  53.1 us (19%)
  other arithmetic  22.4 us (8%)
  between operations  13.8 us (5%)
  starting transfers between devices  12.1 us (4%)
    all_gather x1, waiting for transfers between devices, per_device(): lax.all_gather(stale_keys[0], 'patch', axis=0, tiled=True)  35.6 us
    reduce_scatter x1, waiting for transfers between devices, per_device(): lax.psum_scatter(jnp.dot(attended, weight_local, preferred_element_type=j...  34.7 us
    ppermute x1, waiting for transfers between devices, passed_along(): return lax.ppermute(value, axis, pairs)  22.9 us
    dot_general x1, matrix products, per_device(): jnp.einsum('qhd,khd->hqk', query_heads, key_heads, preferred_element_type...  22.7 us
    dot_general x1, matrix products, per_device(): jnp.einsum('hqk,khd->qhd', weights.astype(jnp.bfloat16), value_heads, pre...  21.6 us
    reduce_sum x1, other arithmetic, per_device(): row_total = jnp.sum(weights, axis=-1)  21.1 us
    all_gather x1, local copies, waits for them, and re-layouts, per_device(): lax.all_gather(stale_keys[0], 'patch', axis=0, tiled=True)  20.5 us
    all_gather x1, local copies, waits for them, and re-layouts, per_device(): lax.all_gather(stale_values[0], 'patch', axis=0, tiled=True)  20.5 us
  transfers between devices with their start and end apart: 7, of which 7 were waited for; matrix products, arithmetic and copies ran while one was open for 26% of the time, Pallas kernels for 0%

commit v1 on v0

v1 whole, which is shorter than its diff:
```python
import functools
import math
import jax
import jax.numpy as jnp
from jax import lax
from jax.experimental import pallas as pl
from jax.experimental.pallas import tpu as pltpu
from jax.sharding import PartitionSpec as P

HEAD_DIM = 128
CHIPS = 4
SCALE_LOG2 = HEAD_DIM ** (-0.5) / math.log(2.0)
BF = jnp.bfloat16
F32 = jnp.float32
VMEM_LIMIT = 40 * 1024 * 1024


def place(z, y, core):
    return ((z % CHIPS) * CHIPS + y % CHIPS) * 2 + core


def along(value, steps, core_on_y):
    pairs = []
    for z in range(CHIPS):
        for y in range(CHIPS):
            for core in range(2):
                to = place(z, y + steps, core) if core == core_on_y else place(z + steps, y, core)
                pairs.append((place(z, y, core), to))
    return lax.ppermute(value, "patch", pairs)


def keys_along(value, steps):
    return along(value, steps, 0)


def queries_along(value, steps):
    return along(value, steps, 1)


def other_core(value):
    return lax.ppermute(value, "patch", [(i, i ^ 1) for i in range(2 * CHIPS * CHIPS)])


def other_half(value, core, head):
    pairs = [
        (b * 2 + h, (b ^ core) * 2 + (h ^ head)) for b in range(2 * CHIPS * CHIPS) for h in range(2)
    ]
    return lax.ppermute(value, ("patch", "head"), pairs)


def onward_to(value, head):
    pairs = [(p * 2 + h, (1 - p) * 2 + (h ^ head)) for p in range(2) for h in range(2)]
    return lax.ppermute(value, ("pipe", "head"), pairs)


def params(**kw):
    return pltpu.CompilerParams(vmem_limit_bytes=VMEM_LIMIT, **kw)


def cost(flops, nbytes, trans=0):
    return pl.CostEstimate(flops=flops, bytes_accessed=nbytes, transcendentals=trans)


def column_blocks(arrays, places, width):
    rows = [arrays[a].shape[0] for a, _ in places]
    table = jnp.stack([jnp.asarray(p, jnp.int32) for _, p in places])
    n = len(places)

    def body(table_ref, *refs):
        for i in range(n):
            refs[n + i][...] = refs[i][...]

    return pl.pallas_call(
        body,
        grid_spec=pltpu.PrefetchScalarGridSpec(
            num_scalar_prefetch=1,
            grid=(1,),
            in_specs=[
                pl.BlockSpec((rows[i], width), functools.partial(lambda i, g, t: (0, t[i]), i))
                for i in range(n)
            ],
            out_specs=[pl.BlockSpec((rows[i], width), lambda g, t: (0, 0)) for i in range(n)],
        ),
        out_shape=[jax.ShapeDtypeStruct((rows[i], width), arrays[0].dtype) for i in range(n)],
        compiler_params=params(),
    )(table, *[arrays[a] for a, _ in places])


def nt(a, b):
    return lax.dot_general(a, b, (((1,), (1,)), ((), ())), preferred_element_type=F32)


def scores_max(pieces):
    by_width = {}
    for s in pieces:
        w = s.shape[1]
        by_width[w] = s if w not in by_width else jnp.maximum(by_width[w], s)
    top = None
    for s in by_width.values():
        t = jnp.max(s, axis=1, keepdims=True)
        top = t if top is None else jnp.maximum(top, t)
    return top


def attend(q, keys, values, state):
    pieces = [nt(q, k) for k in keys]
    top = scores_max(pieces)
    if state is not None:
        top = jnp.maximum(top, state[0])
    sums = None
    for s, v in zip(pieces, values):
        w = jnp.exp2((s - top) * SCALE_LOG2).astype(BF)
        ones = jnp.ones(v.shape, BF)
        part = jnp.dot(w, jnp.concatenate([v, ones], axis=1), preferred_element_type=F32)
        sums = part if sums is None else sums + part
    total = sums[:, HEAD_DIM : HEAD_DIM + 1]
    sums = sums[:, :HEAD_DIM]
    if state is not None:
        keep = jnp.exp2((state[0] - top) * SCALE_LOG2)
        total = total + keep * state[1]
        sums = sums + keep * state[2]
    return top, total, sums


def lane(x, shape):
    return lax.broadcasted_iota(jnp.int32, shape, 1) == x


def first_kernel(row_sets, n_keys, *refs):
    n_q = len(row_sets)
    q_refs = refs[:n_q]
    k_refs = refs[n_q : n_q + n_keys]
    v_refs = refs[n_q + n_keys : n_q + 2 * n_keys]
    s_refs = refs[n_q + 2 * n_keys : 2 * n_q + 2 * n_keys]
    t_refs = refs[2 * n_q + 2 * n_keys :]
    head = pl.program_id(0)
    for i in range(n_q):
        for lo, hi, use in row_sets[i]:
            ks = [k_refs[j][a:b, :] for j, a, b in use]
            vs = [v_refs[j][a:b, :] for j, a, b in use]
            top, total, sums = attend(q_refs[i][lo:hi, :], ks, vs, None)
            s_refs[i][lo:hi, :] = sums
            shape = (hi - lo, HEAD_DIM)
            old = jnp.where(head == 0, 0.0, t_refs[i][lo:hi, :])
            new = jnp.where(lane(head, shape), top, old)
            t_refs[i][lo:hi, :] = jnp.where(lane(head + 8, shape), total, new)


def first_part(queries, keys, values, row_sets):
    n_q, n_k = len(queries), len(keys)
    heads = queries[0].shape[1] // HEAD_DIM
    per_head = lambda a: pl.BlockSpec((a.shape[0], HEAD_DIM), lambda h: (0, h))
    whole = lambda a: pl.BlockSpec((a.shape[0], HEAD_DIM), lambda h: (0, 0))
    work = sum(
        (hi - lo) * sum(b - a for _, a, b in use) for rows in row_sets for lo, hi, use in rows
    )
    outs = pl.pallas_call(
        functools.partial(first_kernel, row_sets, n_k),
        grid=(heads,),
        in_specs=[per_head(a) for a in (*queries, *keys, *values)],
        out_specs=[per_head(a) for a in queries] + [whole(a) for a in queries],
        out_shape=[jax.ShapeDtypeStruct(a.shape, F32) for a in queries]
        + [jax.ShapeDtypeStruct((a.shape[0], HEAD_DIM), F32) for a in queries],
        compiler_params=params(),
        cost_estimate=cost(8 * work * heads * HEAD_DIM, 8 * 2**20, work * heads),
    )(*queries, *keys, *values)
    return outs[:n_q], outs[n_q:]


def last_kernel(n_q, *refs):
    q_refs, s_refs, t_refs = refs[:n_q], refs[n_q : 2 * n_q], refs[2 * n_q : 3 * n_q]
    k_ref, v_ref = refs[3 * n_q : 3 * n_q + 2]
    o_refs = refs[3 * n_q + 2 :]
    rows = k_ref.shape[0]
    heads = o_refs[0].shape[1] // HEAD_DIM - 1
    shape = (192, HEAD_DIM)
    for i in range(n_q):
        for lo in range(0, rows, 192):
            packed = jnp.zeros(shape, F32)
            for h in range(heads):
                cols = slice(h * HEAD_DIM, (h + 1) * HEAD_DIM)
                here = slice(lo, lo + 192)
                state = (t_refs[i][here, h : h + 1], t_refs[i][here, 8 + h : 9 + h], s_refs[i][here, cols])
                top, total, sums = attend(q_refs[i][here, cols], [k_ref[:, cols]], [v_ref[:, cols]], state)
                o_refs[i][here, cols] = (sums / total).astype(BF)
                level = top * SCALE_LOG2 + jnp.log2(total)
                for part in range(3):
                    piece = level.astype(BF).astype(F32)
                    packed = jnp.where(lane(3 * h + part, shape), piece, packed)
                    level = level - piece
            o_refs[i][lo : lo + 192, heads * HEAD_DIM :] = packed.astype(BF)


def last_part(queries, sums, stats, key, value):
    n_q = len(queries)
    rows, width = queries[0].shape
    heads = width // HEAD_DIM
    whole = lambda a: pl.BlockSpec(a.shape, lambda: (0, 0))
    out = jax.ShapeDtypeStruct((rows, width + HEAD_DIM), BF)
    return pl.pallas_call(
        functools.partial(last_kernel, n_q),
        in_specs=[whole(a) for a in (*queries, *sums, *stats, key, value)],
        out_specs=[whole(out)] * n_q,
        out_shape=[out] * n_q,
        compiler_params=params(),
        cost_estimate=cost(8 * n_q * rows * rows * width, 4 * 2**20, n_q * rows * rows * heads),
    )(*queries, *sums, *stats, key, value)


def combine_kernel(a_ref, b_ref, c_ref, d_ref, same_ref, other_ref):
    refs = (a_ref, b_ref, c_ref, d_ref)
    heads = a_ref.shape[1] // HEAD_DIM - 1
    half = same_ref.shape[0]
    for lo, out in ((0, same_ref), (half, other_ref)):
        here = slice(lo, lo + half)
        for h in range(heads):
            cols = slice(h * HEAD_DIM, (h + 1) * HEAD_DIM)
            levels = []
            for r in refs:
                at = heads * HEAD_DIM + 3 * h
                s = r[here, at : at + 3].astype(F32)
                levels.append(s[:, 0:1] + s[:, 1:2] + s[:, 2:3])
            top = functools.reduce(jnp.maximum, levels)
            shares = [jnp.exp2(x - top) for x in levels]
            total = shares[0] + shares[1] + shares[2] + shares[3]
            acc = None
            for r, w in zip(refs, shares):
                part = r[here, cols].astype(F32) * (w / total)
                acc = part if acc is None else acc + part
            out[:, cols] = acc.astype(BF)


def combine(parts):
    rows, width = parts[0].shape
    out = jax.ShapeDtypeStruct((rows // 2, width - HEAD_DIM), BF)
    return pl.pallas_call(
        combine_kernel,
        out_shape=[out, out],
        compiler_params=params(),
        cost_estimate=cost(rows * width * 20, 4 * 2**20),
    )(*parts)


def project_kernel(core_ref, a_ref, b_ref, wa_ref, wb_ref, g_ref, first_ref, second_ref):
    half = first_ref.shape[0]
    r = jnp.dot(a_ref[...], wa_ref[...], preferred_element_type=F32)
    r += jnp.dot(b_ref[...], wb_ref[...], preferred_element_type=F32)
    r = (r * g_ref[...]).astype(BF)
    first_ref[...] = r[:half]
    second_ref[...] = r[half:]


def project(core, mine, theirs, weight, gate):
    rows, depth = mine.shape
    width = weight.shape[1]
    tile = 1024
    out = jax.ShapeDtypeStruct((rows // 2, width), BF)
    return pl.pallas_call(
        project_kernel,
        grid_spec=pltpu.PrefetchScalarGridSpec(
            num_scalar_prefetch=1,
            grid=(width // tile,),
            in_specs=[
                pl.BlockSpec((rows, depth), lambda j, c: (0, 0)),
                pl.BlockSpec((rows, depth), lambda j, c: (0, 0)),
                pl.BlockSpec((depth, tile), lambda j, c: (c[0], j)),
                pl.BlockSpec((depth, tile), lambda j, c: (1 - c[0], j)),
                pl.BlockSpec((1, tile), lambda j, c: (0, j)),
            ],
            out_specs=[pl.BlockSpec((rows // 2, tile), lambda j, c: (0, j))] * 2,
        ),
        out_shape=[out, out],
        compiler_params=params(),
        cost_estimate=cost(4 * rows * depth * width, weight.size * 2),
    )(core, mine, theirs, weight, weight, gate)


def per_device(queries, fresh_keys, fresh_values, stale_keys, stale_values, out_weight, out_gate):
    half = queries.shape[1]
    patch = 2 * half
    width = queries.shape[2] // 4
    head = lax.axis_index("head")
    core = lax.axis_index("patch") % 2
    core_table = jnp.reshape(core, (1,)).astype(jnp.int32)

    sk, sk_out, sv, sv_out = column_blocks(
        [stale_keys[0], stale_values[0]], [(0, core), (0, 1 - core), (1, core), (1, 1 - core)], width
    )
    q_mine, q_head, q_core, q_both = column_blocks(
        [queries[0]],
        [
            (0, head * 2 + core),
            (0, (1 - head) * 2 + core),
            (0, head * 2 + 1 - core),
            (0, (1 - head) * 2 + 1 - core),
        ],
        width,
    )
    q_head, q_core, q_both = (
        other_half(q_head, 0, 1),
        other_half(q_core, 1, 0),
        other_half(q_both, 1, 1),
    )
    k_own = jnp.concatenate([sk, other_core(sk_out)], axis=0)
    v_own = jnp.concatenate([sv, other_core(sv_out)], axis=0)
    q_own = jnp.concatenate([q_mine, q_head, q_core, q_both], axis=0)

    k_up, k_down = keys_along(k_own, 1), keys_along(k_own, -1)
    v_up, v_down = keys_along(v_own, 1), keys_along(v_own, -1)
    q_far = queries_along(q_own, 2)
    q_up, q_down = queries_along(q_own, 1), queries_along(q_own, -1)
    k_far = keys_along(k_up, 1)
    v_far = keys_along(v_down, -1)

    def exchanged(fresh):
        mine, out = column_blocks([fresh[0]], [(0, head), (0, 1 - head)], 2 * width)
        got = other_half(out, 0, 1)
        low, high = jnp.where(head == 0, mine, got), jnp.where(head == 0, got, mine)
        return jnp.concatenate([low, high], axis=0)

    new_keys, new_values = exchanged(fresh_keys), exchanged(fresh_values)
    fk, fk_out, fv, fv_out = column_blocks(
        [new_keys, new_values], [(0, core), (0, 1 - core), (1, core), (1, 1 - core)], width
    )
    fk_core, fv_core = other_core(fk_out), other_core(fv_out)

    every = [(0, 0, 2 * patch), (1, 0, 2 * patch), (2, 0, 2 * patch)]
    plain = [(0, patch, every), (patch, 2 * patch, every)]
    mixed = [
        (0, patch, [(3, 0, patch), (0, patch, 2 * patch), (1, 0, 2 * patch), (2, 0, 2 * patch)]),
        (patch, 2 * patch, [(4, 0, patch), (0, 0, patch), (1, 0, 2 * patch), (2, 0, 2 * patch)]),
    ]
    s_out, t_out = first_part(
        [q_far, q_up, q_down], [k_own, k_up, k_down], [v_own, v_up, v_down], [plain] * 3
    )
    s_own, t_own = first_part(
        [q_own], [k_own, k_up, k_down, fk, fk_core], [v_own, v_up, v_down, fv, fv_core], [mixed]
    )
    o_far, o_up, o_down = last_part([q_far, q_up, q_down], s_out, t_out, k_far, v_far)
    (o_own,) = last_part([q_own], s_own, t_own, k_far, v_far)
    parts = (o_own, queries_along(o_far, 2), queries_along(o_up, -1), queries_along(o_down, 1))
    mine, out = combine(parts)
    theirs = other_core(out)
    first, second = project(core_table, mine, theirs, out_weight[0], out_gate)
    first, second = onward_to(first, 0), onward_to(second, 1)
    branch = (first.astype(F32) + second.astype(F32)).astype(BF)
    return (new_keys[None], new_values[None], branch[None])


def solution(mesh):
    in_specs = (
        P("pipe", ("patch", "head"), None),
        P("pipe", ("patch", "head"), None),
        P("pipe", ("patch", "head"), None),
        P("pipe", "patch", "head"),
        P("pipe", "patch", "head"),
        P("pipe", "head", None),
        P("pipe", None),
    )
    out_specs = (
        P("pipe", "patch", "head"),
        P("pipe", "patch", "head"),
        P("pipe", ("patch", "head"), None),
    )
    return jax.shard_map(
        per_device, mesh=mesh, in_specs=in_specs, out_specs=out_specs, check_vma=False
    )
```

time: 284 us -> 137 us (0.48)
  waiting for transfers between devices: 116 us -> 39.8 us
  local copies, waits for them, and re-layouts: 64.1 us -> 3.13 us
  Pallas kernels: 0 us -> 55.7 us
  matrix products: 53.1 us -> 0 us
  starting transfers between devices: 12.1 us -> 32.4 us
  other arithmetic: 22.4 us -> 4.25 us
  between operations: 13.8 us -> 0.91 us
    pallas_call x0 -> x11, Pallas kernels: none -> 55.7 us  [the longest x2 24.6 us: first_part(): pl.pallas_call(functools.partial(first_kernel, row_sets, n_k), grid=(head...]
    dot_general x3 -> x0, matrix products: 53.1 us -> none  [the longest x1 22.7 us: per_device(): jnp.einsum('qhd,khd->hqk', query_heads, key_heads, preferred_element_type...]
    all_gather x2 -> x0, local copies, waits for them, and re-layouts: 41 us -> none  [the longest x1 20.5 us: per_device(): lax.all_gather(stale_keys[0], 'patch', axis=0, tiled=True)]
    all_gather x2 -> x0, waiting for transfers between devices: 36.6 us -> none  [the longest x1 35.6 us: per_device(): lax.all_gather(stale_keys[0], 'patch', axis=0, tiled=True)]
    reduce_scatter x1 -> x0, waiting for transfers between devices: 34.7 us -> none  [per_device(): lax.psum_scatter(jnp.dot(attended, weight_local, preferred_element_type=j...]
    ppermute x1 -> x24, starting transfers between devices: 0.63 us -> 32.4 us  [the longest x12 22 us: along(): return lax.ppermute(value, 'patch', pairs)]
    reduce_sum x1 -> x0, other arithmetic: 21.1 us -> none  [per_device(): row_total = jnp.sum(weights, axis=-1)]
    all_to_all x3 -> x0, waiting for transfers between devices: 20.7 us -> none  [the longest x1 7.29 us: per_device(): lax.all_to_all(fresh_values[0], 'head', split_axis=1, concat_axis=0, tile...]
  transfers between devices with their start and end apart: 7 -> 24, of which waited for: 7 -> 11; matrix products, arithmetic and copies ran while one was open for 26% -> 4% of each run, Pallas kernels for 0% -> 24%
where the time goes in v1:
time: 137 us; the launch traced here: 136 us
  Pallas kernels  55.7 us (41%)
  waiting for transfers between devices  39.8 us (29%)
  starting transfers between devices  32.4 us (24%)
  other arithmetic  4.25 us (3%)
  local copies, waits for them, and re-layouts  3.13 us (2%)
    pallas_call x2, Pallas kernels, first_part(): pl.pallas_call(functools.partial(first_kernel, row_sets, n_k), grid=(head...  24.6 us
    ppermute x2, waiting for transfers between devices, onward_to(): return lax.ppermute(value, ('pipe', 'head'), pairs)  23.2 us
    ppermute x12, starting transfers between devices, along(): return lax.ppermute(value, 'patch', pairs)  22 us
    pallas_call x2, Pallas kernels, last_part(): pl.pallas_call(functools.partial(last_kernel, n_q), in_specs=[whole(a) fo...  16 us
    pallas_call x1, Pallas kernels, project(): pl.pallas_call(project_kernel, grid_spec=pltpu.PrefetchScalarGridSpec(num...  7.76 us
    ppermute x5, starting transfers between devices, other_half(): return lax.ppermute(value, ('patch', 'head'), pairs)  7.33 us
    ppermute x5, waiting for transfers between devices, other_half(): return lax.ppermute(value, ('patch', 'head'), pairs)  7.1 us
    ppermute x12, waiting for transfers between devices, along(): return lax.ppermute(value, 'patch', pairs)  6.74 us
  transfers between devices with their start and end apart: 24, of which 11 were waited for; matrix products, arithmetic and copies ran while one was open for 4% of the time, Pallas kernels for 24%

profile of v1, /device:TPU:0, one launch (start us, length us, event | category | flops | bytes accessed | tf_op | source)
XLA Modules:
  0.0 136.2 jit_solution(16812405496315378903)
XLA Ops:
  0.6 0.1 pad_add_fusion.1.table_ref
  0.7 1.0 copy-done
  1.8 0.6 shard_map.96
  2.4 0.0 copy-start.1
  2.4 3.2 %collective-permute-start.2 = (bf16[96,640]{1,0:T(8,128)(2,1)S(1)}, bf16[96,640]{1,0:T(8,128)(2,1)S(1)}, u32[]{:S(2)}, u32[]{:S(2)}) collective-permute-start(bf16[96,640]{1,0:T(8,128)(2,1)S(1)} %get-tuple-element.39), channel_id=1, source_target_pairs={{0,1},{1,0},{2,3},{3,2},{4,5},{5,4},{6,7},{7,6},{8,9},{9,8},{10,11... | collective-permute-start | bytes 368648 | tf_op jit(solution)/shard_map/ppermute | solution.py:48
  5.6 0.5 collective-permute-start.4
  6.1 0.1 pad_add_fusion.2.table_ref
  6.2 0.7 shard_map.97
  6.9 0.1 collective-permute-start.5
  7.0 2.3 %collective-permute-done.2 = bf16[96,640]{1,0:T(8,128)(2,1)S(1)} collective-permute-done((bf16[96,640]{1,0:T(8,128)(2,1)S(1)}, bf16[96,640]{1,0:T(8,128)(2,1)S(1)}, u32[]{:S(2)}, u32[]{:S(2)}) %collective-permute-start.2) | collective-permute-done | bytes 122912 | tf_op jit(solution)/shard_map/ppermute | solution.py:48
  9.4 2.7 %collective-permute-done.4 = bf16[96,640]{1,0:T(8,128)(2,1)S(1)} collective-permute-done((bf16[96,640]{1,0:T(8,128)(2,1)S(1)}, bf16[96,640]{1,0:T(8,128)(2,1)S(1)}, u32[]{:S(2)}, u32[]{:S(2)}) %collective-permute-start.4) | collective-permute-done | bytes 122912 | tf_op jit(solution)/shard_map/ppermute | solution.py:48
  12.1 4.1 %collective-permute-start.17 = (bf16[384,640]{1,0:T(8,128)(2,1)S(1)}, bf16[384,640]{1,0:T(8,128)(2,1)S(1)}, u32[]{:S(2)}, u32[]{:S(2)}) collective-permute-start(bf16[384,640]{1,0:T(8,128)(2,1)S(1)} %constant_dynamic-update-slice_fusion.refs_0_), channel_id=1, source_target_pairs={{0,48},{2,14},{4,52},{6,2},{8,56},{10,6},{12,60},{14,10},{16,0},{1... | collective-permute-start | bytes 1474568 | tf_op jit(solution)/shard_map/ppermute | solution.py:29
  16.2 0.0 collective-permute-start.16
  16.2 0.1 pad_add_fusion.table_ref
  16.3 1.3 shard_map.94
  17.5 1.6 %collective-permute-start = (bf16[96,1280]{1,0:T(8,128)(2,1)}, bf16[96,1280]{1,0:T(8,128)(2,1)}, u32[]{:S(2)}, u32[]{:S(2)}) collective-permute-start(bf16[96,1280]{1,0:T(8,128)(2,1)} %get-tuple-element.35), channel_id=1, source_target_pairs={{0,1},{1,0},{2,3},{3,2},{4,5},{5,4},{6,7},{7,6},{8,9},{9,8},{10,11... | collective-permute-start | bytes 737288 | tf_op jit(solution)/shard_map/ppermute | solution.py:48
  19.1 0.6 shard_map.95
  19.7 0.0 collective-permute-done.5
  19.7 0.0 copy-start.6
  19.7 2.0 %collective-permute-start.1 = (bf16[96,1280]{1,0:T(8,128)(2,1)S(1)}, bf16[96,1280]{1,0:T(8,128)(2,1)}, u32[]{:S(2)}, u32[]{:S(2)}) collective-permute-start(bf16[96,1280]{1,0:T(8,128)(2,1)S(1)} %get-tuple-element.37), channel_id=1, source_target_pairs={{0,1},{1,0},{2,3},{3,2},{4,5},{5,4},{6,7},{7,6},{8,9},{9,8},{10,11... | collective-permute-start | bytes 737288 | tf_op jit(solution)/shard_map/ppermute | solution.py:48
  21.8 1.0 constant_dynamic-update-slice_fusion.4.refs_1_.refs_3_
  22.8 0.0 collective-permute-done.9
  22.8 2.8 %collective-permute-start.15 = (bf16[384,640]{1,0:T(8,128)(2,1)S(1)}, bf16[384,640]{1,0:T(8,128)(2,1)S(1)}, u32[]{:S(2)}, u32[]{:S(2)}) collective-permute-start(bf16[384,640]{1,0:T(8,128)(2,1)S(1)} %constant_dynamic-update-slice_fusion.refs_0_), channel_id=1, source_target_pairs={{0,32},{2,10},{4,36},{6,14},{8,40},{10,2},{12,44},{14,6},{16,48},{... | collective-permute-start | bytes 1474568 | tf_op jit(solution)/shard_map/ppermute | solution.py:29
  25.6 1.0 constant_dynamic-update-slice_fusion.6.refs_6_
  26.6 1.5 %collective-permute-done = bf16[96,1280]{1,0:T(8,128)(2,1)} collective-permute-done((bf16[96,1280]{1,0:T(8,128)(2,1)}, bf16[96,1280]{1,0:T(8,128)(2,1)}, u32[]{:S(2)}, u32[]{:S(2)}) %collective-permute-start) | collective-permute-done | bytes 245792 | tf_op jit(solution)/shard_map/ppermute | solution.py:48
  28.2 2.9 %collective-permute-start.11 = (bf16[384,640]{1,0:T(8,128)(2,1)S(1)}, bf16[384,640]{1,0:T(8,128)(2,1)S(1)}, u32[]{:S(2)}, u32[]{:S(2)}) collective-permute-start(bf16[384,640]{1,0:T(8,128)(2,1)S(1)} %constant_dynamic-update-slice_fusion.6.refs_6_), channel_id=1, source_target_pairs={{0,12},{2,50},{4,0},{6,54},{8,4},{10,58},{12,8},{14,62},{16,28},{1... | collective-permute-start | bytes 1474568 | tf_op jit(solution)/shard_map/ppermute | solution.py:29
  31.0 0.6 collective-permute-done.1
  31.6 0.7 collective-permute-start.10
  32.4 0.0 collective-permute-done.17.refs_2_
  32.4 2.5 %collective-permute-start.7 = (bf16[384,640]{1,0:T(8,128)(2,1)S(1)}, bf16[384,640]{1,0:T(8,128)(2,1)S(1)}, u32[]{:S(2)}, u32[]{:S(2)}) collective-permute-start(bf16[384,640]{1,0:T(8,128)(2,1)S(1)} %constant_dynamic-update-slice_fusion.4.refs_1_.refs_3_), channel_id=1, source_target_pairs={{0,12},{2,50},{4,0},{6,54},{8,4},{10,58},{12,8},{14,62},{16,28},{1... | collective-permute-start | bytes 1474568 | tf_op jit(solution)/shard_map/ppermute | solution.py:29
  34.9 0.0 collective-permute-done.16.refs_1_
  34.9 0.0 collective-permute-start.6
  34.9 1.1 broadcast_select_fusion.1
  36.0 0.8 pad_maximum_fusion.1
  36.9 1.2 collective-permute-done.11.refs_8_
  38.1 3.4 %collective-permute-start.14 = (bf16[384,640]{1,0:T(8,128)(2,1)S(1)}, bf16[384,640]{1,0:T(8,128)(2,1)S(1)}, u32[]{:S(2)}, u32[]{:S(2)}) collective-permute-start(bf16[384,640]{1,0:T(8,128)(2,1)S(1)} %collective-permute-done.11.refs_8_), channel_id=1, source_target_pairs={{0,12},{2,50},{4,0},{6,54},{8,4},{10,58},{12,8},{14,62},{16,28},{1... | collective-permute-start | bytes 1474568 | tf_op jit(solution)/shard_map/ppermute | solution.py:29
  41.4 5.5 %collective-permute-done.6.refs_2_.refs_4_ = bf16[384,640]{1,0:T(8,128)(2,1)S(1)} collective-permute-done((bf16[384,640]{1,0:T(8,128)(2,1)S(1)}, bf16[384,640]{1,0:T(8,128)(2,1)S(1)}, u32[]{:S(2)}, u32[]{:S(2)}) %collective-permute-start.6) | collective-permute-done | bytes 491552 | tf_op jit(solution)/shard_map/ppermute | solution.py:29
  46.9 0.0 collective-permute-start.13
  47.0 0.0 collective-permute-done.15.refs_0_
  47.0 0.0 collective-permute-done.10.refs_7_
  47.0 16.3 %shard_map.101 = (f32[384,640]{1,0:T(8,128)S(1)}, f32[384,640]{1,0:T(8,128)S(1)}, f32[384,640]{1,0:T(8,128)S(1)}, f32[384,128]{1,0:T(8,128)S(1)}, f32[384,128]{1,0:T(8,128)S(1)}, /*index=5*/f32[384,128]{1,0:T(8,128)S(1)}) custom-call(bf16[384,640]{1,0:T(8,128)(2,1)S(1)} %collective-permute-done.15.refs_0_, ...), custom_call_target="tpu_custom_call" | custom-call | flops 6794772480 | bytes 8388608 | tf_op jit(solution)/shard_map/pallas_call | solution.py:157
  63.3 0.0 collective-permute-done.13.refs_3_.refs_9_
  63.3 11.9 %shard_map.102 = (bf16[384,768]{1,0:T(8,128)(2,1)S(1)}, bf16[384,768]{1,0:T(8,128)(2,1)S(1)}, bf16[384,768]{1,0:T(8,128)(2,1)S(1)}) custom-call(bf16[384,640]{1,0:T(8,128)(2,1)S(1)} %collective-permute-done.15.refs_0_, bf16[384,640]{1,0:T(8,128)(2,1)S(1)} %collective-permute-done.16.refs_1_, bf16[384,640]{1,0:T(8,128)(2,1)S(1)} %collective-permute-done.17.refs_2_, ...), custom_call_target="tpu_custom_call" | custom-call | flops 2264924160 | bytes 4194304 | tf_op jit(solution)/shard_map/pallas_call | solution.py:200
  75.2 3.5 %collective-permute-start.18 = (bf16[384,768]{1,0:T(8,128)(2,1)S(1)}, bf16[384,768]{1,0:T(8,128)(2,1)S(1)}, u32[]{:S(2)}, u32[]{:S(2)}) collective-permute-start(bf16[384,768]{1,0:T(8,128)(2,1)S(1)} %get-tuple-element.58), channel_id=1, source_target_pairs={{0,32},{2,10},{4,36},{6,14},{8,40},{10,2},{12,44},{14,6},{16,48},{... | collective-permute-start | bytes 1769480 | tf_op jit(solution)/shard_map/ppermute | solution.py:29
  78.7 0.7 collective-permute-start.19
  79.4 1.3 collective-permute-start.20
  80.7 0.8 pad_maximum_fusion
  81.6 0.7 shard_map.98
  82.3 0.1 collective-permute-start.8
  82.4 0.5 collective-permute-start.12
  82.9 1.0 collective-permute-done.8.refs_5_
  83.9 0.4 collective-permute-done.12.refs_10_
  84.2 8.3 %shard_map.99 = (f32[384,640]{1,0:T(8,128)S(1)}, f32[384,128]{1,0:T(8,128)S(1)}) custom-call(bf16[384,640]{1,0:T(8,128)(2,1)S(1)} %constant_dynamic-update-slice_fusion.refs_0_, bf16[384,640]{1,0:T(8,128)(2,1)S(1)} %constant_dynamic-update-slice_fusion.4.refs_1_.refs_3_, bf16[384,640]{1,0:T(8,128)(2,1)S(1)} %collective-permute-done.6.refs_2_.refs_4_, ...), custom_call_target="tpu_custom_call" | custom-call | flops 2264924160 | bytes 8388608 | tf_op jit(solution)/shard_map/pallas_call | solution.py:157
  92.5 4.2 %shard_map.100.a_ref = bf16[384,768]{1,0:T(8,128)(2,1)S(1)} custom-call(bf16[384,640]{1,0:T(8,128)(2,1)S(1)} %constant_dynamic-update-slice_fusion.refs_0_, f32[384,640]{1,0:T(8,128)S(1)} %get-tuple-element.50.refs_1_, f32[384,128]{1,0:T(8,128)S(1)} %get-tuple-element.51.refs_2_, bf16[384,640]{1,0:T(8,128)(2,1)S(1)} %collective-permute-done.13.refs_3_.refs_9_, ...), custom_call_target="tpu_custom_call" | custom-call | flops 754974720 | bytes 4194304 | tf_op jit(solution)/shard_map/pallas_call | solution.py:200
  96.7 0.0 copy-start.5
  96.8 3.5 %shard_map.103 = (bf16[192,640]{1,0:T(8,128)(2,1)S(1)}, bf16[192,640]{1,0:T(8,128)(2,1)S(1)}) custom-call(bf16[384,768]{1,0:T(8,128)(2,1)S(1)} %shard_map.100.a_ref, bf16[384,768]{1,0:T(8,128)(2,1)S(1)} %collective-permute-done.18.b_ref, bf16[384,768]{1,0:T(8,128)(2,1)S(1)} %collective-permute-done.19.c_ref, bf16[384,768]{1,0:T(8,128)(2,1)S(1)} %collective-permute-done.20.d_ref), custom_call_target="tpu_custom_call" | custom-call | flops 5898240 | bytes 4194304 | tf_op jit(solution)/shard_map/pallas_call | solution.py:236
  100.2 0.2 collective-permute-start.21
  100.5 1.4 collective-permute-done.21.b_ref
  101.8 7.8 %shard_map.104 = (bf16[96,5120]{1,0:T(8,128)(2,1)S(1)}, bf16[96,5120]{1,0:T(8,128)(2,1)S(1)}) custom-call(s32[1]{0:T(128)} %bitcast.6.core_ref, bf16[192,640]{1,0:T(8,128)(2,1)S(1)} %get-tuple-element.61.a_ref, bf16[192,640]{1,0:T(8,128)(2,1)S(1)} %collective-permute-done.21.b_ref, bf16[1280,5120]{1,0:T(8,128)(2,1)} %bitcast.32, ...), custom_call_target="tpu_custom_call" | custom-call | flops 2516582400 | bytes 13107200 | tf_op jit(solution)/shard_map/pallas_call | solution.py:258
  109.6 0.7 collective-permute-start.22
  110.2 1.5 %collective-permute-start.23 = (bf16[96,5120]{1,0:T(8,128)(2,1)S(1)}, bf16[96,5120]{1,0:T(8,128)(2,1)S(1)}, u32[]{:S(2)}, u32[]{:S(2)}) collective-permute-start(bf16[96,5120]{1,0:T(8,128)(2,1)S(1)} %get-tuple-element.64), channel_id=1, source_target_pairs={{0,65},{1,64},{64,1},{65,0},{2,67},{3,66},{66,3},{67,2},{4,69},{5,... | collective-permute-start | bytes 2949128 | tf_op jit(solution)/shard_map/ppermute | solution.py:53
  111.8 21.7 %collective-permute-done.22 = bf16[96,5120]{1,0:T(8,128)(2,1)S(1)} collective-permute-done((bf16[96,5120]{1,0:T(8,128)(2,1)S(1)}, bf16[96,5120]{1,0:T(8,128)(2,1)S(1)}, u32[]{:S(2)}, u32[]{:S(2)}) %collective-permute-start.22) | collective-permute-done | bytes 983072 | tf_op jit(solution)/shard_map/ppermute | solution.py:53
  133.5 1.5 %collective-permute-done.23 = bf16[96,5120]{1,0:T(8,128)(2,1)S(1)} collective-permute-done((bf16[96,5120]{1,0:T(8,128)(2,1)S(1)}, bf16[96,5120]{1,0:T(8,128)(2,1)S(1)}, u32[]{:S(2)}, u32[]{:S(2)}) %collective-permute-start.23) | collective-permute-done | bytes 983072 | tf_op jit(solution)/shard_map/ppermute | solution.py:53
  135.0 1.2 fusion
  (24 shorter events, 0.2 us)
Async XLA Ops:
  0.7 1.0 copy-start
  1.8 4.4 %copy-start.3 = (bf16[1,192,1280]{2,1,0:T(8,128)(2,1)S(1)}, bf16[1,192,1280]{2,1,0:T(8,128)(2,1)}, u32[]{:S(2)}) copy-start(bf16[1,192,1280]{2,1,0:T(8,128)(2,1)} %param.10) | copy-start | bytes 1474564
  1.8 4.4 %copy-start.4 = (bf16[1,192,1280]{2,1,0:T(8,128)(2,1)S(1)}, bf16[1,192,1280]{2,1,0:T(8,128)(2,1)}, u32[]{:S(2)}) copy-start(bf16[1,192,1280]{2,1,0:T(8,128)(2,1)} %param.11) | copy-start | bytes 1474564
  2.4 13.9 %copy-start.1 = (bf16[1,96,2560]{2,1,0:T(8,128)(2,1)S(1)}, bf16[1,96,2560]{2,1,0:T(8,128)(2,1)}, u32[]{:S(2)}) copy-start(bf16[1,96,2560]{2,1,0:T(8,128)(2,1)} %param.8) | copy-start | bytes 1474564
  2.4 6.9 %collective-permute-start.2 = (bf16[96,640]{1,0:T(8,128)(2,1)S(1)}, bf16[96,640]{1,0:T(8,128)(2,1)S(1)}, u32[]{:S(2)}, u32[]{:S(2)}) collective-permute-start(bf16[96,640]{1,0:T(8,128)(2,1)S(1)} %get-tuple-element.39), channel_id=1, source_target_pairs={{0,1},{1,0},{2,3},{3,2},{4,5},{5,4},{6,7},{7,6},{8,9},{9,8},{10,11... | collective-permute-start | bytes 368648 | tf_op jit(solution)/shard_map/ppermute | solution.py:48
  5.6 3.7 %collective-permute-start.3 = (bf16[96,640]{1,0:T(8,128)(2,1)S(1)}, bf16[96,640]{1,0:T(8,128)(2,1)S(1)}, u32[]{:S(2)}, u32[]{:S(2)}) collective-permute-start(bf16[96,640]{1,0:T(8,128)(2,1)S(1)} %get-tuple-element.40), channel_id=1, source_target_pairs={{0,2},{1,3},{2,0},{3,1},{4,6},{5,7},{6,4},{7,5},{8,10},{9,11},{10,... | collective-permute-start | bytes 368648 | tf_op jit(solution)/shard_map/ppermute | solution.py:48
  5.6 6.5 %collective-permute-start.4 = (bf16[96,640]{1,0:T(8,128)(2,1)S(1)}, bf16[96,640]{1,0:T(8,128)(2,1)S(1)}, u32[]{:S(2)}, u32[]{:S(2)}) collective-permute-start(bf16[96,640]{1,0:T(8,128)(2,1)S(1)} %get-tuple-element.41), channel_id=1, source_target_pairs={{0,3},{1,2},{2,1},{3,0},{4,7},{5,6},{6,5},{7,4},{8,11},{9,10},{10,... | collective-permute-start | bytes 368648 | tf_op jit(solution)/shard_map/ppermute | solution.py:48
  6.2 12.9 %copy-start.2 = (bf16[1,96,2560]{2,1,0:T(8,128)(2,1)S(1)}, bf16[1,96,2560]{2,1,0:T(8,128)(2,1)}, u32[]{:S(2)}) copy-start(bf16[1,96,2560]{2,1,0:T(8,128)(2,1)} %param.9) | copy-start | bytes 1474564
  6.9 12.8 %collective-permute-start.5 = (bf16[192,640]{1,0:T(8,128)(2,1)S(1)}, bf16[192,640]{1,0:T(8,128)(2,1)S(1)}, u32[]{:S(2)}, u32[]{:S(2)}) collective-permute-start(bf16[192,640]{1,0:T(8,128)(2,1)S(1)} %get-tuple-element.43), channel_id=1, source_target_pairs={{0,2},{2,0},{4,6},{6,4},{8,10},{10,8},{12,14},{14,12},{16,18},{18,... | collective-permute-start | bytes 737288 | tf_op jit(solution)/shard_map/ppermute | solution.py:41
  12.1 20.3 %collective-permute-start.17 = (bf16[384,640]{1,0:T(8,128)(2,1)S(1)}, bf16[384,640]{1,0:T(8,128)(2,1)S(1)}, u32[]{:S(2)}, u32[]{:S(2)}) collective-permute-start(bf16[384,640]{1,0:T(8,128)(2,1)S(1)} %constant_dynamic-update-slice_fusion.refs_0_), channel_id=1, source_target_pairs={{0,48},{2,14},{4,52},{6,2},{8,56},{10,6},{12,60},{14,10},{16,0},{1... | collective-permute-start | bytes 1474568 | tf_op jit(solution)/shard_map/ppermute | solution.py:29
  16.2 18.7 %collective-permute-start.16 = (bf16[384,640]{1,0:T(8,128)(2,1)S(1)}, bf16[384,640]{1,0:T(8,128)(2,1)S(1)}, u32[]{:S(2)}, u32[]{:S(2)}) collective-permute-start(bf16[384,640]{1,0:T(8,128)(2,1)S(1)} %constant_dynamic-update-slice_fusion.refs_0_), channel_id=1, source_target_pairs={{0,16},{2,6},{4,20},{6,10},{8,24},{10,14},{12,28},{14,2},{16,32},{... | collective-permute-start | bytes 1474568 | tf_op jit(solution)/shard_map/ppermute | solution.py:29
  17.5 10.6 %collective-permute-start = (bf16[96,1280]{1,0:T(8,128)(2,1)}, bf16[96,1280]{1,0:T(8,128)(2,1)}, u32[]{:S(2)}, u32[]{:S(2)}) collective-permute-start(bf16[96,1280]{1,0:T(8,128)(2,1)} %get-tuple-element.35), channel_id=1, source_target_pairs={{0,1},{1,0},{2,3},{3,2},{4,5},{5,4},{6,7},{7,6},{8,9},{9,8},{10,11... | collective-permute-start | bytes 737288 | tf_op jit(solution)/shard_map/ppermute | solution.py:48
  19.1 3.7 %collective-permute-start.9 = (bf16[192,640]{1,0:T(8,128)(2,1)S(1)}, bf16[192,640]{1,0:T(8,128)(2,1)}, u32[]{:S(2)}, u32[]{:S(2)}) collective-permute-start(bf16[192,640]{1,0:T(8,128)(2,1)S(1)} %get-tuple-element.47), channel_id=1, source_target_pairs={{0,2},{2,0},{4,6},{6,4},{8,10},{10,8},{12,14},{14,12},{16,18},{18,... | collective-permute-start | bytes 737288 | tf_op jit(solution)/shard_map/ppermute | solution.py:41
  19.7 2.1 %copy-start.6 = (bf16[192,640]{1,0:T(8,128)(2,1)}, bf16[192,640]{1,0:T(8,128)(2,1)S(1)}, u32[]{:S(2)}) copy-start(bf16[192,640]{1,0:T(8,128)(2,1)S(1)} %collective-permute-done.5) | copy-start | bytes 737284
  19.7 11.9 %collective-permute-start.1 = (bf16[96,1280]{1,0:T(8,128)(2,1)S(1)}, bf16[96,1280]{1,0:T(8,128)(2,1)}, u32[]{:S(2)}, u32[]{:S(2)}) collective-permute-start(bf16[96,1280]{1,0:T(8,128)(2,1)S(1)} %get-tuple-element.37), channel_id=1, source_target_pairs={{0,1},{1,0},{2,3},{3,2},{4,5},{5,4},{6,7},{7,6},{8,9},{9,8},{10,11... | collective-permute-start | bytes 737288 | tf_op jit(solution)/shard_map/ppermute | solution.py:48
  22.8 24.1 %collective-permute-start.15 = (bf16[384,640]{1,0:T(8,128)(2,1)S(1)}, bf16[384,640]{1,0:T(8,128)(2,1)S(1)}, u32[]{:S(2)}, u32[]{:S(2)}) collective-permute-start(bf16[384,640]{1,0:T(8,128)(2,1)S(1)} %constant_dynamic-update-slice_fusion.refs_0_), channel_id=1, source_target_pairs={{0,32},{2,10},{4,36},{6,14},{8,40},{10,2},{12,44},{14,6},{16,48},{... | collective-permute-start | bytes 1474568 | tf_op jit(solution)/shard_map/ppermute | solution.py:29
  28.2 9.9 %collective-permute-start.11 = (bf16[384,640]{1,0:T(8,128)(2,1)S(1)}, bf16[384,640]{1,0:T(8,128)(2,1)S(1)}, u32[]{:S(2)}, u32[]{:S(2)}) collective-permute-start(bf16[384,640]{1,0:T(8,128)(2,1)S(1)} %constant_dynamic-update-slice_fusion.6.refs_6_), channel_id=1, source_target_pairs={{0,12},{2,50},{4,0},{6,54},{8,4},{10,58},{12,8},{14,62},{16,28},{1... | collective-permute-start | bytes 1474568 | tf_op jit(solution)/shard_map/ppermute | solution.py:29
  31.6 15.3 %collective-permute-start.10 = (bf16[384,640]{1,0:T(8,128)(2,1)S(1)}, bf16[384,640]{1,0:T(8,128)(2,1)S(1)}, u32[]{:S(2)}, u32[]{:S(2)}) collective-permute-start(bf16[384,640]{1,0:T(8,128)(2,1)S(1)} %constant_dynamic-update-slice_fusion.6.refs_6_), channel_id=1, source_target_pairs={{0,4},{2,18},{4,8},{6,22},{8,12},{10,26},{12,0},{14,30},{16,20},{1... | collective-permute-start | bytes 1474568 | tf_op jit(solution)/shard_map/ppermute | solution.py:29
  32.4 14.6 %collective-permute-start.7 = (bf16[384,640]{1,0:T(8,128)(2,1)S(1)}, bf16[384,640]{1,0:T(8,128)(2,1)S(1)}, u32[]{:S(2)}, u32[]{:S(2)}) collective-permute-start(bf16[384,640]{1,0:T(8,128)(2,1)S(1)} %constant_dynamic-update-slice_fusion.4.refs_1_.refs_3_), channel_id=1, source_target_pairs={{0,12},{2,50},{4,0},{6,54},{8,4},{10,58},{12,8},{14,62},{16,28},{1... | collective-permute-start | bytes 1474568 | tf_op jit(solution)/shard_map/ppermute | solution.py:29
  34.9 12.1 %collective-permute-start.6 = (bf16[384,640]{1,0:T(8,128)(2,1)S(1)}, bf16[384,640]{1,0:T(8,128)(2,1)S(1)}, u32[]{:S(2)}, u32[]{:S(2)}) collective-permute-start(bf16[384,640]{1,0:T(8,128)(2,1)S(1)} %constant_dynamic-update-slice_fusion.4.refs_1_.refs_3_), channel_id=1, source_target_pairs={{0,4},{2,18},{4,8},{6,22},{8,12},{10,26},{12,0},{14,30},{16,20},{1... | collective-permute-start | bytes 1474568 | tf_op jit(solution)/shard_map/ppermute | solution.py:29
  38.1 25.2 %collective-permute-start.14 = (bf16[384,640]{1,0:T(8,128)(2,1)S(1)}, bf16[384,640]{1,0:T(8,128)(2,1)S(1)}, u32[]{:S(2)}, u32[]{:S(2)}) collective-permute-start(bf16[384,640]{1,0:T(8,128)(2,1)S(1)} %collective-permute-done.11.refs_8_), channel_id=1, source_target_pairs={{0,12},{2,50},{4,0},{6,54},{8,4},{10,58},{12,8},{14,62},{16,28},{1... | collective-permute-start | bytes 1474568 | tf_op jit(solution)/shard_map/ppermute | solution.py:29
  46.9 16.3 %collective-permute-start.13 = (bf16[384,640]{1,0:T(8,128)(2,1)S(1)}, bf16[384,640]{1,0:T(8,128)(2,1)S(1)}, u32[]{:S(2)}, u32[]{:S(2)}) collective-permute-start(bf16[384,640]{1,0:T(8,128)(2,1)S(1)} %collective-permute-done.6.refs_2_.refs_4_), channel_id=1, source_target_pairs={{0,4},{2,18},{4,8},{6,22},{8,12},{10,26},{12,0},{14,30},{16,20},{1... | collective-permute-start | bytes 1474568 | tf_op jit(solution)/shard_map/ppermute | solution.py:29
  75.2 21.6 %collective-permute-start.18 = (bf16[384,768]{1,0:T(8,128)(2,1)S(1)}, bf16[384,768]{1,0:T(8,128)(2,1)S(1)}, u32[]{:S(2)}, u32[]{:S(2)}) collective-permute-start(bf16[384,768]{1,0:T(8,128)(2,1)S(1)} %get-tuple-element.58), channel_id=1, source_target_pairs={{0,32},{2,10},{4,36},{6,14},{8,40},{10,2},{12,44},{14,6},{16,48},{... | collective-permute-start | bytes 1769480 | tf_op jit(solution)/shard_map/ppermute | solution.py:29
  78.7 18.0 %collective-permute-start.19 = (bf16[384,768]{1,0:T(8,128)(2,1)S(1)}, bf16[384,768]{1,0:T(8,128)(2,1)S(1)}, u32[]{:S(2)}, u32[]{:S(2)}) collective-permute-start(bf16[384,768]{1,0:T(8,128)(2,1)S(1)} %get-tuple-element.59), channel_id=1, source_target_pairs={{0,48},{2,14},{4,52},{6,2},{8,56},{10,6},{12,60},{14,10},{16,0},{1... | collective-permute-start | bytes 1769480 | tf_op jit(solution)/shard_map/ppermute | solution.py:29
  79.4 17.3 %collective-permute-start.20 = (bf16[384,768]{1,0:T(8,128)(2,1)S(1)}, bf16[384,768]{1,0:T(8,128)(2,1)S(1)}, u32[]{:S(2)}, u32[]{:S(2)}) collective-permute-start(bf16[384,768]{1,0:T(8,128)(2,1)S(1)} %get-tuple-element.60), channel_id=1, source_target_pairs={{0,16},{2,6},{4,20},{6,10},{8,24},{10,14},{12,28},{14,2},{16,32},{... | collective-permute-start | bytes 1769480 | tf_op jit(solution)/shard_map/ppermute | solution.py:29
  82.3 1.6 %collective-permute-start.8 = (bf16[192,640]{1,0:T(8,128)(2,1)S(1)}, bf16[192,640]{1,0:T(8,128)(2,1)S(1)}, u32[]{:S(2)}, u32[]{:S(2)}) collective-permute-start(bf16[192,640]{1,0:T(8,128)(2,1)S(1)} %get-tuple-element.45), channel_id=1, source_target_pairs={{0,2},{2,0},{4,6},{6,4},{8,10},{10,8},{12,14},{14,12},{16,18},{18,... | collective-permute-start | bytes 737288 | tf_op jit(solution)/shard_map/ppermute | solution.py:41
  82.4 1.9 %collective-permute-start.12 = (bf16[192,640]{1,0:T(8,128)(2,1)S(1)}, bf16[192,640]{1,0:T(8,128)(2,1)S(1)}, u32[]{:S(2)}, u32[]{:S(2)}) collective-permute-start(bf16[192,640]{1,0:T(8,128)(2,1)S(1)} %get-tuple-element.49), channel_id=1, source_target_pairs={{0,2},{2,0},{4,6},{6,4},{8,10},{10,8},{12,14},{14,12},{16,18},{18,... | collective-permute-start | bytes 737288 | tf_op jit(solution)/shard_map/ppermute | solution.py:41
  96.7 5.1 %copy-start.5 = (f32[1,5120]{1,0:T(1,128)S(1)}, f32[1,5120]{1,0:T(1,128)}, u32[]{:S(2)}) copy-start(f32[1,5120]{1,0:T(1,128)} %g_ref.1) | copy-start | bytes 61444
  100.2 1.6 %collective-permute-start.21 = (bf16[192,640]{1,0:T(8,128)(2,1)S(1)}, bf16[192,640]{1,0:T(8,128)(2,1)S(1)}, u32[]{:S(2)}, u32[]{:S(2)}) collective-permute-start(bf16[192,640]{1,0:T(8,128)(2,1)S(1)} %get-tuple-element.62), channel_id=1, source_target_pairs={{0,2},{2,0},{4,6},{6,4},{8,10},{10,8},{12,14},{14,12},{16,18},{18,... | collective-permute-start | bytes 737288 | tf_op jit(solution)/shard_map/ppermute | solution.py:41
  109.6 23.9 %collective-permute-start.22 = (bf16[96,5120]{1,0:T(8,128)(2,1)S(1)}, bf16[96,5120]{1,0:T(8,128)(2,1)S(1)}, u32[]{:S(2)}, u32[]{:S(2)}) collective-permute-start(bf16[96,5120]{1,0:T(8,128)(2,1)S(1)} %get-tuple-element.63), channel_id=1, source_target_pairs={{0,64},{1,65},{64,0},{65,1},{2,66},{3,67},{66,2},{67,3},{4,68},{5,... | collective-permute-start | bytes 2949128 | tf_op jit(solution)/shard_map/ppermute | solution.py:53
  110.2 24.7 %collective-permute-start.23 = (bf16[96,5120]{1,0:T(8,128)(2,1)S(1)}, bf16[96,5120]{1,0:T(8,128)(2,1)S(1)}, u32[]{:S(2)}, u32[]{:S(2)}) collective-permute-start(bf16[96,5120]{1,0:T(8,128)(2,1)S(1)} %get-tuple-element.64), channel_id=1, source_target_pairs={{0,65},{1,64},{64,1},{65,0},{2,67},{3,66},{66,3},{67,2},{4,69},{5,... | collective-permute-start | bytes 2949128 | tf_op jit(solution)/shard_map/ppermute | solution.py:53

commit v2 on v0

v2 whole, which is shorter than its diff:
```python
import functools
import math
import jax
import jax.numpy as jnp
from jax import lax
from jax.experimental import pallas as pl
from jax.experimental.pallas import tpu as pltpu
from jax.sharding import PartitionSpec as P

HEAD_DIM = 128
CHIPS = 4
SCALE_LOG2 = HEAD_DIM ** (-0.5) / math.log(2.0)
BF = jnp.bfloat16
F32 = jnp.float32
VMEM_LIMIT = 20 * 1024 * 1024


def place(z, y, core):
    return ((z % CHIPS) * CHIPS + y % CHIPS) * 2 + core


def along(value, steps, core_on_y):
    pairs = []
    for z in range(CHIPS):
        for y in range(CHIPS):
            for core in range(2):
                to = place(z, y + steps, core) if core == core_on_y else place(z + steps, y, core)
                pairs.append((place(z, y, core), to))
    return lax.ppermute(value, "patch", pairs)


def keys_along(value, steps):
    return along(value, steps, 0)


def queries_along(value, steps):
    return along(value, steps, 1)


def other_core(value):
    return lax.ppermute(value, "patch", [(i, i ^ 1) for i in range(2 * CHIPS * CHIPS)])


def other_half(value, core, head):
    pairs = [
        (b * 2 + h, (b ^ core) * 2 + (h ^ head)) for b in range(2 * CHIPS * CHIPS) for h in range(2)
    ]
    return lax.ppermute(value, ("patch", "head"), pairs)


def onward_to(value, head):
    pairs = [(p * 2 + h, (1 - p) * 2 + (h ^ head)) for p in range(2) for h in range(2)]
    return lax.ppermute(value, ("pipe", "head"), pairs)


def params(limit=VMEM_LIMIT):
    return pltpu.CompilerParams(vmem_limit_bytes=limit)


def cost(flops, nbytes, trans=0):
    return pl.CostEstimate(flops=flops, bytes_accessed=nbytes, transcendentals=trans)


def split_by_core(table, keys, values, queries):
    rows, width = keys.shape[1], keys.shape[2] // 2
    few = queries.shape[1]

    def body(table_ref, k_ref, v_ref, q_ref, same_ref, q_same_ref, other_ref, sems):
        head, core = table_ref[0], table_ref[1]

        def columns(ref, i):
            return ref.at[0, :, pl.ds(pl.multiple_of(i * width, HEAD_DIM), width)]

        moves = [
            (columns(k_ref, 1 - core), other_ref.at[pl.ds(0, rows)]),
            (columns(v_ref, 1 - core), other_ref.at[pl.ds(rows, rows)]),
            (columns(q_ref, 2 * head + 1 - core), other_ref.at[pl.ds(2 * rows, few)]),
            (columns(q_ref, 2 * (1 - head) + 1 - core), other_ref.at[pl.ds(2 * rows + few, few)]),
            (columns(k_ref, core), same_ref.at[pl.ds(0, rows)]),
            (columns(v_ref, core), same_ref.at[pl.ds(rows, rows)]),
            (columns(q_ref, 2 * head + core), q_same_ref.at[pl.ds(0, few)]),
            (columns(q_ref, 2 * (1 - head) + core), q_same_ref.at[pl.ds(few, few)]),
        ]
        copies = [pltpu.make_async_copy(a, b, sems.at[i]) for i, (a, b) in enumerate(moves)]
        for c in copies:
            c.start()
        for c in copies:
            c.wait()

    vmem = pl.BlockSpec(memory_space=pltpu.VMEM)
    hbm = pl.BlockSpec(memory_space=pltpu.HBM)
    return pl.pallas_call(
        body,
        in_specs=[pl.BlockSpec(memory_space=pltpu.SMEM), hbm, hbm, hbm],
        out_specs=[vmem] * 3,
        out_shape=[
            jax.ShapeDtypeStruct((2 * rows, width), BF),
            jax.ShapeDtypeStruct((2 * few, width), BF),
            jax.ShapeDtypeStruct((2 * rows + 2 * few, width), BF),
        ],
        scratch_shapes=[pltpu.SemaphoreType.DMA((8,))],
        compiler_params=params(),
    )(table, keys, values, queries)


def outgoing_fresh(head, keys, values):
    rows, width = keys.shape[0], keys.shape[1] // 2

    def body(head_ref, k_ref, v_ref, out_ref):
        out_ref[:rows] = k_ref[...]
        out_ref[rows:] = v_ref[...]

    block = pl.BlockSpec((rows, width), lambda g, h: (0, 1 - h[0]))
    return pl.pallas_call(
        body,
        grid_spec=pltpu.PrefetchScalarGridSpec(
            num_scalar_prefetch=1,
            grid=(1,),
            in_specs=[block, block],
            out_specs=pl.BlockSpec((2 * rows, width), lambda g, h: (0, 0)),
        ),
        out_shape=jax.ShapeDtypeStruct((2 * rows, width), BF),
        compiler_params=params(),
    )(head, keys, values)


def assemble_fresh(table, keys, values, got):
    rows, width = keys.shape[0], keys.shape[1] // 2
    narrow = width // 2

    def body(table_ref, k_ref, v_ref, got_ref, nk_ref, nv_ref, same_ref, other_ref):
        head, core = table_ref[0], table_ref[1]
        for mine, at, new in ((k_ref, 0, nk_ref), (v_ref, rows, nv_ref)):
            theirs = got_ref[at : at + rows]
            low = jnp.where(head == 0, mine[...], theirs)
            high = jnp.where(head == 0, theirs, mine[...])
            new[:rows] = low
            new[rows:] = high
            for lo, x in ((2 * at, low), (2 * at + rows, high)):
                left, right = x[:, :narrow], x[:, narrow:]
                same_ref[lo : lo + rows] = jnp.where(core == 0, left, right)
                other_ref[lo : lo + rows] = jnp.where(core == 0, right, left)

    block = pl.BlockSpec((rows, width), lambda g, t: (0, t[0]))
    whole = lambda r, w: pl.BlockSpec((r, w), lambda g, t: (0, 0))
    return pl.pallas_call(
        body,
        grid_spec=pltpu.PrefetchScalarGridSpec(
            num_scalar_prefetch=1,
            grid=(1,),
            in_specs=[block, block, whole(2 * rows, width)],
            out_specs=[whole(2 * rows, width)] * 2 + [whole(4 * rows, narrow)] * 2,
        ),
        out_shape=[jax.ShapeDtypeStruct((2 * rows, width), BF)] * 2
        + [jax.ShapeDtypeStruct((4 * rows, narrow), BF)] * 2,
        compiler_params=params(),
    )(table, keys, values, got)


def nt(a, b):
    return lax.dot_general(a, b, (((1,), (1,)), ((), ())), preferred_element_type=F32)


def with_ones(v):
    return jnp.concatenate([v, jnp.ones(v.shape, BF)], axis=1)


def lanes(shape):
    return lax.broadcasted_iota(jnp.int32, shape, 1)


def attend(jobs, q_ref, o_ref):
    heads = q_ref.shape[1] // HEAD_DIM
    work = [(i, h) for h in range(heads) for i in range(len(jobs))]

    def columns(refs, h):
        cols = slice(h * HEAD_DIM, (h + 1) * HEAD_DIM)
        return jnp.concatenate([r[lo:hi, cols] for r, lo, hi in refs], axis=0)

    def product(i, h):
        here, keys, _ = jobs[i]
        return nt(q_ref[here, h * HEAD_DIM : (h + 1) * HEAD_DIM], columns(keys, h))

    shapes = [(here.stop - here.start, HEAD_DIM) for here, _, _ in jobs]
    tops = [jnp.zeros(s, F32) for s in shapes]
    totals = [jnp.ones(s, F32) for s in shapes]
    scores = product(*work[0])
    for n, (i, h) in enumerate(work):
        later = product(*work[n + 1]) if n + 1 < len(work) else None
        here, _, values = jobs[i]
        top = jnp.max(scores, axis=1, keepdims=True)
        w = jnp.exp2((scores - top) * SCALE_LOG2).astype(BF)
        part = jnp.dot(w, with_ones(columns(values, h)), preferred_element_type=F32)
        total = part[:, HEAD_DIM:]
        o_ref[here, h * HEAD_DIM : (h + 1) * HEAD_DIM] = (part[:, :HEAD_DIM] / total).astype(BF)
        at = lanes(shapes[i]) == h
        tops[i] = jnp.where(at, top, tops[i])
        totals[i] = jnp.where(at, total, totals[i])
        scores = later
    for (here, _, _), top, total in zip(jobs, tops, totals):
        level = top * SCALE_LOG2 + jnp.log2(total)
        high = level.astype(BF).astype(F32)
        rest = level - high
        middle = rest.astype(BF).astype(F32)
        packed = high + pltpu.roll(middle, 8, 1) + pltpu.roll(rest - middle, 16, 1)
        o_ref[here, heads * HEAD_DIM :] = packed.astype(BF)


def halves(refs):
    rows = refs[0].shape[0] // 2
    return [(r, 0, rows) for r in refs], [(r, rows, 2 * rows) for r in refs]


def remote_kernel(q_ref, *refs):
    *near, k_far, v_far, o_ref = refs
    rows = q_ref.shape[0]
    keys, values = halves(near)
    attend([(slice(0, rows), keys + [(k_far, 0, rows)], values + [(v_far, 0, rows)])], q_ref, o_ref)


def own_kernel(q_ref, same, other, *refs):
    *near, k_far, v_far, f_same, f_other, o_ref = refs
    rows = q_ref.shape[0]
    half = rows // 2
    jobs = []
    for i, mine in enumerate(((f_same, other), (f_other, same))):
        keys, values = halves([*mine, *near])
        here = slice(i * half, (i + 1) * half)
        jobs.append((here, keys + [(k_far, 0, rows)], values + [(v_far, 0, rows)]))
    attend(jobs, q_ref, o_ref)


def attention(kernel, query, blocks):
    rows, width = query.shape
    heads = width // HEAD_DIM
    return pl.pallas_call(
        kernel,
        out_shape=jax.ShapeDtypeStruct((rows, width + HEAD_DIM), BF),
        compiler_params=params(),
        cost_estimate=cost(16 * rows * rows * width, 4 * 2**20, 4 * rows * rows * heads),
    )(query, *blocks)


def combine_kernel(start, a_ref, b_ref, c_ref, d_ref, out):
    refs = (a_ref, b_ref, c_ref, d_ref)
    heads = a_ref.shape[1] // HEAD_DIM - 1
    here = slice(start, start + out.shape[0])
    levels = []
    for r in refs:
        s = r[here, heads * HEAD_DIM :].astype(F32)
        levels.append(s + pltpu.roll(s, HEAD_DIM - 8, 1) + pltpu.roll(s, HEAD_DIM - 16, 1))
    top = functools.reduce(jnp.maximum, levels)
    shares = [jnp.exp2(x - top) for x in levels]
    total = 1.0 / (shares[0] + shares[1] + shares[2] + shares[3])
    shares = [x * total for x in shares]
    for h in range(heads):
        cols = slice(h * HEAD_DIM, (h + 1) * HEAD_DIM)
        acc = None
        for r, w in zip(refs, shares):
            part = r[here, cols].astype(F32) * w[:, h : h + 1]
            acc = part if acc is None else acc + part
        out[:, cols] = acc.astype(BF)


def combine(parts, start):
    rows, width = parts[0].shape
    return pl.pallas_call(
        functools.partial(combine_kernel, start),
        out_shape=jax.ShapeDtypeStruct((rows // 2, width - HEAD_DIM), BF),
        compiler_params=params(),
        cost_estimate=cost(rows * width * 10, 2 * 2**20),
    )(*parts)


def project_kernel(core_ref, a_ref, b_ref, w_ref, g_ref, first_ref, second_ref, x_ref):
    half = first_ref.shape[0]
    depth = a_ref.shape[1]

    @pl.when(pl.program_id(0) == 0)
    def _():
        a, b = a_ref[...], b_ref[...]
        x_ref[:, :depth] = jnp.where(core_ref[0] == 0, a, b)
        x_ref[:, depth:] = jnp.where(core_ref[0] == 0, b, a)

    r = jnp.dot(x_ref[...], w_ref[...], preferred_element_type=F32)
    r = (r * g_ref[...]).astype(BF)
    first_ref[...] = r[:half]
    second_ref[...] = r[half:]


def project(core, mine, theirs, weight, gate, first, width):
    rows, depth = mine.shape
    tile = 512
    start = first // tile
    out = jax.ShapeDtypeStruct((rows // 2, width), BF)
    return pl.pallas_call(
        project_kernel,
        grid_spec=pltpu.PrefetchScalarGridSpec(
            num_scalar_prefetch=1,
            grid=(width // tile,),
            in_specs=[
                pl.BlockSpec((rows, depth), lambda j, c: (0, 0)),
                pl.BlockSpec((rows, depth), lambda j, c: (0, 0)),
                pl.BlockSpec((2 * depth, tile), lambda j, c: (0, start + j)),
                pl.BlockSpec((1, tile), lambda j, c: (0, start + j)),
            ],
            out_specs=[pl.BlockSpec((rows // 2, tile), lambda j, c: (0, j))] * 2,
            scratch_shapes=[pltpu.VMEM((rows, 2 * depth), BF)],
        ),
        out_shape=[out, out],
        compiler_params=params(),
        cost_estimate=cost(4 * rows * depth * width, depth * width * 4),
    )(core, mine, theirs, weight, gate)


def per_device(queries, fresh_keys, fresh_values, stale_keys, stale_values, out_weight, out_gate):
    half = queries.shape[1]
    patch = 2 * half
    head = lax.axis_index("head").astype(jnp.int32)
    core = (lax.axis_index("patch") % 2).astype(jnp.int32)
    core_table = jnp.reshape(core, (1,))
    head_table = jnp.reshape(head, (1,))

    table = jnp.stack([head, core])
    same, q_same, other = split_by_core(table, stale_keys, stale_values, queries)
    up_same, down_same = keys_along(same, 1), keys_along(same, -1)
    other = other_core(other)
    other, q_core = other[: 2 * patch], other[2 * patch :]
    up_other, down_other = keys_along(other, 1), keys_along(other, -1)

    q_got = other_half(jnp.concatenate([q_same[half:], q_core[half:]], axis=0), 0, 1)
    q_own = jnp.concatenate([q_same[:half], q_got[:half], q_core[:half], q_got[half:]], axis=0)
    q_up, q_down = queries_along(q_own, 1), queries_along(q_own, -1)
    q_far = queries_along(q_own, 2)

    k_far = keys_along(jnp.concatenate([up_same[:patch], up_other[:patch]], axis=0), 1)
    v_far = keys_along(jnp.concatenate([down_same[patch:], down_other[patch:]], axis=0), -1)

    fresh_keys, fresh_values, up_other, down_other, q_up, q_down = lax.optimization_barrier(
        (fresh_keys, fresh_values, up_other, down_other, q_up, q_down)
    )
    got = other_half(outgoing_fresh(head_table, fresh_keys[0], fresh_values[0]), 0, 1)
    blocks = [same, other, up_same, up_other, down_same, down_other, k_far, v_far]
    o_far = attention(remote_kernel, q_far, blocks)
    o_up = attention(remote_kernel, q_up, blocks)
    o_down = attention(remote_kernel, q_down, blocks)
    got, _ = lax.optimization_barrier((got, o_down))
    new_keys, new_values, f_same, f_other = assemble_fresh(
        table, fresh_keys[0], fresh_values[0], got
    )
    f_other = other_core(f_other)
    o_own = attention(own_kernel, q_own, blocks + [f_same, f_other])
    parts = (o_own, queries_along(o_far, 2), queries_along(o_up, -1), queries_along(o_down, 1))
    theirs = other_core(combine(parts, patch))
    mine = combine(parts, 0)
    pieces = []
    for start, width in ((0, 1536), (1536, out_weight.shape[2] - 1536)):
        first, second = project(core_table, mine, theirs, out_weight[0], out_gate, start, width)
        pieces.append((onward_to(first, 0), onward_to(second, 1)))
    branch = jnp.concatenate(
        [(first.astype(F32) + second.astype(F32)).astype(BF) for first, second in pieces], axis=1
    )
    return (new_keys[None], new_values[None], branch[None])


def solution(mesh):
    in_specs = (
        P("pipe", ("patch", "head"), None),
        P("pipe", ("patch", "head"), None),
        P("pipe", ("patch", "head"), None),
        P("pipe", "patch", "head"),
        P("pipe", "patch", "head"),
        P("pipe", "head", None),
        P("pipe", None),
    )
    out_specs = (
        P("pipe", "patch", "head"),
        P("pipe", "patch", "head"),
        P("pipe", ("patch", "head"), None),
    )
    return jax.shard_map(
        per_device, mesh=mesh, in_specs=in_specs, out_specs=out_specs, check_vma=False
    )
```

time: 284 us -> 101 us (0.36)
  waiting for transfers between devices: 116 us -> 39 us
  local copies, waits for them, and re-layouts: 64.1 us -> 3.33 us
  matrix products: 53.1 us -> 0 us
  Pallas kernels: 0 us -> 24.7 us
  other arithmetic: 22.4 us -> 1.49 us
  starting transfers between devices: 12.1 us -> 31.1 us
  between operations: 13.8 us -> 0.9 us
    dot_general x3 -> x0, matrix products: 53.1 us -> none  [the longest x1 22.7 us: per_device(): jnp.einsum('qhd,khd->hqk', query_heads, key_heads, preferred_element_type...]
    all_gather x2 -> x0, local copies, waits for them, and re-layouts: 41 us -> none  [the longest x1 20.5 us: per_device(): lax.all_gather(stale_keys[0], 'patch', axis=0, tiled=True)]
    all_gather x2 -> x0, waiting for transfers between devices: 36.6 us -> none  [the longest x1 35.6 us: per_device(): lax.all_gather(stale_keys[0], 'patch', axis=0, tiled=True)]
    reduce_scatter x1 -> x0, waiting for transfers between devices: 34.7 us -> none  [per_device(): lax.psum_scatter(jnp.dot(attended, weight_local, preferred_element_type=j...]
    ppermute x1 -> x21, starting transfers between devices: 0.63 us -> 31.1 us  [the longest x12 19.3 us: along(): return lax.ppermute(value, 'patch', pairs)]
    pallas_call x0 -> x11, Pallas kernels: none -> 24.7 us  [the longest x4 15.1 us: attention(): pl.pallas_call(kernel, out_shape=jax.ShapeDtypeStruct((rows, width + HEAD...]
    reduce_sum x1 -> x0, other arithmetic: 21.1 us -> none  [per_device(): row_total = jnp.sum(weights, axis=-1)]
    all_to_all x3 -> x0, waiting for transfers between devices: 20.7 us -> none  [the longest x1 7.29 us: per_device(): lax.all_to_all(fresh_values[0], 'head', split_axis=1, concat_axis=0, tile...]
  transfers between devices with their start and end apart: 7 -> 21, of which waited for: 7 -> 13; matrix products, arithmetic and copies ran while one was open for 26% -> 0% of each run, Pallas kernels for 0% -> 21%
where the time goes in v2:
time: 101 us
  waiting for transfers between devices  39 us (39%)
  starting transfers between devices  31.1 us (31%)
  Pallas kernels  24.7 us (24%)
  local copies, waits for them, and re-layouts  3.33 us (3%)
  other arithmetic  1.49 us (1%)
    ppermute x12, starting transfers between devices, along(): return lax.ppermute(value, 'patch', pairs)  19.3 us
    ppermute x12, waiting for transfers between devices, along(): return lax.ppermute(value, 'patch', pairs)  17.8 us
    ppermute x4, waiting for transfers between devices, onward_to(): return lax.ppermute(value, ('pipe', 'head'), pairs)  17.4 us
    pallas_call x4, Pallas kernels, attention(): pl.pallas_call(kernel, out_shape=jax.ShapeDtypeStruct((rows, width + HEAD...  15.1 us
    ppermute x2, starting transfers between devices, other_half(): return lax.ppermute(value, ('patch', 'head'), pairs)  6.56 us
    pallas_call x2, Pallas kernels, project(): pl.pallas_call(project_kernel, grid_spec=pltpu.PrefetchScalarGridSpec(num...  5.53 us
    ppermute x4, starting transfers between devices, onward_to(): return lax.ppermute(value, ('pipe', 'head'), pairs)  5.04 us
    ppermute x2, waiting for transfers between devices, other_half(): return lax.ppermute(value, ('patch', 'head'), pairs)  3.17 us
  transfers between devices with their start and end apart: 21, of which 13 were waited for; matrix products, arithmetic and copies ran while one was open for 0% of the time, Pallas kernels for 21%

profile of v2, /device:TPU:0, one launch (start us, length us, event | category | flops | bytes accessed | tf_op | source)
XLA Modules:
  0.0 100.6 jit_solution(6549290239257653473)
XLA Ops:
  0.6 0.1 pad_add_fusion.table_ref
  0.7 1.0 %copy-done.2 = bf16[1,192,1280]{2,1,0:T(8,128)(2,1)S(1)} copy-done((bf16[1,192,1280]{2,1,0:T(8,128)(2,1)S(1)}, bf16[1,192,1280]{2,1,0:T(8,128)(2,1)}, u32[]{:S(2)}) %copy-start.2) | copy-done | bytes 491544
  1.8 1.0 %copy-done.3 = bf16[1,192,1280]{2,1,0:T(8,128)(2,1)S(1)} copy-done((bf16[1,192,1280]{2,1,0:T(8,128)(2,1)S(1)}, bf16[1,192,1280]{2,1,0:T(8,128)(2,1)}, u32[]{:S(2)}) %copy-start.3) | copy-done | bytes 491544
  2.8 1.0 %copy-done.4 = bf16[1,96,2560]{2,1,0:T(8,128)(2,1)S(1)} copy-done((bf16[1,96,2560]{2,1,0:T(8,128)(2,1)S(1)}, bf16[1,96,2560]{2,1,0:T(8,128)(2,1)}, u32[]{:S(2)}) %copy-start.4) | copy-done | bytes 491544
  3.8 0.8 shard_map.94
  4.6 0.1 collective-permute-start
  4.7 1.7 %collective-permute-start.7 = (bf16[384,640]{1,0:T(8,128)(2,1)S(1)}, bf16[384,640]{1,0:T(8,128)(2,1)S(1)}, u32[]{:S(2)}, u32[]{:S(2)}) collective-permute-start(bf16[384,640]{1,0:T(8,128)(2,1)S(1)} %get-tuple-element.26.refs_0_.same), channel_id=1, source_target_pairs={{0,4},{2,18},{4,8},{6,22},{8,12},{10,26},{12,0},{14,30},{16,20},{1... | collective-permute-start | bytes 1474568 | tf_op jit(solution)/shard_map/ppermute | solution.py:29
  6.4 1.6 %collective-permute-start.8 = (bf16[384,640]{1,0:T(8,128)(2,1)S(1)}, bf16[384,640]{1,0:T(8,128)(2,1)S(1)}, u32[]{:S(2)}, u32[]{:S(2)}) collective-permute-start(bf16[384,640]{1,0:T(8,128)(2,1)S(1)} %get-tuple-element.26.refs_0_.same), channel_id=1, source_target_pairs={{0,12},{2,50},{4,0},{6,54},{8,4},{10,58},{12,8},{14,62},{16,28},{1... | collective-permute-start | bytes 1474568 | tf_op jit(solution)/shard_map/ppermute | solution.py:29
  8.0 0.0 collective-permute-done
  8.1 3.2 %collective-permute-start.3 = (bf16[192,640]{1,0:T(8,128)(2,1)S(1)}, bf16[192,640]{1,0:T(8,128)(2,1)S(1)}, u32[]{:S(2)}, u32[]{:S(2)}) collective-permute-start(bf16[192,640]{1,0:T(8,128)(2,1)S(1)} %pad_maximum_fusion.3), channel_id=1, source_target_pairs={{0,1},{1,0},{2,3},{3,2},{4,5},{5,4},{6,7},{7,6},{8,9},{9,8},{10,11... | collective-permute-start | bytes 737288 | tf_op jit(solution)/shard_map/ppermute | solution.py:48
  11.3 0.5 collective-permute-start.1
  11.8 2.8 %collective-permute-start.2 = (bf16[384,640]{1,0:T(8,128)(2,1)S(1)}, bf16[384,640]{1,0:T(8,128)(2,1)S(1)}, u32[]{:S(2)}, u32[]{:S(2)}) collective-permute-start(bf16[384,640]{1,0:T(8,128)(2,1)S(1)} %slice.47.refs_1_.other), channel_id=1, source_target_pairs={{0,12},{2,50},{4,0},{6,54},{8,4},{10,58},{12,8},{14,62},{16,28},{1... | collective-permute-start | bytes 1474568 | tf_op jit(solution)/shard_map/ppermute | solution.py:29
  14.6 0.2 collective-permute-done.7.refs_2_.refs_0_
  14.8 0.4 collective-permute-done.8.refs_4_.refs_2_
  15.3 3.2 %collective-permute-done.3 = bf16[192,640]{1,0:T(8,128)(2,1)S(1)} collective-permute-done((bf16[192,640]{1,0:T(8,128)(2,1)S(1)}, bf16[192,640]{1,0:T(8,128)(2,1)S(1)}, u32[]{:S(2)}, u32[]{:S(2)}) %collective-permute-start.3) | collective-permute-done | bytes 245792 | tf_op jit(solution)/shard_map/ppermute | solution.py:48
  18.5 0.0 copy-start
  18.5 0.0 copy-start.1
  18.6 0.2 collective-permute-start.4
  18.7 3.2 %collective-permute-start.5 = (bf16[384,640]{1,0:T(8,128)(2,1)S(1)}, bf16[384,640]{1,0:T(8,128)(2,1)S(1)}, u32[]{:S(2)}, u32[]{:S(2)}) collective-permute-start(bf16[384,640]{1,0:T(8,128)(2,1)S(1)} %pad_maximum_fusion.q_ref), channel_id=1, source_target_pairs={{0,48},{2,14},{4,52},{6,2},{8,56},{10,6},{12,60},{14,10},{16,0},{1... | collective-permute-start | bytes 1474568 | tf_op jit(solution)/shard_map/ppermute | solution.py:29
  21.9 0.8 collective-permute-start.12
  22.7 0.0 collective-permute-done.1.refs_3_.refs_1_
  22.8 1.6 %collective-permute-start.9 = (bf16[384,640]{1,0:T(8,128)(2,1)S(1)}, bf16[384,640]{1,0:T(8,128)(2,1)S(1)}, u32[]{:S(2)}, u32[]{:S(2)}) collective-permute-start(bf16[384,640]{1,0:T(8,128)(2,1)S(1)} %pad_maximum_fusion.1), channel_id=1, source_target_pairs={{0,4},{2,18},{4,8},{6,22},{8,12},{10,26},{12,0},{14,30},{16,20},{1... | collective-permute-start | bytes 1474568 | tf_op jit(solution)/shard_map/ppermute | solution.py:29
  24.4 0.0 collective-permute-done.2.refs_5_.refs_3_
  24.5 1.7 %collective-permute-start.10 = (bf16[384,640]{1,0:T(8,128)(2,1)S(1)}, bf16[384,640]{1,0:T(8,128)(2,1)S(1)}, u32[]{:S(2)}, u32[]{:S(2)}) collective-permute-start(bf16[384,640]{1,0:T(8,128)(2,1)S(1)} %pad_maximum_fusion.2), channel_id=1, source_target_pairs={{0,12},{2,50},{4,0},{6,54},{8,4},{10,58},{12,8},{14,62},{16,28},{1... | collective-permute-start | bytes 1474568 | tf_op jit(solution)/shard_map/ppermute | solution.py:29
  26.2 5.3 %collective-permute-done.4.q_ref = bf16[384,640]{1,0:T(8,128)(2,1)S(1)} collective-permute-done((bf16[384,640]{1,0:T(8,128)(2,1)S(1)}, bf16[384,640]{1,0:T(8,128)(2,1)S(1)}, u32[]{:S(2)}, u32[]{:S(2)}) %collective-permute-start.4) | collective-permute-done | bytes 491552 | tf_op jit(solution)/shard_map/ppermute | solution.py:29
  31.5 1.5 %collective-permute-done.5.q_ref = bf16[384,640]{1,0:T(8,128)(2,1)S(1)} collective-permute-done((bf16[384,640]{1,0:T(8,128)(2,1)S(1)}, bf16[384,640]{1,0:T(8,128)(2,1)S(1)}, u32[]{:S(2)}, u32[]{:S(2)}) %collective-permute-start.5) | collective-permute-done | bytes 491552 | tf_op jit(solution)/shard_map/ppermute | solution.py:29
  33.0 0.0 copy-done
  33.0 3.4 %collective-permute-start.6 = (bf16[192,1280]{1,0:T(8,128)(2,1)S(1)}, bf16[192,1280]{1,0:T(8,128)(2,1)S(1)}, u32[]{:S(2)}, u32[]{:S(2)}) collective-permute-start(bf16[192,1280]{1,0:T(8,128)(2,1)S(1)} %shard_map.95), channel_id=1, source_target_pairs={{0,1},{1,0},{2,3},{3,2},{4,5},{5,4},{6,7},{7,6},{8,9},{9,8},{10,11... | collective-permute-start | bytes 1474568 | tf_op jit(solution)/shard_map/ppermute | solution.py:48
  36.4 3.2 %collective-permute-done.12.q_ref = bf16[384,640]{1,0:T(8,128)(2,1)S(1)} collective-permute-done((bf16[384,640]{1,0:T(8,128)(2,1)S(1)}, bf16[384,640]{1,0:T(8,128)(2,1)S(1)}, u32[]{:S(2)}, u32[]{:S(2)}) %collective-permute-start.12) | collective-permute-done | bytes 491552 | tf_op jit(solution)/shard_map/ppermute | solution.py:29
  39.6 0.0 collective-permute-done.9.refs_6_.refs_4_
  39.6 0.0 collective-permute-done.10.refs_7_.refs_5_
  39.6 3.8 %shard_map.99 = bf16[384,768]{1,0:T(8,128)(2,1)S(1)} custom-call(bf16[384,640]{1,0:T(8,128)(2,1)S(1)} %collective-permute-done.12.q_ref, bf16[384,640]{1,0:T(8,128)(2,1)S(1)} %get-tuple-element.26.refs_0_.same, bf16[384,640]{1,0:T(8,128)(2,1)S(1)} %slice.47.refs_1_.other, bf16[384,640]{1,0:T(8,128)(2,1)S(1)} %collective-permute-done.7.refs_2_.refs_0_, ...), custom_call_target="tpu_custom_call" | custom-call | flops 1509949440 | bytes 4194304 | tf_op jit(solution)/shard_map/pallas_call | solution.py:236
  43.4 0.0 slice-start.1
  43.4 2.3 %collective-permute-start.13 = (bf16[384,768]{1,0:T(8,128)(2,1)S(1)}, bf16[384,768]{1,0:T(8,128)(2,1)S(1)}, u32[]{:S(2)}, u32[]{:S(2)}) collective-permute-start(bf16[384,768]{1,0:T(8,128)(2,1)S(1)} %shard_map.99), channel_id=1, source_target_pairs={{0,32},{2,10},{4,36},{6,14},{8,40},{10,2},{12,44},{14,6},{16,48},{... | collective-permute-start | bytes 1769480 | tf_op jit(solution)/shard_map/ppermute | solution.py:29
  45.8 3.8 %shard_map.96 = bf16[384,768]{1,0:T(8,128)(2,1)S(1)} custom-call(bf16[384,640]{1,0:T(8,128)(2,1)S(1)} %collective-permute-done.5.q_ref, bf16[384,640]{1,0:T(8,128)(2,1)S(1)} %get-tuple-element.26.refs_0_.same, bf16[384,640]{1,0:T(8,128)(2,1)S(1)} %slice.47.refs_1_.other, bf16[384,640]{1,0:T(8,128)(2,1)S(1)} %collective-permute-done.7.refs_2_.refs_0_, ...), custom_call_target="tpu_custom_call" | custom-call | flops 1509949440 | bytes 4194304 | tf_op jit(solution)/shard_map/pallas_call | solution.py:236
  49.5 0.0 collective-permute-done.6.got_ref
  49.5 1.6 %shard_map.97 = (bf16[192,1280]{1,0:T(8,128)(2,1)}, bf16[192,1280]{1,0:T(8,128)(2,1)}, bf16[384,640]{1,0:T(8,128)(2,1)S(1)}, bf16[384,640]{1,0:T(8,128)(2,1)S(1)}) custom-call(s32[2]{0:T(128)S(1)} %pad_add_fusion.table_ref, bf16[96,2560]{1,0:T(8,128)(2,1)S(1)} %bitcast.14, bf16[96,2560]{1,0:T(8,128)(2,1)S(1)} %bitcast.16, ...), custom_call_target="tpu_custom_call" | custom-call | tf_op jit(solution)/shard_map/pallas_call | solution.py:146
  51.1 0.0 collective-permute-start.11
  51.1 3.8 %shard_map.100 = bf16[384,768]{1,0:T(8,128)(2,1)S(1)} custom-call(bf16[384,640]{1,0:T(8,128)(2,1)S(1)} %collective-permute-done.4.q_ref, bf16[384,640]{1,0:T(8,128)(2,1)S(1)} %get-tuple-element.26.refs_0_.same, bf16[384,640]{1,0:T(8,128)(2,1)S(1)} %slice.47.refs_1_.other, bf16[384,640]{1,0:T(8,128)(2,1)S(1)} %collective-permute-done.7.refs_2_.refs_0_, ...), custom_call_target="tpu_custom_call" | custom-call | flops 1509949440 | bytes 4194304 | tf_op jit(solution)/shard_map/pallas_call | solution.py:236
  54.9 2.9 %collective-permute-start.14 = (bf16[384,768]{1,0:T(8,128)(2,1)S(1)}, bf16[384,768]{1,0:T(8,128)(2,1)S(1)}, u32[]{:S(2)}, u32[]{:S(2)}) collective-permute-start(bf16[384,768]{1,0:T(8,128)(2,1)S(1)} %shard_map.100), channel_id=1, source_target_pairs={{0,48},{2,14},{4,52},{6,2},{8,56},{10,6},{12,60},{14,10},{16,0},{1... | collective-permute-start | bytes 1769480 | tf_op jit(solution)/shard_map/ppermute | solution.py:29
  57.8 0.0 collective-permute-start.15
  57.8 0.0 collective-permute-done.11.refs_7_
  57.8 3.9 %shard_map.98.a_ref = bf16[384,768]{1,0:T(8,128)(2,1)S(1)} custom-call(bf16[384,640]{1,0:T(8,128)(2,1)S(1)} %pad_maximum_fusion.q_ref, bf16[384,640]{1,0:T(8,128)(2,1)S(1)} %get-tuple-element.26.refs_0_.same, bf16[384,640]{1,0:T(8,128)(2,1)S(1)} %slice.47.refs_1_.other, bf16[384,640]{1,0:T(8,128)(2,1)S(1)} %collective-permute-done.7.refs_2_.refs_0_, ...), custom_call_target="tpu_custom_call" | custom-call | flops 1509949440 | bytes 4194304 | tf_op jit(solution)/shard_map/pallas_call | solution.py:236
  61.6 0.0 copy-start.5
  61.7 0.0 collective-permute-done.13.b_ref
  61.7 3.5 %collective-permute-done.14.c_ref = bf16[384,768]{1,0:T(8,128)(2,1)S(1)} collective-permute-done((bf16[384,768]{1,0:T(8,128)(2,1)S(1)}, bf16[384,768]{1,0:T(8,128)(2,1)S(1)}, u32[]{:S(2)}, u32[]{:S(2)}) %collective-permute-start.14) | collective-permute-done | bytes 589856 | tf_op jit(solution)/shard_map/ppermute | solution.py:29
  65.2 3.7 %collective-permute-done.15.d_ref = bf16[384,768]{1,0:T(8,128)(2,1)S(1)} collective-permute-done((bf16[384,768]{1,0:T(8,128)(2,1)S(1)}, bf16[384,768]{1,0:T(8,128)(2,1)S(1)}, u32[]{:S(2)}, u32[]{:S(2)}) %collective-permute-start.15) | collective-permute-done | bytes 589856 | tf_op jit(solution)/shard_map/ppermute | solution.py:29
  68.9 0.8 shard_map.102
  69.7 0.1 collective-permute-start.16
  69.8 0.8 shard_map.101.a_ref
  70.6 0.7 collective-permute-done.16.b_ref
  71.3 1.7 %shard_map.103 = (bf16[96,1536]{1,0:T(8,128)(2,1)S(1)}, bf16[96,1536]{1,0:T(8,128)(2,1)S(1)}) custom-call(s32[1]{0:T(128)} %bitcast.1.core_ref, bf16[192,640]{1,0:T(8,128)(2,1)S(1)} %shard_map.101.a_ref, bf16[192,640]{1,0:T(8,128)(2,1)S(1)} %collective-permute-done.16.b_ref, bf16[1280,5120]{1,0:T(8,128)(2,1)S(1)} %bitcast.11, f32[1,5120]{1,0:T(1,128)S(1)} %copy-done.5), custom_call_target="tpu_custom_call" | custom-call | flops 754974720 | bytes 3932160 | tf_op jit(solution)/shard_map/pallas_call | solution.py:296
  73.0 2.8 %collective-permute-start.18 = (bf16[96,1536]{1,0:T(8,128)(2,1)S(1)}, bf16[96,1536]{1,0:T(8,128)(2,1)S(1)}, u32[]{:S(2)}, u32[]{:S(2)}) collective-permute-start(bf16[96,1536]{1,0:T(8,128)(2,1)S(1)} %get-tuple-element.36), channel_id=1, source_target_pairs={{0,65},{1,64},{64,1},{65,0},{2,67},{3,66},{66,3},{67,2},{4,69},{5,... | collective-permute-start | bytes 884744 | tf_op jit(solution)/shard_map/ppermute | solution.py:53
  75.9 0.1 collective-permute-start.17
  75.9 3.8 %shard_map.104 = (bf16[96,3584]{1,0:T(8,128)(2,1)S(1)}, bf16[96,3584]{1,0:T(8,128)(2,1)S(1)}) custom-call(s32[1]{0:T(128)} %bitcast.1.core_ref, bf16[192,640]{1,0:T(8,128)(2,1)S(1)} %shard_map.101.a_ref, bf16[192,640]{1,0:T(8,128)(2,1)S(1)} %collective-permute-done.16.b_ref, bf16[1280,5120]{1,0:T(8,128)(2,1)S(1)} %bitcast.12, f32[1,5120]{1,0:T(1,128)S(1)} %copy-done.5), custom_call_target="tpu_custom_call" | custom-call | flops 1761607680 | bytes 9175040 | tf_op jit(solution)/shard_map/pallas_call | solution.py:296
  79.8 1.2 %collective-permute-start.20 = (bf16[96,3584]{1,0:T(8,128)(2,1)S(1)}, bf16[96,3584]{1,0:T(8,128)(2,1)S(1)}, u32[]{:S(2)}, u32[]{:S(2)}) collective-permute-start(bf16[96,3584]{1,0:T(8,128)(2,1)S(1)} %get-tuple-element.38), channel_id=1, source_target_pairs={{0,65},{1,64},{64,1},{65,0},{2,67},{3,66},{66,3},{67,2},{4,69},{5,... | collective-permute-start | bytes 2064392 | tf_op jit(solution)/shard_map/ppermute | solution.py:53
  81.0 0.9 collective-permute-start.19
  81.9 1.4 %collective-permute-done.18 = bf16[96,1536]{1,0:T(8,128)(2,1)S(1)} collective-permute-done((bf16[96,1536]{1,0:T(8,128)(2,1)S(1)}, bf16[96,1536]{1,0:T(8,128)(2,1)S(1)}, u32[]{:S(2)}, u32[]{:S(2)}) %collective-permute-start.18) | collective-permute-done | bytes 294944 | tf_op jit(solution)/shard_map/ppermute | solution.py:53
  83.4 2.4 %collective-permute-done.17 = bf16[96,1536]{1,0:T(8,128)(2,1)S(1)} collective-permute-done((bf16[96,1536]{1,0:T(8,128)(2,1)S(1)}, bf16[96,1536]{1,0:T(8,128)(2,1)S(1)}, u32[]{:S(2)}, u32[]{:S(2)}) %collective-permute-start.17) | collective-permute-done | bytes 294944 | tf_op jit(solution)/shard_map/ppermute | solution.py:53
  85.8 0.1 add_convert_fusion.1
  85.8 12.4 %collective-permute-done.20 = bf16[96,3584]{1,0:T(8,128)(2,1)S(1)} collective-permute-done((bf16[96,3584]{1,0:T(8,128)(2,1)S(1)}, bf16[96,3584]{1,0:T(8,128)(2,1)S(1)}, u32[]{:S(2)}, u32[]{:S(2)}) %collective-permute-start.20) | collective-permute-done | bytes 688160 | tf_op jit(solution)/shard_map/ppermute | solution.py:53
  98.2 1.2 %collective-permute-done.19 = bf16[96,3584]{1,0:T(8,128)(2,1)S(1)} collective-permute-done((bf16[96,3584]{1,0:T(8,128)(2,1)S(1)}, bf16[96,3584]{1,0:T(8,128)(2,1)S(1)}, u32[]{:S(2)}, u32[]{:S(2)}) %collective-permute-start.19) | collective-permute-done | bytes 688160 | tf_op jit(solution)/shard_map/ppermute | solution.py:53
  99.4 0.2 add_convert_fusion
  99.5 1.0 %maximum_bitcast_fusion = bf16[1,96,5120]{2,1,0:T(8,128)(2,1)} fusion(bf16[96,3584]{1,0:T(8,128)(2,1)S(1)} %add_convert_fusion, bf16[96,1536]{1,0:T(8,128)(2,1)S(1)} %add_convert_fusion.1), kind=kLoop, calls=%fused_computation.1 | loop fusion | flops 1966080 | bytes 1966080 | tf_op jit(solution)/shard_map/broadcast_in_dim | solution.py:363
  (26 shorter events, 0.4 us)
Async XLA Ops:
  0.7 1.0 %copy-start.2 = (bf16[1,192,1280]{2,1,0:T(8,128)(2,1)S(1)}, bf16[1,192,1280]{2,1,0:T(8,128)(2,1)}, u32[]{:S(2)}) copy-start(bf16[1,192,1280]{2,1,0:T(8,128)(2,1)} %k_ref.1) | copy-start | bytes 1474564
  1.7 1.0 %copy-start.3 = (bf16[1,192,1280]{2,1,0:T(8,128)(2,1)S(1)}, bf16[1,192,1280]{2,1,0:T(8,128)(2,1)}, u32[]{:S(2)}) copy-start(bf16[1,192,1280]{2,1,0:T(8,128)(2,1)} %v_ref.1) | copy-start | bytes 1474564
  2.8 1.0 %copy-start.4 = (bf16[1,96,2560]{2,1,0:T(8,128)(2,1)S(1)}, bf16[1,96,2560]{2,1,0:T(8,128)(2,1)}, u32[]{:S(2)}) copy-start(bf16[1,96,2560]{2,1,0:T(8,128)(2,1)} %q_ref.1) | copy-start | bytes 1474564
  4.6 3.4 %collective-permute-start = (bf16[576,640]{1,0:T(8,128)(2,1)S(1)}, bf16[576,640]{1,0:T(8,128)(2,1)S(1)}, u32[]{:S(2)}, u32[]{:S(2)}) collective-permute-start(bf16[576,640]{1,0:T(8,128)(2,1)S(1)} %get-tuple-element.21), channel_id=1, source_target_pairs={{0,2},{2,0},{4,6},{6,4},{8,10},{10,8},{12,14},{14,12},{16,18},{18,... | collective-permute-start | bytes 2211848 | tf_op jit(solution)/shard_map/ppermute | solution.py:41
  4.7 10.1 %collective-permute-start.7 = (bf16[384,640]{1,0:T(8,128)(2,1)S(1)}, bf16[384,640]{1,0:T(8,128)(2,1)S(1)}, u32[]{:S(2)}, u32[]{:S(2)}) collective-permute-start(bf16[384,640]{1,0:T(8,128)(2,1)S(1)} %get-tuple-element.26.refs_0_.same), channel_id=1, source_target_pairs={{0,4},{2,18},{4,8},{6,22},{8,12},{10,26},{12,0},{14,30},{16,20},{1... | collective-permute-start | bytes 1474568 | tf_op jit(solution)/shard_map/ppermute | solution.py:29
  6.4 8.8 %collective-permute-start.8 = (bf16[384,640]{1,0:T(8,128)(2,1)S(1)}, bf16[384,640]{1,0:T(8,128)(2,1)S(1)}, u32[]{:S(2)}, u32[]{:S(2)}) collective-permute-start(bf16[384,640]{1,0:T(8,128)(2,1)S(1)} %get-tuple-element.26.refs_0_.same), channel_id=1, source_target_pairs={{0,12},{2,50},{4,0},{6,54},{8,4},{10,58},{12,8},{14,62},{16,28},{1... | collective-permute-start | bytes 1474568 | tf_op jit(solution)/shard_map/ppermute | solution.py:29
  8.1 10.3 %collective-permute-start.3 = (bf16[192,640]{1,0:T(8,128)(2,1)S(1)}, bf16[192,640]{1,0:T(8,128)(2,1)S(1)}, u32[]{:S(2)}, u32[]{:S(2)}) collective-permute-start(bf16[192,640]{1,0:T(8,128)(2,1)S(1)} %pad_maximum_fusion.3), channel_id=1, source_target_pairs={{0,1},{1,0},{2,3},{3,2},{4,5},{5,4},{6,7},{7,6},{8,9},{9,8},{10,11... | collective-permute-start | bytes 737288 | tf_op jit(solution)/shard_map/ppermute | solution.py:48
  11.3 11.4 %collective-permute-start.1 = (bf16[384,640]{1,0:T(8,128)(2,1)S(1)}, bf16[384,640]{1,0:T(8,128)(2,1)S(1)}, u32[]{:S(2)}, u32[]{:S(2)}) collective-permute-start(bf16[384,640]{1,0:T(8,128)(2,1)S(1)} %slice.47.refs_1_.other), channel_id=1, source_target_pairs={{0,4},{2,18},{4,8},{6,22},{8,12},{10,26},{12,0},{14,30},{16,20},{1... | collective-permute-start | bytes 1474568 | tf_op jit(solution)/shard_map/ppermute | solution.py:29
  11.8 12.6 %collective-permute-start.2 = (bf16[384,640]{1,0:T(8,128)(2,1)S(1)}, bf16[384,640]{1,0:T(8,128)(2,1)S(1)}, u32[]{:S(2)}, u32[]{:S(2)}) collective-permute-start(bf16[384,640]{1,0:T(8,128)(2,1)S(1)} %slice.47.refs_1_.other), channel_id=1, source_target_pairs={{0,12},{2,50},{4,0},{6,54},{8,4},{10,58},{12,8},{14,62},{16,28},{1... | collective-permute-start | bytes 1474568 | tf_op jit(solution)/shard_map/ppermute | solution.py:29
  18.5 14.5 %copy-start = (bf16[1,96,2560]{2,1,0:T(8,128)(2,1)S(1)}, bf16[1,96,2560]{2,1,0:T(8,128)(2,1)}, u32[]{:S(2)}) copy-start(bf16[1,96,2560]{2,1,0:T(8,128)(2,1)} %param.8) | copy-start | bytes 1474564
  18.5 14.5 %copy-start.1 = (bf16[1,96,2560]{2,1,0:T(8,128)(2,1)S(1)}, bf16[1,96,2560]{2,1,0:T(8,128)(2,1)}, u32[]{:S(2)}) copy-start(bf16[1,96,2560]{2,1,0:T(8,128)(2,1)} %param.9) | copy-start | bytes 1474564
  18.6 13.0 %collective-permute-start.4 = (bf16[384,640]{1,0:T(8,128)(2,1)S(1)}, bf16[384,640]{1,0:T(8,128)(2,1)S(1)}, u32[]{:S(2)}, u32[]{:S(2)}) collective-permute-start(bf16[384,640]{1,0:T(8,128)(2,1)S(1)} %pad_maximum_fusion.q_ref), channel_id=1, source_target_pairs={{0,16},{2,6},{4,20},{6,10},{8,24},{10,14},{12,28},{14,2},{16,32},{... | collective-permute-start | bytes 1474568 | tf_op jit(solution)/shard_map/ppermute | solution.py:29
  18.7 14.3 %collective-permute-start.5 = (bf16[384,640]{1,0:T(8,128)(2,1)S(1)}, bf16[384,640]{1,0:T(8,128)(2,1)S(1)}, u32[]{:S(2)}, u32[]{:S(2)}) collective-permute-start(bf16[384,640]{1,0:T(8,128)(2,1)S(1)} %pad_maximum_fusion.q_ref), channel_id=1, source_target_pairs={{0,48},{2,14},{4,52},{6,2},{8,56},{10,6},{12,60},{14,10},{16,0},{1... | collective-permute-start | bytes 1474568 | tf_op jit(solution)/shard_map/ppermute | solution.py:29
  21.9 17.8 %collective-permute-start.12 = (bf16[384,640]{1,0:T(8,128)(2,1)S(1)}, bf16[384,640]{1,0:T(8,128)(2,1)S(1)}, u32[]{:S(2)}, u32[]{:S(2)}) collective-permute-start(bf16[384,640]{1,0:T(8,128)(2,1)S(1)} %pad_maximum_fusion.q_ref), channel_id=1, source_target_pairs={{0,32},{2,10},{4,36},{6,14},{8,40},{10,2},{12,44},{14,6},{16,48},{... | collective-permute-start | bytes 1474568 | tf_op jit(solution)/shard_map/ppermute | solution.py:29
  22.8 16.9 %collective-permute-start.9 = (bf16[384,640]{1,0:T(8,128)(2,1)S(1)}, bf16[384,640]{1,0:T(8,128)(2,1)S(1)}, u32[]{:S(2)}, u32[]{:S(2)}) collective-permute-start(bf16[384,640]{1,0:T(8,128)(2,1)S(1)} %pad_maximum_fusion.1), channel_id=1, source_target_pairs={{0,4},{2,18},{4,8},{6,22},{8,12},{10,26},{12,0},{14,30},{16,20},{1... | collective-permute-start | bytes 1474568 | tf_op jit(solution)/shard_map/ppermute | solution.py:29
  24.5 15.1 %collective-permute-start.10 = (bf16[384,640]{1,0:T(8,128)(2,1)S(1)}, bf16[384,640]{1,0:T(8,128)(2,1)S(1)}, u32[]{:S(2)}, u32[]{:S(2)}) collective-permute-start(bf16[384,640]{1,0:T(8,128)(2,1)S(1)} %pad_maximum_fusion.2), channel_id=1, source_target_pairs={{0,12},{2,50},{4,0},{6,54},{8,4},{10,58},{12,8},{14,62},{16,28},{1... | collective-permute-start | bytes 1474568 | tf_op jit(solution)/shard_map/ppermute | solution.py:29
  33.0 16.5 %collective-permute-start.6 = (bf16[192,1280]{1,0:T(8,128)(2,1)S(1)}, bf16[192,1280]{1,0:T(8,128)(2,1)S(1)}, u32[]{:S(2)}, u32[]{:S(2)}) collective-permute-start(bf16[192,1280]{1,0:T(8,128)(2,1)S(1)} %shard_map.95), channel_id=1, source_target_pairs={{0,1},{1,0},{2,3},{3,2},{4,5},{5,4},{6,7},{7,6},{8,9},{9,8},{10,11... | collective-permute-start | bytes 1474568 | tf_op jit(solution)/shard_map/ppermute | solution.py:48
  39.6 31.7 %slice-start = ((s8[13107200]{0:T(1024)(128)(4,1)}), s8[4194304]{0:T(1024)(128)(4,1)S(1)}, s32[]{:S(2)}) async-start(s8[13107200]{0:T(1024)(128)(4,1)} %bitcast.9), calls=%async_computation | async-start | bytes 8388608
  43.4 27.9 %slice-start.1 = ((s8[13107200]{0:T(1024)(128)(4,1)}), s8[4194304]{0:T(1024)(128)(4,1)S(1)}, s32[]{:S(2)}) async-start(s8[13107200]{0:T(1024)(128)(4,1)} %bitcast.9), calls=%async_computation.1 | async-start | bytes 8388608
  43.4 18.2 %collective-permute-start.13 = (bf16[384,768]{1,0:T(8,128)(2,1)S(1)}, bf16[384,768]{1,0:T(8,128)(2,1)S(1)}, u32[]{:S(2)}, u32[]{:S(2)}) collective-permute-start(bf16[384,768]{1,0:T(8,128)(2,1)S(1)} %shard_map.99), channel_id=1, source_target_pairs={{0,32},{2,10},{4,36},{6,14},{8,40},{10,2},{12,44},{14,6},{16,48},{... | collective-permute-start | bytes 1769480 | tf_op jit(solution)/shard_map/ppermute | solution.py:29
  51.1 20.2 %slice-start.2 = ((s8[13107200]{0:T(1024)(128)(4,1)}), s8[4194304]{0:T(1024)(128)(4,1)S(1)}, s32[]{:S(2)}) async-start(s8[13107200]{0:T(1024)(128)(4,1)} %bitcast.9), calls=%async_computation.2 | async-start | bytes 8388608
  51.1 6.6 %collective-permute-start.11 = (bf16[384,640]{1,0:T(8,128)(2,1)S(1)}, bf16[384,640]{1,0:T(8,128)(2,1)S(1)}, u32[]{:S(2)}, u32[]{:S(2)}) collective-permute-start(bf16[384,640]{1,0:T(8,128)(2,1)S(1)} %get-tuple-element.33), channel_id=1, source_target_pairs={{0,2},{2,0},{4,6},{6,4},{8,10},{10,8},{12,14},{14,12},{16,18},{18,... | collective-permute-start | bytes 1474568 | tf_op jit(solution)/shard_map/ppermute | solution.py:41
  54.9 10.3 %collective-permute-start.14 = (bf16[384,768]{1,0:T(8,128)(2,1)S(1)}, bf16[384,768]{1,0:T(8,128)(2,1)S(1)}, u32[]{:S(2)}, u32[]{:S(2)}) collective-permute-start(bf16[384,768]{1,0:T(8,128)(2,1)S(1)} %shard_map.100), channel_id=1, source_target_pairs={{0,48},{2,14},{4,52},{6,2},{8,56},{10,6},{12,60},{14,10},{16,0},{1... | collective-permute-start | bytes 1769480 | tf_op jit(solution)/shard_map/ppermute | solution.py:29
  57.8 11.1 %collective-permute-start.15 = (bf16[384,768]{1,0:T(8,128)(2,1)S(1)}, bf16[384,768]{1,0:T(8,128)(2,1)S(1)}, u32[]{:S(2)}, u32[]{:S(2)}) collective-permute-start(bf16[384,768]{1,0:T(8,128)(2,1)S(1)} %shard_map.96), channel_id=1, source_target_pairs={{0,16},{2,6},{4,20},{6,10},{8,24},{10,14},{12,28},{14,2},{16,32},{... | collective-permute-start | bytes 1769480 | tf_op jit(solution)/shard_map/ppermute | solution.py:29
  57.8 13.5 %slice-start.3 = ((s8[13107200]{0:T(1024)(128)(4,1)}), s8[524288]{0:T(1024)(128)(4,1)S(1)}, s32[]{:S(2)}) async-start(s8[13107200]{0:T(1024)(128)(4,1)} %bitcast.9), calls=%async_computation.3 | async-start | bytes 1048576
  61.6 9.7 %copy-start.5 = (f32[1,5120]{1,0:T(1,128)S(1)}, f32[1,5120]{1,0:T(1,128)}, u32[]{:S(2)}) copy-start(f32[1,5120]{1,0:T(1,128)} %g_ref.3) | copy-start | bytes 61444
  69.7 1.6 %collective-permute-start.16 = (bf16[192,640]{1,0:T(8,128)(2,1)S(1)}, bf16[192,640]{1,0:T(8,128)(2,1)S(1)}, u32[]{:S(2)}, u32[]{:S(2)}) collective-permute-start(bf16[192,640]{1,0:T(8,128)(2,1)S(1)} %shard_map.102), channel_id=1, source_target_pairs={{0,2},{2,0},{4,6},{6,4},{8,10},{10,8},{12,14},{14,12},{16,18},{18,... | collective-permute-start | bytes 737288 | tf_op jit(solution)/shard_map/ppermute | solution.py:41
  73.0 10.3 %collective-permute-start.18 = (bf16[96,1536]{1,0:T(8,128)(2,1)S(1)}, bf16[96,1536]{1,0:T(8,128)(2,1)S(1)}, u32[]{:S(2)}, u32[]{:S(2)}) collective-permute-start(bf16[96,1536]{1,0:T(8,128)(2,1)S(1)} %get-tuple-element.36), channel_id=1, source_target_pairs={{0,65},{1,64},{64,1},{65,0},{2,67},{3,66},{66,3},{67,2},{4,69},{5,... | collective-permute-start | bytes 884744 | tf_op jit(solution)/shard_map/ppermute | solution.py:53
  75.9 9.9 %collective-permute-start.17 = (bf16[96,1536]{1,0:T(8,128)(2,1)S(1)}, bf16[96,1536]{1,0:T(8,128)(2,1)S(1)}, u32[]{:S(2)}, u32[]{:S(2)}) collective-permute-start(bf16[96,1536]{1,0:T(8,128)(2,1)S(1)} %get-tuple-element.35), channel_id=1, source_target_pairs={{0,64},{1,65},{64,0},{65,1},{2,66},{3,67},{66,2},{67,3},{4,68},{5,... | collective-permute-start | bytes 884744 | tf_op jit(solution)/shard_map/ppermute | solution.py:53
  79.8 18.4 %collective-permute-start.20 = (bf16[96,3584]{1,0:T(8,128)(2,1)S(1)}, bf16[96,3584]{1,0:T(8,128)(2,1)S(1)}, u32[]{:S(2)}, u32[]{:S(2)}) collective-permute-start(bf16[96,3584]{1,0:T(8,128)(2,1)S(1)} %get-tuple-element.38), channel_id=1, source_target_pairs={{0,65},{1,64},{64,1},{65,0},{2,67},{3,66},{66,3},{67,2},{4,69},{5,... | collective-permute-start | bytes 2064392 | tf_op jit(solution)/shard_map/ppermute | solution.py:53
  81.0 18.4 %collective-permute-start.19 = (bf16[96,3584]{1,0:T(8,128)(2,1)S(1)}, bf16[96,3584]{1,0:T(8,128)(2,1)S(1)}, u32[]{:S(2)}, u32[]{:S(2)}) collective-permute-start(bf16[96,3584]{1,0:T(8,128)(2,1)S(1)} %get-tuple-element.37), channel_id=1, source_target_pairs={{0,64},{1,65},{64,0},{65,1},{2,66},{3,67},{66,2},{67,3},{4,68},{5,... | collective-permute-start | bytes 2064392 | tf_op jit(solution)/shard_map/ppermute | solution.py:53

commit v3 on v2

--- a/solution.py
+++ b/solution.py
@@ -24,7 +24,7 @@
     for z in range(CHIPS):
         for y in range(CHIPS):
             for core in range(2):
-                to = place(z, y + steps, core) if core == core_on_y else place(z + steps, y, core)
+                to = place(z, y - steps, core) if core == core_on_y else place(z - steps, y, core)
                 pairs.append((place(z, y, core), to))
     return lax.ppermute(value, "patch", pairs)
 
@@ -336,21 +336,23 @@
     k_far = keys_along(jnp.concatenate([up_same[:patch], up_other[:patch]], axis=0), 1)
     v_far = keys_along(jnp.concatenate([down_same[patch:], down_other[patch:]], axis=0), -1)
 
-    fresh_keys, fresh_values, up_other, down_other, q_up, q_down = lax.optimization_barrier(
-        (fresh_keys, fresh_values, up_other, down_other, q_up, q_down)
+    fresh_keys, fresh_values, up_other, down_other, q_far = lax.optimization_barrier(
+        (fresh_keys, fresh_values, up_other, down_other, q_far)
     )
     got = other_half(outgoing_fresh(head_table, fresh_keys[0], fresh_values[0]), 0, 1)
     blocks = [same, other, up_same, up_other, down_same, down_other, k_far, v_far]
     o_far = attention(remote_kernel, q_far, blocks)
     o_up = attention(remote_kernel, q_up, blocks)
     o_down = attention(remote_kernel, q_down, blocks)
-    got, _ = lax.optimization_barrier((got, o_down))
+    far, up, down = queries_along(o_far, 2), queries_along(o_up, -1), queries_along(o_down, 1)
+    got, _, _, _ = lax.optimization_barrier((got, o_far, o_up, o_down))
     new_keys, new_values, f_same, f_other = assemble_fresh(
         table, fresh_keys[0], fresh_values[0], got
     )
     f_other = other_core(f_other)
+    q_own, far, down = lax.optimization_barrier((q_own, far, down))
     o_own = attention(own_kernel, q_own, blocks + [f_same, f_other])
-    parts = (o_own, queries_along(o_far, 2), queries_along(o_up, -1), queries_along(o_down, 1))
+    parts = (o_own, far, up, down)
     theirs = other_core(combine(parts, patch))
     mine = combine(parts, 0)
     pieces = []

time: 101 us -> 98.1 us (0.971)
  waiting for transfers between devices: 39 us -> 30.1 us
  starting transfers between devices: 31.1 us -> 37.3 us
    ppermute x12, starting transfers between devices: 19.3 us -> 28.3 us  [along(): return lax.ppermute(value, 'patch', pairs)]
    ppermute x12, waiting for transfers between devices: 17.8 us -> 9.27 us  [along(): return lax.ppermute(value, 'patch', pairs)]
    ppermute x2, starting transfers between devices: 6.56 us -> 3.86 us  [other_half(): return lax.ppermute(value, ('patch', 'head'), pairs)]
  transfers between devices with their start and end apart: 21 -> 21, of which waited for: 13 -> 12; matrix products, arithmetic and copies ran while one was open for 0% -> 0% of each run, Pallas kernels for 21% -> 22%
where the time goes in v3:
time: 98.1 us; the launch traced here: 97.8 us
  starting transfers between devices  37.3 us (38%)
  waiting for transfers between devices  30.1 us (31%)
  Pallas kernels  24.7 us (25%)
  local copies, waits for them, and re-layouts  3.33 us (3%)
  other arithmetic  1.49 us (2%)
    ppermute x12, starting transfers between devices, along(): return lax.ppermute(value, 'patch', pairs)  28.3 us
    ppermute x4, waiting for transfers between devices, onward_to(): return lax.ppermute(value, ('pipe', 'head'), pairs)  17.1 us
    pallas_call x4, Pallas kernels, attention(): pl.pallas_call(kernel, out_shape=jax.ShapeDtypeStruct((rows, width + HEAD...  15.1 us
    ppermute x12, waiting for transfers between devices, along(): return lax.ppermute(value, 'patch', pairs)  9.27 us
    pallas_call x2, Pallas kernels, project(): pl.pallas_call(project_kernel, grid_spec=pltpu.PrefetchScalarGridSpec(num...  5.53 us
    ppermute x4, starting transfers between devices, onward_to(): return lax.ppermute(value, ('pipe', 'head'), pairs)  4.81 us
    ppermute x2, starting transfers between devices, other_half(): return lax.ppermute(value, ('patch', 'head'), pairs)  3.86 us
    ppermute x2, waiting for transfers between devices, other_half(): return lax.ppermute(value, ('patch', 'head'), pairs)  3.17 us
  transfers between devices with their start and end apart: 21, of which 12 were waited for; matrix products, arithmetic and copies ran while one was open for 0% of the time, Pallas kernels for 22%

profile of v3, /device:TPU:0, one launch (start us, length us, event | category | flops | bytes accessed | tf_op | source)
XLA Modules:
  0.0 97.8 jit_solution(16528665385844467703)
XLA Ops:
  0.6 0.1 pad_add_fusion.table_ref
  0.7 1.0 %copy-done.2 = bf16[1,192,1280]{2,1,0:T(8,128)(2,1)S(1)} copy-done((bf16[1,192,1280]{2,1,0:T(8,128)(2,1)S(1)}, bf16[1,192,1280]{2,1,0:T(8,128)(2,1)}, u32[]{:S(2)}) %copy-start.2) | copy-done | bytes 491544
  1.8 1.0 %copy-done.3 = bf16[1,192,1280]{2,1,0:T(8,128)(2,1)S(1)} copy-done((bf16[1,192,1280]{2,1,0:T(8,128)(2,1)S(1)}, bf16[1,192,1280]{2,1,0:T(8,128)(2,1)}, u32[]{:S(2)}) %copy-start.3) | copy-done | bytes 491544
  2.8 1.0 %copy-done.4 = bf16[1,96,2560]{2,1,0:T(8,128)(2,1)S(1)} copy-done((bf16[1,96,2560]{2,1,0:T(8,128)(2,1)S(1)}, bf16[1,96,2560]{2,1,0:T(8,128)(2,1)}, u32[]{:S(2)}) %copy-start.4) | copy-done | bytes 491544
  3.8 0.8 shard_map.94
  4.6 0.1 collective-permute-start
  4.7 1.7 %collective-permute-start.7 = (bf16[384,640]{1,0:T(8,128)(2,1)S(1)}, bf16[384,640]{1,0:T(8,128)(2,1)S(1)}, u32[]{:S(2)}, u32[]{:S(2)}) collective-permute-start(bf16[384,640]{1,0:T(8,128)(2,1)S(1)} %get-tuple-element.28.refs_0_.same), channel_id=1, source_target_pairs={{0,4},{2,18},{4,8},{6,22},{8,12},{10,26},{12,0},{14,30},{16,20},{1... | collective-permute-start | bytes 1474568 | tf_op jit(solution)/shard_map/ppermute | solution.py:29
  6.4 1.6 %collective-permute-start.6 = (bf16[384,640]{1,0:T(8,128)(2,1)S(1)}, bf16[384,640]{1,0:T(8,128)(2,1)S(1)}, u32[]{:S(2)}, u32[]{:S(2)}) collective-permute-start(bf16[384,640]{1,0:T(8,128)(2,1)S(1)} %get-tuple-element.28.refs_0_.same), channel_id=1, source_target_pairs={{0,12},{2,50},{4,0},{6,54},{8,4},{10,58},{12,8},{14,62},{16,28},{1... | collective-permute-start | bytes 1474568 | tf_op jit(solution)/shard_map/ppermute | solution.py:29
  8.0 0.0 collective-permute-done
  8.1 3.2 %collective-permute-start.3 = (bf16[192,640]{1,0:T(8,128)(2,1)S(1)}, bf16[192,640]{1,0:T(8,128)(2,1)S(1)}, u32[]{:S(2)}, u32[]{:S(2)}) collective-permute-start(bf16[192,640]{1,0:T(8,128)(2,1)S(1)} %pad_maximum_fusion.3), channel_id=1, source_target_pairs={{0,1},{1,0},{2,3},{3,2},{4,5},{5,4},{6,7},{7,6},{8,9},{9,8},{10,11... | collective-permute-start | bytes 737288 | tf_op jit(solution)/shard_map/ppermute | solution.py:48
  11.3 0.5 collective-permute-start.2
  11.8 2.8 %collective-permute-start.1 = (bf16[384,640]{1,0:T(8,128)(2,1)S(1)}, bf16[384,640]{1,0:T(8,128)(2,1)S(1)}, u32[]{:S(2)}, u32[]{:S(2)}) collective-permute-start(bf16[384,640]{1,0:T(8,128)(2,1)S(1)} %slice.47.refs_1_.other), channel_id=1, source_target_pairs={{0,12},{2,50},{4,0},{6,54},{8,4},{10,58},{12,8},{14,62},{16,28},{1... | collective-permute-start | bytes 1474568 | tf_op jit(solution)/shard_map/ppermute | solution.py:29
  14.6 0.2 collective-permute-done.7.refs_4_.refs_2_
  14.8 0.4 collective-permute-done.6.refs_2_.refs_0_
  15.3 3.2 %collective-permute-done.3 = bf16[192,640]{1,0:T(8,128)(2,1)S(1)} collective-permute-done((bf16[192,640]{1,0:T(8,128)(2,1)S(1)}, bf16[192,640]{1,0:T(8,128)(2,1)S(1)}, u32[]{:S(2)}, u32[]{:S(2)}) %collective-permute-start.3) | collective-permute-done | bytes 245792 | tf_op jit(solution)/shard_map/ppermute | solution.py:48
  18.5 0.0 copy-start
  18.5 0.0 copy-start.1
  18.6 2.1 %collective-permute-start.4 = (bf16[384,640]{1,0:T(8,128)(2,1)S(1)}, bf16[384,640]{1,0:T(8,128)(2,1)S(1)}, u32[]{:S(2)}, u32[]{:S(2)}) collective-permute-start(bf16[384,640]{1,0:T(8,128)(2,1)S(1)} %pad_maximum_fusion.q_ref), channel_id=1, source_target_pairs={{0,32},{2,10},{4,36},{6,14},{8,40},{10,2},{12,44},{14,6},{16,48},{... | collective-permute-start | bytes 1474568 | tf_op jit(solution)/shard_map/ppermute | solution.py:29
  20.7 0.8 collective-permute-done.2.refs_5_.refs_3_
  21.5 0.9 collective-permute-start.9
  22.4 0.0 collective-permute-done.1.refs_3_.refs_1_
  22.5 6.6 %collective-permute-start.8 = (bf16[384,640]{1,0:T(8,128)(2,1)S(1)}, bf16[384,640]{1,0:T(8,128)(2,1)S(1)}, u32[]{:S(2)}, u32[]{:S(2)}) collective-permute-start(bf16[384,640]{1,0:T(8,128)(2,1)S(1)} %pad_maximum_fusion.1), channel_id=1, source_target_pairs={{0,12},{2,50},{4,0},{6,54},{8,4},{10,58},{12,8},{14,62},{16,28},{1... | collective-permute-start | bytes 1474568 | tf_op jit(solution)/shard_map/ppermute | solution.py:29
  29.1 4.1 %collective-permute-start.11 = (bf16[384,640]{1,0:T(8,128)(2,1)S(1)}, bf16[384,640]{1,0:T(8,128)(2,1)S(1)}, u32[]{:S(2)}, u32[]{:S(2)}) collective-permute-start(bf16[384,640]{1,0:T(8,128)(2,1)S(1)} %pad_maximum_fusion.q_ref), channel_id=1, source_target_pairs={{0,16},{2,6},{4,20},{6,10},{8,24},{10,14},{12,28},{14,2},{16,32},{... | collective-permute-start | bytes 1474568 | tf_op jit(solution)/shard_map/ppermute | solution.py:29
  33.2 2.1 %collective-permute-start.10 = (bf16[384,640]{1,0:T(8,128)(2,1)S(1)}, bf16[384,640]{1,0:T(8,128)(2,1)S(1)}, u32[]{:S(2)}, u32[]{:S(2)}) collective-permute-start(bf16[384,640]{1,0:T(8,128)(2,1)S(1)} %pad_maximum_fusion.q_ref), channel_id=1, source_target_pairs={{0,48},{2,14},{4,52},{6,2},{8,56},{10,6},{12,60},{14,10},{16,0},{1... | collective-permute-start | bytes 1474568 | tf_op jit(solution)/shard_map/ppermute | solution.py:29
  35.3 0.0 collective-permute-done.4.q_ref
  35.4 0.7 collective-permute-start.5
  36.0 1.9 %collective-permute-done.9.refs_7_.refs_5_ = bf16[384,640]{1,0:T(8,128)(2,1)S(1)} collective-permute-done((bf16[384,640]{1,0:T(8,128)(2,1)S(1)}, bf16[384,640]{1,0:T(8,128)(2,1)S(1)}, u32[]{:S(2)}, u32[]{:S(2)}) %collective-permute-start.9) | collective-permute-done | bytes 491552 | tf_op jit(solution)/shard_map/ppermute | solution.py:29
  38.0 0.0 collective-permute-done.8.refs_6_.refs_4_
  38.0 3.8 %shard_map.96 = bf16[384,768]{1,0:T(8,128)(2,1)S(1)} custom-call(bf16[384,640]{1,0:T(8,128)(2,1)S(1)} %collective-permute-done.4.q_ref, bf16[384,640]{1,0:T(8,128)(2,1)S(1)} %get-tuple-element.28.refs_0_.same, bf16[384,640]{1,0:T(8,128)(2,1)S(1)} %slice.47.refs_1_.other, bf16[384,640]{1,0:T(8,128)(2,1)S(1)} %collective-permute-done.6.refs_2_.refs_0_, ...), custom_call_target="tpu_custom_call" | custom-call | flops 1509949440 | bytes 4194304 | tf_op jit(solution)/shard_map/pallas_call | solution.py:236
  41.8 0.0 slice-start.1
  41.8 3.8 %collective-permute-start.12 = (bf16[384,768]{1,0:T(8,128)(2,1)S(1)}, bf16[384,768]{1,0:T(8,128)(2,1)S(1)}, u32[]{:S(2)}, u32[]{:S(2)}) collective-permute-start(bf16[384,768]{1,0:T(8,128)(2,1)S(1)} %shard_map.96), channel_id=1, source_target_pairs={{0,32},{2,10},{4,36},{6,14},{8,40},{10,2},{12,44},{14,6},{16,48},{... | collective-permute-start | bytes 1769480 | tf_op jit(solution)/shard_map/ppermute | solution.py:29
  45.6 0.0 collective-permute-done.11.q_ref
  45.6 3.7 %shard_map.98 = bf16[384,768]{1,0:T(8,128)(2,1)S(1)} custom-call(bf16[384,640]{1,0:T(8,128)(2,1)S(1)} %collective-permute-done.11.q_ref, bf16[384,640]{1,0:T(8,128)(2,1)S(1)} %get-tuple-element.28.refs_0_.same, bf16[384,640]{1,0:T(8,128)(2,1)S(1)} %slice.47.refs_1_.other, bf16[384,640]{1,0:T(8,128)(2,1)S(1)} %collective-permute-done.6.refs_2_.refs_0_, ...), custom_call_target="tpu_custom_call" | custom-call | flops 1509949440 | bytes 4194304 | tf_op jit(solution)/shard_map/pallas_call | solution.py:236
  49.4 0.0 slice-start.2
  49.4 0.8 collective-permute-start.13
  50.1 0.0 collective-permute-done.10.q_ref
  50.1 3.7 %shard_map.97 = bf16[384,768]{1,0:T(8,128)(2,1)S(1)} custom-call(bf16[384,640]{1,0:T(8,128)(2,1)S(1)} %collective-permute-done.10.q_ref, bf16[384,640]{1,0:T(8,128)(2,1)S(1)} %get-tuple-element.28.refs_0_.same, bf16[384,640]{1,0:T(8,128)(2,1)S(1)} %slice.47.refs_1_.other, bf16[384,640]{1,0:T(8,128)(2,1)S(1)} %collective-permute-done.6.refs_2_.refs_0_, ...), custom_call_target="tpu_custom_call" | custom-call | flops 1509949440 | bytes 4194304 | tf_op jit(solution)/shard_map/pallas_call | solution.py:236
  53.9 0.0 collective-permute-done.5.got_ref
  53.9 1.6 %shard_map.99 = (bf16[192,1280]{1,0:T(8,128)(2,1)}, bf16[192,1280]{1,0:T(8,128)(2,1)}, bf16[384,640]{1,0:T(8,128)(2,1)S(1)}, bf16[384,640]{1,0:T(8,128)(2,1)S(1)}) custom-call(s32[2]{0:T(128)S(1)} %pad_add_fusion.table_ref, bf16[96,2560]{1,0:T(8,128)(2,1)S(1)} %bitcast.14, bf16[96,2560]{1,0:T(8,128)(2,1)S(1)} %bitcast.16, ...), custom_call_target="tpu_custom_call" | custom-call | tf_op jit(solution)/shard_map/pallas_call | solution.py:146
  55.5 0.0 collective-permute-start.14
  55.5 1.3 %collective-permute-start.15 = (bf16[384,768]{1,0:T(8,128)(2,1)S(1)}, bf16[384,768]{1,0:T(8,128)(2,1)S(1)}, u32[]{:S(2)}, u32[]{:S(2)}) collective-permute-start(bf16[384,768]{1,0:T(8,128)(2,1)S(1)} %shard_map.97), channel_id=1, source_target_pairs={{0,16},{2,6},{4,20},{6,10},{8,24},{10,14},{12,28},{14,2},{16,32},{... | collective-permute-start | bytes 1769480 | tf_op jit(solution)/shard_map/ppermute | solution.py:29
  56.8 0.0 collective-permute-done.12.b_ref
  56.8 4.0 %collective-permute-done.13.d_ref = bf16[384,768]{1,0:T(8,128)(2,1)S(1)} collective-permute-done((bf16[384,768]{1,0:T(8,128)(2,1)S(1)}, bf16[384,768]{1,0:T(8,128)(2,1)S(1)}, u32[]{:S(2)}, u32[]{:S(2)}) %collective-permute-start.13) | collective-permute-done | bytes 589856 | tf_op jit(solution)/shard_map/ppermute | solution.py:29
  60.8 0.0 collective-permute-done.14.refs_7_
  60.8 3.8 %shard_map.100.a_ref = bf16[384,768]{1,0:T(8,128)(2,1)S(1)} custom-call(bf16[384,640]{1,0:T(8,128)(2,1)S(1)} %pad_maximum_fusion.q_ref, bf16[384,640]{1,0:T(8,128)(2,1)S(1)} %get-tuple-element.28.refs_0_.same, bf16[384,640]{1,0:T(8,128)(2,1)S(1)} %slice.47.refs_1_.other, bf16[384,640]{1,0:T(8,128)(2,1)S(1)} %collective-permute-done.6.refs_2_.refs_0_, ...), custom_call_target="tpu_custom_call" | custom-call | flops 1509949440 | bytes 4194304 | tf_op jit(solution)/shard_map/pallas_call | solution.py:236
  64.6 0.0 copy-start.5
  64.6 2.0 %collective-permute-done.15.c_ref = bf16[384,768]{1,0:T(8,128)(2,1)S(1)} collective-permute-done((bf16[384,768]{1,0:T(8,128)(2,1)S(1)}, bf16[384,768]{1,0:T(8,128)(2,1)S(1)}, u32[]{:S(2)}, u32[]{:S(2)}) %collective-permute-start.15) | collective-permute-done | bytes 589856 | tf_op jit(solution)/shard_map/ppermute | solution.py:29
  66.6 0.8 shard_map.102
  67.4 0.2 collective-permute-start.16
  67.6 0.8 shard_map.101.a_ref
  68.5 0.6 collective-permute-done.16.b_ref
  69.1 1.7 %shard_map.103 = (bf16[96,1536]{1,0:T(8,128)(2,1)S(1)}, bf16[96,1536]{1,0:T(8,128)(2,1)S(1)}) custom-call(s32[1]{0:T(128)} %bitcast.1.core_ref, bf16[192,640]{1,0:T(8,128)(2,1)S(1)} %shard_map.101.a_ref, bf16[192,640]{1,0:T(8,128)(2,1)S(1)} %collective-permute-done.16.b_ref, bf16[1280,5120]{1,0:T(8,128)(2,1)S(1)} %bitcast.11, f32[1,5120]{1,0:T(1,128)S(1)} %copy-done.5), custom_call_target="tpu_custom_call" | custom-call | flops 754974720 | bytes 3932160 | tf_op jit(solution)/shard_map/pallas_call | solution.py:296
  70.8 1.2 %collective-permute-start.17 = (bf16[96,1536]{1,0:T(8,128)(2,1)S(1)}, bf16[96,1536]{1,0:T(8,128)(2,1)S(1)}, u32[]{:S(2)}, u32[]{:S(2)}) collective-permute-start(bf16[96,1536]{1,0:T(8,128)(2,1)S(1)} %get-tuple-element.39), channel_id=1, source_target_pairs={{0,64},{1,65},{64,0},{65,1},{2,66},{3,67},{66,2},{67,3},{4,68},{5,... | collective-permute-start | bytes 884744 | tf_op jit(solution)/shard_map/ppermute | solution.py:53
  71.9 2.1 %collective-permute-start.18 = (bf16[96,1536]{1,0:T(8,128)(2,1)S(1)}, bf16[96,1536]{1,0:T(8,128)(2,1)S(1)}, u32[]{:S(2)}, u32[]{:S(2)}) collective-permute-start(bf16[96,1536]{1,0:T(8,128)(2,1)S(1)} %get-tuple-element.40), channel_id=1, source_target_pairs={{0,65},{1,64},{64,1},{65,0},{2,67},{3,66},{66,3},{67,2},{4,69},{5,... | collective-permute-start | bytes 884744 | tf_op jit(solution)/shard_map/ppermute | solution.py:53
  74.0 3.8 %shard_map.104 = (bf16[96,3584]{1,0:T(8,128)(2,1)S(1)}, bf16[96,3584]{1,0:T(8,128)(2,1)S(1)}) custom-call(s32[1]{0:T(128)} %bitcast.1.core_ref, bf16[192,640]{1,0:T(8,128)(2,1)S(1)} %shard_map.101.a_ref, bf16[192,640]{1,0:T(8,128)(2,1)S(1)} %collective-permute-done.16.b_ref, bf16[1280,5120]{1,0:T(8,128)(2,1)S(1)} %bitcast.12, f32[1,5120]{1,0:T(1,128)S(1)} %copy-done.5), custom_call_target="tpu_custom_call" | custom-call | flops 1761607680 | bytes 9175040 | tf_op jit(solution)/shard_map/pallas_call | solution.py:296
  77.9 0.7 collective-permute-start.19
  78.5 0.9 collective-permute-start.20
  79.4 0.5 collective-permute-done.17
  79.9 2.2 %collective-permute-done.18 = bf16[96,1536]{1,0:T(8,128)(2,1)S(1)} collective-permute-done((bf16[96,1536]{1,0:T(8,128)(2,1)S(1)}, bf16[96,1536]{1,0:T(8,128)(2,1)S(1)}, u32[]{:S(2)}, u32[]{:S(2)}) %collective-permute-start.18) | collective-permute-done | bytes 294944 | tf_op jit(solution)/shard_map/ppermute | solution.py:53
  82.1 0.1 add_convert_fusion.1
  82.2 12.7 %collective-permute-done.19 = bf16[96,3584]{1,0:T(8,128)(2,1)S(1)} collective-permute-done((bf16[96,3584]{1,0:T(8,128)(2,1)S(1)}, bf16[96,3584]{1,0:T(8,128)(2,1)S(1)}, u32[]{:S(2)}, u32[]{:S(2)}) %collective-permute-start.19) | collective-permute-done | bytes 688160 | tf_op jit(solution)/shard_map/ppermute | solution.py:53
  94.9 1.8 %collective-permute-done.20 = bf16[96,3584]{1,0:T(8,128)(2,1)S(1)} collective-permute-done((bf16[96,3584]{1,0:T(8,128)(2,1)S(1)}, bf16[96,3584]{1,0:T(8,128)(2,1)S(1)}, u32[]{:S(2)}, u32[]{:S(2)}) %collective-permute-start.20) | collective-permute-done | bytes 688160 | tf_op jit(solution)/shard_map/ppermute | solution.py:53
  96.6 0.2 add_convert_fusion
  96.8 1.0 %maximum_bitcast_fusion = bf16[1,96,5120]{2,1,0:T(8,128)(2,1)} fusion(bf16[96,3584]{1,0:T(8,128)(2,1)S(1)} %add_convert_fusion, bf16[96,1536]{1,0:T(8,128)(2,1)S(1)} %add_convert_fusion.1), kind=kLoop, calls=%fused_computation.1 | loop fusion | flops 1966080 | bytes 1966080 | tf_op jit(solution)/shard_map/broadcast_in_dim | solution.py:365
  (26 shorter events, 0.4 us)
Async XLA Ops:
  0.7 1.0 %copy-start.2 = (bf16[1,192,1280]{2,1,0:T(8,128)(2,1)S(1)}, bf16[1,192,1280]{2,1,0:T(8,128)(2,1)}, u32[]{:S(2)}) copy-start(bf16[1,192,1280]{2,1,0:T(8,128)(2,1)} %k_ref.1) | copy-start | bytes 1474564
  1.7 1.0 %copy-start.3 = (bf16[1,192,1280]{2,1,0:T(8,128)(2,1)S(1)}, bf16[1,192,1280]{2,1,0:T(8,128)(2,1)}, u32[]{:S(2)}) copy-start(bf16[1,192,1280]{2,1,0:T(8,128)(2,1)} %v_ref.1) | copy-start | bytes 1474564
  2.8 1.0 %copy-start.4 = (bf16[1,96,2560]{2,1,0:T(8,128)(2,1)S(1)}, bf16[1,96,2560]{2,1,0:T(8,128)(2,1)}, u32[]{:S(2)}) copy-start(bf16[1,96,2560]{2,1,0:T(8,128)(2,1)} %q_ref.1) | copy-start | bytes 1474564
  4.6 3.4 %collective-permute-start = (bf16[576,640]{1,0:T(8,128)(2,1)S(1)}, bf16[576,640]{1,0:T(8,128)(2,1)S(1)}, u32[]{:S(2)}, u32[]{:S(2)}) collective-permute-start(bf16[576,640]{1,0:T(8,128)(2,1)S(1)} %get-tuple-element.23), channel_id=1, source_target_pairs={{0,2},{2,0},{4,6},{6,4},{8,10},{10,8},{12,14},{14,12},{16,18},{18,... | collective-permute-start | bytes 2211848 | tf_op jit(solution)/shard_map/ppermute | solution.py:41
  4.7 10.1 %collective-permute-start.7 = (bf16[384,640]{1,0:T(8,128)(2,1)S(1)}, bf16[384,640]{1,0:T(8,128)(2,1)S(1)}, u32[]{:S(2)}, u32[]{:S(2)}) collective-permute-start(bf16[384,640]{1,0:T(8,128)(2,1)S(1)} %get-tuple-element.28.refs_0_.same), channel_id=1, source_target_pairs={{0,4},{2,18},{4,8},{6,22},{8,12},{10,26},{12,0},{14,30},{16,20},{1... | collective-permute-start | bytes 1474568 | tf_op jit(solution)/shard_map/ppermute | solution.py:29
  6.4 8.8 %collective-permute-start.6 = (bf16[384,640]{1,0:T(8,128)(2,1)S(1)}, bf16[384,640]{1,0:T(8,128)(2,1)S(1)}, u32[]{:S(2)}, u32[]{:S(2)}) collective-permute-start(bf16[384,640]{1,0:T(8,128)(2,1)S(1)} %get-tuple-element.28.refs_0_.same), channel_id=1, source_target_pairs={{0,12},{2,50},{4,0},{6,54},{8,4},{10,58},{12,8},{14,62},{16,28},{1... | collective-permute-start | bytes 1474568 | tf_op jit(solution)/shard_map/ppermute | solution.py:29
  8.1 10.3 %collective-permute-start.3 = (bf16[192,640]{1,0:T(8,128)(2,1)S(1)}, bf16[192,640]{1,0:T(8,128)(2,1)S(1)}, u32[]{:S(2)}, u32[]{:S(2)}) collective-permute-start(bf16[192,640]{1,0:T(8,128)(2,1)S(1)} %pad_maximum_fusion.3), channel_id=1, source_target_pairs={{0,1},{1,0},{2,3},{3,2},{4,5},{5,4},{6,7},{7,6},{8,9},{9,8},{10,11... | collective-permute-start | bytes 737288 | tf_op jit(solution)/shard_map/ppermute | solution.py:48
  11.3 10.1 %collective-permute-start.2 = (bf16[384,640]{1,0:T(8,128)(2,1)S(1)}, bf16[384,640]{1,0:T(8,128)(2,1)S(1)}, u32[]{:S(2)}, u32[]{:S(2)}) collective-permute-start(bf16[384,640]{1,0:T(8,128)(2,1)S(1)} %slice.47.refs_1_.other), channel_id=1, source_target_pairs={{0,4},{2,18},{4,8},{6,22},{8,12},{10,26},{12,0},{14,30},{16,20},{1... | collective-permute-start | bytes 1474568 | tf_op jit(solution)/shard_map/ppermute | solution.py:29
  11.8 10.6 %collective-permute-start.1 = (bf16[384,640]{1,0:T(8,128)(2,1)S(1)}, bf16[384,640]{1,0:T(8,128)(2,1)S(1)}, u32[]{:S(2)}, u32[]{:S(2)}) collective-permute-start(bf16[384,640]{1,0:T(8,128)(2,1)S(1)} %slice.47.refs_1_.other), channel_id=1, source_target_pairs={{0,12},{2,50},{4,0},{6,54},{8,4},{10,58},{12,8},{14,62},{16,28},{1... | collective-permute-start | bytes 1474568 | tf_op jit(solution)/shard_map/ppermute | solution.py:29
  18.5 16.8 %copy-start = (bf16[1,96,2560]{2,1,0:T(8,128)(2,1)S(1)}, bf16[1,96,2560]{2,1,0:T(8,128)(2,1)}, u32[]{:S(2)}) copy-start(bf16[1,96,2560]{2,1,0:T(8,128)(2,1)} %param.8) | copy-start | bytes 1474564
  18.5 16.8 %copy-start.1 = (bf16[1,96,2560]{2,1,0:T(8,128)(2,1)S(1)}, bf16[1,96,2560]{2,1,0:T(8,128)(2,1)}, u32[]{:S(2)}) copy-start(bf16[1,96,2560]{2,1,0:T(8,128)(2,1)} %param.9) | copy-start | bytes 1474564
  18.6 16.8 %collective-permute-start.4 = (bf16[384,640]{1,0:T(8,128)(2,1)S(1)}, bf16[384,640]{1,0:T(8,128)(2,1)S(1)}, u32[]{:S(2)}, u32[]{:S(2)}) collective-permute-start(bf16[384,640]{1,0:T(8,128)(2,1)S(1)} %pad_maximum_fusion.q_ref), channel_id=1, source_target_pairs={{0,32},{2,10},{4,36},{6,14},{8,40},{10,2},{12,44},{14,6},{16,48},{... | collective-permute-start | bytes 1474568 | tf_op jit(solution)/shard_map/ppermute | solution.py:29
  21.5 16.5 %collective-permute-start.9 = (bf16[384,640]{1,0:T(8,128)(2,1)S(1)}, bf16[384,640]{1,0:T(8,128)(2,1)S(1)}, u32[]{:S(2)}, u32[]{:S(2)}) collective-permute-start(bf16[384,640]{1,0:T(8,128)(2,1)S(1)} %pad_maximum_fusion.2), channel_id=1, source_target_pairs={{0,4},{2,18},{4,8},{6,22},{8,12},{10,26},{12,0},{14,30},{16,20},{1... | collective-permute-start | bytes 1474568 | tf_op jit(solution)/shard_map/ppermute | solution.py:29
  22.5 15.5 %collective-permute-start.8 = (bf16[384,640]{1,0:T(8,128)(2,1)S(1)}, bf16[384,640]{1,0:T(8,128)(2,1)S(1)}, u32[]{:S(2)}, u32[]{:S(2)}) collective-permute-start(bf16[384,640]{1,0:T(8,128)(2,1)S(1)} %pad_maximum_fusion.1), channel_id=1, source_target_pairs={{0,12},{2,50},{4,0},{6,54},{8,4},{10,58},{12,8},{14,62},{16,28},{1... | collective-permute-start | bytes 1474568 | tf_op jit(solution)/shard_map/ppermute | solution.py:29
  29.1 16.5 %collective-permute-start.11 = (bf16[384,640]{1,0:T(8,128)(2,1)S(1)}, bf16[384,640]{1,0:T(8,128)(2,1)S(1)}, u32[]{:S(2)}, u32[]{:S(2)}) collective-permute-start(bf16[384,640]{1,0:T(8,128)(2,1)S(1)} %pad_maximum_fusion.q_ref), channel_id=1, source_target_pairs={{0,16},{2,6},{4,20},{6,10},{8,24},{10,14},{12,28},{14,2},{16,32},{... | collective-permute-start | bytes 1474568 | tf_op jit(solution)/shard_map/ppermute | solution.py:29
  33.2 17.0 %collective-permute-start.10 = (bf16[384,640]{1,0:T(8,128)(2,1)S(1)}, bf16[384,640]{1,0:T(8,128)(2,1)S(1)}, u32[]{:S(2)}, u32[]{:S(2)}) collective-permute-start(bf16[384,640]{1,0:T(8,128)(2,1)S(1)} %pad_maximum_fusion.q_ref), channel_id=1, source_target_pairs={{0,48},{2,14},{4,52},{6,2},{8,56},{10,6},{12,60},{14,10},{16,0},{1... | collective-permute-start | bytes 1474568 | tf_op jit(solution)/shard_map/ppermute | solution.py:29
  35.4 18.5 %collective-permute-start.5 = (bf16[192,1280]{1,0:T(8,128)(2,1)S(1)}, bf16[192,1280]{1,0:T(8,128)(2,1)S(1)}, u32[]{:S(2)}, u32[]{:S(2)}) collective-permute-start(bf16[192,1280]{1,0:T(8,128)(2,1)S(1)} %shard_map.95), channel_id=1, source_target_pairs={{0,1},{1,0},{2,3},{3,2},{4,5},{5,4},{6,7},{7,6},{8,9},{9,8},{10,11... | collective-permute-start | bytes 1474568 | tf_op jit(solution)/shard_map/ppermute | solution.py:48
  38.0 31.0 %slice-start = ((s8[13107200]{0:T(1024)(128)(4,1)}), s8[4194304]{0:T(1024)(128)(4,1)S(1)}, s32[]{:S(2)}) async-start(s8[13107200]{0:T(1024)(128)(4,1)} %bitcast.9), calls=%async_computation | async-start | bytes 8388608
  41.8 27.2 %slice-start.1 = ((s8[13107200]{0:T(1024)(128)(4,1)}), s8[4194304]{0:T(1024)(128)(4,1)S(1)}, s32[]{:S(2)}) async-start(s8[13107200]{0:T(1024)(128)(4,1)} %bitcast.9), calls=%async_computation.1 | async-start | bytes 8388608
  41.8 15.0 %collective-permute-start.12 = (bf16[384,768]{1,0:T(8,128)(2,1)S(1)}, bf16[384,768]{1,0:T(8,128)(2,1)S(1)}, u32[]{:S(2)}, u32[]{:S(2)}) collective-permute-start(bf16[384,768]{1,0:T(8,128)(2,1)S(1)} %shard_map.96), channel_id=1, source_target_pairs={{0,32},{2,10},{4,36},{6,14},{8,40},{10,2},{12,44},{14,6},{16,48},{... | collective-permute-start | bytes 1769480 | tf_op jit(solution)/shard_map/ppermute | solution.py:29
  49.4 19.7 %slice-start.2 = ((s8[13107200]{0:T(1024)(128)(4,1)}), s8[4194304]{0:T(1024)(128)(4,1)S(1)}, s32[]{:S(2)}) async-start(s8[13107200]{0:T(1024)(128)(4,1)} %bitcast.9), calls=%async_computation.2 | async-start | bytes 8388608
  49.4 11.5 %collective-permute-start.13 = (bf16[384,768]{1,0:T(8,128)(2,1)S(1)}, bf16[384,768]{1,0:T(8,128)(2,1)S(1)}, u32[]{:S(2)}, u32[]{:S(2)}) collective-permute-start(bf16[384,768]{1,0:T(8,128)(2,1)S(1)} %shard_map.98), channel_id=1, source_target_pairs={{0,48},{2,14},{4,52},{6,2},{8,56},{10,6},{12,60},{14,10},{16,0},{1... | collective-permute-start | bytes 1769480 | tf_op jit(solution)/shard_map/ppermute | solution.py:29
  55.5 5.3 %collective-permute-start.14 = (bf16[384,640]{1,0:T(8,128)(2,1)S(1)}, bf16[384,640]{1,0:T(8,128)(2,1)S(1)}, u32[]{:S(2)}, u32[]{:S(2)}) collective-permute-start(bf16[384,640]{1,0:T(8,128)(2,1)S(1)} %get-tuple-element.36), channel_id=1, source_target_pairs={{0,2},{2,0},{4,6},{6,4},{8,10},{10,8},{12,14},{14,12},{16,18},{18,... | collective-permute-start | bytes 1474568 | tf_op jit(solution)/shard_map/ppermute | solution.py:41
  55.5 11.1 %collective-permute-start.15 = (bf16[384,768]{1,0:T(8,128)(2,1)S(1)}, bf16[384,768]{1,0:T(8,128)(2,1)S(1)}, u32[]{:S(2)}, u32[]{:S(2)}) collective-permute-start(bf16[384,768]{1,0:T(8,128)(2,1)S(1)} %shard_map.97), channel_id=1, source_target_pairs={{0,16},{2,6},{4,20},{6,10},{8,24},{10,14},{12,28},{14,2},{16,32},{... | collective-permute-start | bytes 1769480 | tf_op jit(solution)/shard_map/ppermute | solution.py:29
  60.8 8.2 %slice-start.3 = ((s8[13107200]{0:T(1024)(128)(4,1)}), s8[524288]{0:T(1024)(128)(4,1)S(1)}, s32[]{:S(2)}) async-start(s8[13107200]{0:T(1024)(128)(4,1)} %bitcast.9), calls=%async_computation.3 | async-start | bytes 1048576
  64.6 4.4 %copy-start.5 = (f32[1,5120]{1,0:T(1,128)S(1)}, f32[1,5120]{1,0:T(1,128)}, u32[]{:S(2)}) copy-start(f32[1,5120]{1,0:T(1,128)} %g_ref.3) | copy-start | bytes 61444
  67.4 1.6 %collective-permute-start.16 = (bf16[192,640]{1,0:T(8,128)(2,1)S(1)}, bf16[192,640]{1,0:T(8,128)(2,1)S(1)}, u32[]{:S(2)}, u32[]{:S(2)}) collective-permute-start(bf16[192,640]{1,0:T(8,128)(2,1)S(1)} %shard_map.102), channel_id=1, source_target_pairs={{0,2},{2,0},{4,6},{6,4},{8,10},{10,8},{12,14},{14,12},{16,18},{18,... | collective-permute-start | bytes 737288 | tf_op jit(solution)/shard_map/ppermute | solution.py:41
  70.8 9.1 %collective-permute-start.17 = (bf16[96,1536]{1,0:T(8,128)(2,1)S(1)}, bf16[96,1536]{1,0:T(8,128)(2,1)S(1)}, u32[]{:S(2)}, u32[]{:S(2)}) collective-permute-start(bf16[96,1536]{1,0:T(8,128)(2,1)S(1)} %get-tuple-element.39), channel_id=1, source_target_pairs={{0,64},{1,65},{64,0},{65,1},{2,66},{3,67},{66,2},{67,3},{4,68},{5,... | collective-permute-start | bytes 884744 | tf_op jit(solution)/shard_map/ppermute | solution.py:53
  71.9 10.2 %collective-permute-start.18 = (bf16[96,1536]{1,0:T(8,128)(2,1)S(1)}, bf16[96,1536]{1,0:T(8,128)(2,1)S(1)}, u32[]{:S(2)}, u32[]{:S(2)}) collective-permute-start(bf16[96,1536]{1,0:T(8,128)(2,1)S(1)} %get-tuple-element.40), channel_id=1, source_target_pairs={{0,65},{1,64},{64,1},{65,0},{2,67},{3,66},{66,3},{67,2},{4,69},{5,... | collective-permute-start | bytes 884744 | tf_op jit(solution)/shard_map/ppermute | solution.py:53
  77.9 17.0 %collective-permute-start.19 = (bf16[96,3584]{1,0:T(8,128)(2,1)S(1)}, bf16[96,3584]{1,0:T(8,128)(2,1)S(1)}, u32[]{:S(2)}, u32[]{:S(2)}) collective-permute-start(bf16[96,3584]{1,0:T(8,128)(2,1)S(1)} %get-tuple-element.41), channel_id=1, source_target_pairs={{0,64},{1,65},{64,0},{65,1},{2,66},{3,67},{66,2},{67,3},{4,68},{5,... | collective-permute-start | bytes 2064392 | tf_op jit(solution)/shard_map/ppermute | solution.py:53
  78.5 18.1 %collective-permute-start.20 = (bf16[96,3584]{1,0:T(8,128)(2,1)S(1)}, bf16[96,3584]{1,0:T(8,128)(2,1)S(1)}, u32[]{:S(2)}, u32[]{:S(2)}) collective-permute-start(bf16[96,3584]{1,0:T(8,128)(2,1)S(1)} %get-tuple-element.42), channel_id=1, source_target_pairs={{0,65},{1,64},{64,1},{65,0},{2,67},{3,66},{66,3},{67,2},{4,69},{5,... | collective-permute-start | bytes 2064392 | tf_op jit(solution)/shard_map/ppermute | solution.py:53

commit v4 on v3

--- a/solution.py
+++ b/solution.py
@@ -24,7 +24,7 @@
     for z in range(CHIPS):
         for y in range(CHIPS):
             for core in range(2):
-                to = place(z, y - steps, core) if core == core_on_y else place(z - steps, y, core)
+                to = place(z, y + steps, core) if core == core_on_y else place(z + steps, y, core)
                 pairs.append((place(z, y, core), to))
     return lax.ppermute(value, "patch", pairs)
 
@@ -124,18 +124,16 @@
     )(head, keys, values)
 
 
-def assemble_fresh(table, keys, values, got):
+def fresh_by_core(table, keys, values, got):
     rows, width = keys.shape[0], keys.shape[1] // 2
     narrow = width // 2
 
-    def body(table_ref, k_ref, v_ref, got_ref, nk_ref, nv_ref, same_ref, other_ref):
+    def body(table_ref, k_ref, v_ref, got_ref, same_ref, other_ref):
         head, core = table_ref[0], table_ref[1]
-        for mine, at, new in ((k_ref, 0, nk_ref), (v_ref, rows, nv_ref)):
+        for mine, at in ((k_ref, 0), (v_ref, rows)):
             theirs = got_ref[at : at + rows]
             low = jnp.where(head == 0, mine[...], theirs)
             high = jnp.where(head == 0, theirs, mine[...])
-            new[:rows] = low
-            new[rows:] = high
             for lo, x in ((2 * at, low), (2 * at + rows, high)):
                 left, right = x[:, :narrow], x[:, narrow:]
                 same_ref[lo : lo + rows] = jnp.where(core == 0, left, right)
@@ -149,10 +147,34 @@
             num_scalar_prefetch=1,
             grid=(1,),
             in_specs=[block, block, whole(2 * rows, width)],
-            out_specs=[whole(2 * rows, width)] * 2 + [whole(4 * rows, narrow)] * 2,
+            out_specs=[whole(4 * rows, narrow)] * 2,
         ),
-        out_shape=[jax.ShapeDtypeStruct((2 * rows, width), BF)] * 2
-        + [jax.ShapeDtypeStruct((4 * rows, narrow), BF)] * 2,
+        out_shape=[jax.ShapeDtypeStruct((4 * rows, narrow), BF)] * 2,
+        compiler_params=params(),
+    )(table, keys, values, got)
+
+
+def new_in_order(table, keys, values, got):
+    rows, width = keys.shape[0], keys.shape[1] // 2
+
+    def body(table_ref, k_ref, v_ref, got_ref, nk_ref, nv_ref):
+        head = table_ref[0]
+        for mine, at, new in ((k_ref, 0, nk_ref), (v_ref, rows, nv_ref)):
+            theirs = got_ref[at : at + rows]
+            new[:rows] = jnp.where(head == 0, mine[...], theirs)
+            new[rows:] = jnp.where(head == 0, theirs, mine[...])
+
+    block = pl.BlockSpec((rows, width), lambda g, t: (0, t[0]))
+    whole = lambda r, w: pl.BlockSpec((r, w), lambda g, t: (0, 0))
+    return pl.pallas_call(
+        body,
+        grid_spec=pltpu.PrefetchScalarGridSpec(
+            num_scalar_prefetch=1,
+            grid=(1,),
+            in_specs=[block, block, whole(2 * rows, width)],
+            out_specs=[whole(2 * rows, width)] * 2,
+        ),
+        out_shape=[jax.ShapeDtypeStruct((2 * rows, width), BF)] * 2,
         compiler_params=params(),
     )(table, keys, values, got)
 
@@ -346,9 +368,7 @@
     o_down = attention(remote_kernel, q_down, blocks)
     far, up, down = queries_along(o_far, 2), queries_along(o_up, -1), queries_along(o_down, 1)
     got, _, _, _ = lax.optimization_barrier((got, o_far, o_up, o_down))
-    new_keys, new_values, f_same, f_other = assemble_fresh(
-        table, fresh_keys[0], fresh_values[0], got
-    )
+    f_same, f_other = fresh_by_core(table, fresh_keys[0], fresh_values[0], got)
     f_other = other_core(f_other)
     q_own, far, down = lax.optimization_barrier((q_own, far, down))
     o_own = attention(own_kernel, q_own, blocks + [f_same, f_other])
@@ -362,6 +382,7 @@
     branch = jnp.concatenate(
         [(first.astype(F32) + second.astype(F32)).astype(BF) for first, second in pieces], axis=1
     )
+    new_keys, new_values = new_in_order(table, fresh_keys[0], fresh_values[0], got)
     return (new_keys[None], new_values[None], branch[None])
 
 

time: 98.1 us -> 97.4 us (level)
  waiting for transfers between devices: 30.1 us -> 27.1 us
  starting transfers between devices: 37.3 us -> 38.9 us
    ppermute x4, waiting for transfers between devices: 17.1 us -> 15.5 us  [onward_to(): return lax.ppermute(value, ('pipe', 'head'), pairs)]
    ppermute x2, starting transfers between devices: 3.86 us -> 5.2 us  [other_half(): return lax.ppermute(value, ('patch', 'head'), pairs)]
    ppermute x12, waiting for transfers between devices: 9.27 us -> 8.14 us  [along(): return lax.ppermute(value, 'patch', pairs)]
    pallas_call x1 -> x2, Pallas kernels: 1.61 us -> 2.26 us  [the longest x1 1.54 us: new_in_order(): pl.pallas_call(body, grid_spec=pltpu.PrefetchScalarGridSpec(num_scalar_pr...]
  transfers between devices with their start and end apart: 21 -> 21, of which waited for: 12 -> 11; matrix products, arithmetic and copies ran while one was open for 0% -> 0% of each run, Pallas kernels for 22% -> 23%
where the time goes in v4:
time: 97.4 us; the launch traced here: 97.1 us
  starting transfers between devices  38.9 us (40%)
  waiting for transfers between devices  27.1 us (28%)
  Pallas kernels  25.4 us (26%)
  local copies, waits for them, and re-layouts  3.33 us (3%)
  other arithmetic  1.49 us (2%)
    ppermute x12, starting transfers between devices, along(): return lax.ppermute(value, 'patch', pairs)  28 us
    ppermute x4, waiting for transfers between devices, onward_to(): return lax.ppermute(value, ('pipe', 'head'), pairs)  15.5 us
    pallas_call x4, Pallas kernels, attention(): pl.pallas_call(kernel, out_shape=jax.ShapeDtypeStruct((rows, width + HEAD...  15.1 us
    ppermute x12, waiting for transfers between devices, along(): return lax.ppermute(value, 'patch', pairs)  8.14 us
    pallas_call x2, Pallas kernels, project(): pl.pallas_call(project_kernel, grid_spec=pltpu.PrefetchScalarGridSpec(num...  5.54 us
    ppermute x2, starting transfers between devices, other_half(): return lax.ppermute(value, ('patch', 'head'), pairs)  5.2 us
    ppermute x4, starting transfers between devices, onward_to(): return lax.ppermute(value, ('pipe', 'head'), pairs)  4.82 us
    ppermute x2, waiting for transfers between devices, other_half(): return lax.ppermute(value, ('patch', 'head'), pairs)  3.17 us
  transfers between devices with their start and end apart: 21, of which 11 were waited for; matrix products, arithmetic and copies ran while one was open for 0% of the time, Pallas kernels for 23%

profile of v4, /device:TPU:0, one launch (start us, length us, event | category | flops | bytes accessed | tf_op | source)
XLA Modules:
  0.0 97.1 jit_solution(5992498080427821220)
XLA Ops:
  0.6 0.1 pad_add_fusion.table_ref
  0.7 1.0 %copy-done.2 = bf16[1,192,1280]{2,1,0:T(8,128)(2,1)S(1)} copy-done((bf16[1,192,1280]{2,1,0:T(8,128)(2,1)S(1)}, bf16[1,192,1280]{2,1,0:T(8,128)(2,1)}, u32[]{:S(2)}) %copy-start.2) | copy-done | bytes 491544
  1.8 1.0 %copy-done.3 = bf16[1,192,1280]{2,1,0:T(8,128)(2,1)S(1)} copy-done((bf16[1,192,1280]{2,1,0:T(8,128)(2,1)S(1)}, bf16[1,192,1280]{2,1,0:T(8,128)(2,1)}, u32[]{:S(2)}) %copy-start.3) | copy-done | bytes 491544
  2.8 1.0 %copy-done.4 = bf16[1,96,2560]{2,1,0:T(8,128)(2,1)S(1)} copy-done((bf16[1,96,2560]{2,1,0:T(8,128)(2,1)S(1)}, bf16[1,96,2560]{2,1,0:T(8,128)(2,1)}, u32[]{:S(2)}) %copy-start.4) | copy-done | bytes 491544
  3.8 0.8 shard_map.94
  4.6 0.1 collective-permute-start
  4.7 1.7 %collective-permute-start.6 = (bf16[384,640]{1,0:T(8,128)(2,1)S(1)}, bf16[384,640]{1,0:T(8,128)(2,1)S(1)}, u32[]{:S(2)}, u32[]{:S(2)}) collective-permute-start(bf16[384,640]{1,0:T(8,128)(2,1)S(1)} %get-tuple-element.28.refs_0_.same), channel_id=1, source_target_pairs={{0,4},{2,18},{4,8},{6,22},{8,12},{10,26},{12,0},{14,30},{16,20},{1... | collective-permute-start | bytes 1474568 | tf_op jit(solution)/shard_map/ppermute | solution.py:29
  6.4 1.6 %collective-permute-start.7 = (bf16[384,640]{1,0:T(8,128)(2,1)S(1)}, bf16[384,640]{1,0:T(8,128)(2,1)S(1)}, u32[]{:S(2)}, u32[]{:S(2)}) collective-permute-start(bf16[384,640]{1,0:T(8,128)(2,1)S(1)} %get-tuple-element.28.refs_0_.same), channel_id=1, source_target_pairs={{0,12},{2,50},{4,0},{6,54},{8,4},{10,58},{12,8},{14,62},{16,28},{1... | collective-permute-start | bytes 1474568 | tf_op jit(solution)/shard_map/ppermute | solution.py:29
  8.0 0.0 collective-permute-done
  8.1 3.2 %collective-permute-start.3 = (bf16[192,640]{1,0:T(8,128)(2,1)S(1)}, bf16[192,640]{1,0:T(8,128)(2,1)S(1)}, u32[]{:S(2)}, u32[]{:S(2)}) collective-permute-start(bf16[192,640]{1,0:T(8,128)(2,1)S(1)} %pad_maximum_fusion.3), channel_id=1, source_target_pairs={{0,1},{1,0},{2,3},{3,2},{4,5},{5,4},{6,7},{7,6},{8,9},{9,8},{10,11... | collective-permute-start | bytes 737288 | tf_op jit(solution)/shard_map/ppermute | solution.py:48
  11.3 0.5 collective-permute-start.1
  11.8 2.8 %collective-permute-start.2 = (bf16[384,640]{1,0:T(8,128)(2,1)S(1)}, bf16[384,640]{1,0:T(8,128)(2,1)S(1)}, u32[]{:S(2)}, u32[]{:S(2)}) collective-permute-start(bf16[384,640]{1,0:T(8,128)(2,1)S(1)} %slice.47.refs_1_.other), channel_id=1, source_target_pairs={{0,12},{2,50},{4,0},{6,54},{8,4},{10,58},{12,8},{14,62},{16,28},{1... | collective-permute-start | bytes 1474568 | tf_op jit(solution)/shard_map/ppermute | solution.py:29
  14.6 0.2 collective-permute-done.6.refs_2_.refs_0_
  14.8 0.4 collective-permute-done.7.refs_4_.refs_2_
  15.3 3.2 %collective-permute-done.3 = bf16[192,640]{1,0:T(8,128)(2,1)S(1)} collective-permute-done((bf16[192,640]{1,0:T(8,128)(2,1)S(1)}, bf16[192,640]{1,0:T(8,128)(2,1)S(1)}, u32[]{:S(2)}, u32[]{:S(2)}) %collective-permute-start.3) | collective-permute-done | bytes 245792 | tf_op jit(solution)/shard_map/ppermute | solution.py:48
  18.5 0.0 copy-start
  18.5 0.0 copy-start.1
  18.6 2.1 %collective-permute-start.4 = (bf16[384,640]{1,0:T(8,128)(2,1)S(1)}, bf16[384,640]{1,0:T(8,128)(2,1)S(1)}, u32[]{:S(2)}, u32[]{:S(2)}) collective-permute-start(bf16[384,640]{1,0:T(8,128)(2,1)S(1)} %pad_maximum_fusion.q_ref), channel_id=1, source_target_pairs={{0,32},{2,10},{4,36},{6,14},{8,40},{10,2},{12,44},{14,6},{16,48},{... | collective-permute-start | bytes 1474568 | tf_op jit(solution)/shard_map/ppermute | solution.py:29
  20.7 0.7 collective-permute-start.11
  21.4 0.1 collective-permute-done.1.refs_3_.refs_1_
  21.5 1.6 %collective-permute-start.8 = (bf16[384,640]{1,0:T(8,128)(2,1)S(1)}, bf16[384,640]{1,0:T(8,128)(2,1)S(1)}, u32[]{:S(2)}, u32[]{:S(2)}) collective-permute-start(bf16[384,640]{1,0:T(8,128)(2,1)S(1)} %pad_maximum_fusion.1), channel_id=1, source_target_pairs={{0,4},{2,18},{4,8},{6,22},{8,12},{10,26},{12,0},{14,30},{16,20},{1... | collective-permute-start | bytes 1474568 | tf_op jit(solution)/shard_map/ppermute | solution.py:29
  23.1 0.0 collective-permute-done.2.refs_5_.refs_3_
  23.2 6.6 %collective-permute-start.9 = (bf16[384,640]{1,0:T(8,128)(2,1)S(1)}, bf16[384,640]{1,0:T(8,128)(2,1)S(1)}, u32[]{:S(2)}, u32[]{:S(2)}) collective-permute-start(bf16[384,640]{1,0:T(8,128)(2,1)S(1)} %pad_maximum_fusion.2), channel_id=1, source_target_pairs={{0,12},{2,50},{4,0},{6,54},{8,4},{10,58},{12,8},{14,62},{16,28},{1... | collective-permute-start | bytes 1474568 | tf_op jit(solution)/shard_map/ppermute | solution.py:29
  29.8 3.3 %collective-permute-start.10 = (bf16[384,640]{1,0:T(8,128)(2,1)S(1)}, bf16[384,640]{1,0:T(8,128)(2,1)S(1)}, u32[]{:S(2)}, u32[]{:S(2)}) collective-permute-start(bf16[384,640]{1,0:T(8,128)(2,1)S(1)} %pad_maximum_fusion.q_ref), channel_id=1, source_target_pairs={{0,16},{2,6},{4,20},{6,10},{8,24},{10,14},{12,28},{14,2},{16,32},{... | collective-permute-start | bytes 1474568 | tf_op jit(solution)/shard_map/ppermute | solution.py:29
  33.2 0.0 collective-permute-done.4.q_ref
  33.2 2.0 %collective-permute-start.5 = (bf16[192,1280]{1,0:T(8,128)(2,1)S(1)}, bf16[192,1280]{1,0:T(8,128)(2,1)S(1)}, u32[]{:S(2)}, u32[]{:S(2)}) collective-permute-start(bf16[192,1280]{1,0:T(8,128)(2,1)S(1)} %shard_map.95), channel_id=1, source_target_pairs={{0,1},{1,0},{2,3},{3,2},{4,5},{5,4},{6,7},{7,6},{8,9},{9,8},{10,11... | collective-permute-start | bytes 1474568 | tf_op jit(solution)/shard_map/ppermute | solution.py:48
  35.3 3.8 %collective-permute-done.11.q_ref = bf16[384,640]{1,0:T(8,128)(2,1)S(1)} collective-permute-done((bf16[384,640]{1,0:T(8,128)(2,1)S(1)}, bf16[384,640]{1,0:T(8,128)(2,1)S(1)}, u32[]{:S(2)}, u32[]{:S(2)}) %collective-permute-start.11) | collective-permute-done | bytes 491552 | tf_op jit(solution)/shard_map/ppermute | solution.py:29
  39.0 0.0 collective-permute-done.8.refs_6_.refs_4_
  39.0 0.0 collective-permute-done.9.refs_7_.refs_5_
  39.0 3.8 %shard_map.98 = bf16[384,768]{1,0:T(8,128)(2,1)S(1)} custom-call(bf16[384,640]{1,0:T(8,128)(2,1)S(1)} %collective-permute-done.11.q_ref, bf16[384,640]{1,0:T(8,128)(2,1)S(1)} %get-tuple-element.28.refs_0_.same, bf16[384,640]{1,0:T(8,128)(2,1)S(1)} %slice.47.refs_1_.other, bf16[384,640]{1,0:T(8,128)(2,1)S(1)} %collective-permute-done.6.refs_2_.refs_0_, ...), custom_call_target="tpu_custom_call" | custom-call | flops 1509949440 | bytes 4194304 | tf_op jit(solution)/shard_map/pallas_call | solution.py:258
  42.8 0.0 slice-start.1
  42.8 0.7 collective-permute-start.13
  43.6 3.8 %shard_map.96 = bf16[384,768]{1,0:T(8,128)(2,1)S(1)} custom-call(bf16[384,640]{1,0:T(8,128)(2,1)S(1)} %collective-permute-done.4.q_ref, bf16[384,640]{1,0:T(8,128)(2,1)S(1)} %get-tuple-element.28.refs_0_.same, bf16[384,640]{1,0:T(8,128)(2,1)S(1)} %slice.47.refs_1_.other, bf16[384,640]{1,0:T(8,128)(2,1)S(1)} %collective-permute-done.6.refs_2_.refs_0_, ...), custom_call_target="tpu_custom_call" | custom-call | flops 1509949440 | bytes 4194304 | tf_op jit(solution)/shard_map/pallas_call | solution.py:258
  47.3 0.0 slice-start.2
  47.3 3.7 %collective-permute-start.12 = (bf16[384,768]{1,0:T(8,128)(2,1)S(1)}, bf16[384,768]{1,0:T(8,128)(2,1)S(1)}, u32[]{:S(2)}, u32[]{:S(2)}) collective-permute-start(bf16[384,768]{1,0:T(8,128)(2,1)S(1)} %shard_map.96), channel_id=1, source_target_pairs={{0,32},{2,10},{4,36},{6,14},{8,40},{10,2},{12,44},{14,6},{16,48},{... | collective-permute-start | bytes 1769480 | tf_op jit(solution)/shard_map/ppermute | solution.py:29
  51.0 0.0 collective-permute-done.10.q_ref
  51.0 3.8 %shard_map.97 = bf16[384,768]{1,0:T(8,128)(2,1)S(1)} custom-call(bf16[384,640]{1,0:T(8,128)(2,1)S(1)} %collective-permute-done.10.q_ref, bf16[384,640]{1,0:T(8,128)(2,1)S(1)} %get-tuple-element.28.refs_0_.same, bf16[384,640]{1,0:T(8,128)(2,1)S(1)} %slice.47.refs_1_.other, bf16[384,640]{1,0:T(8,128)(2,1)S(1)} %collective-permute-done.6.refs_2_.refs_0_, ...), custom_call_target="tpu_custom_call" | custom-call | flops 1509949440 | bytes 4194304 | tf_op jit(solution)/shard_map/pallas_call | solution.py:258
  54.8 0.0 collective-permute-done.5.got_ref
  54.8 0.7 shard_map.100
  55.5 0.1 collective-permute-start.14
  55.6 2.6 %collective-permute-start.15 = (bf16[384,768]{1,0:T(8,128)(2,1)S(1)}, bf16[384,768]{1,0:T(8,128)(2,1)S(1)}, u32[]{:S(2)}, u32[]{:S(2)}) collective-permute-start(bf16[384,768]{1,0:T(8,128)(2,1)S(1)} %shard_map.97), channel_id=1, source_target_pairs={{0,48},{2,14},{4,52},{6,2},{8,56},{10,6},{12,60},{14,10},{16,0},{1... | collective-permute-start | bytes 1769480 | tf_op jit(solution)/shard_map/ppermute | solution.py:29
  58.2 3.1 %collective-permute-done.12.b_ref = bf16[384,768]{1,0:T(8,128)(2,1)S(1)} collective-permute-done((bf16[384,768]{1,0:T(8,128)(2,1)S(1)}, bf16[384,768]{1,0:T(8,128)(2,1)S(1)}, u32[]{:S(2)}, u32[]{:S(2)}) %collective-permute-start.12) | collective-permute-done | bytes 589856 | tf_op jit(solution)/shard_map/ppermute | solution.py:29
  61.3 0.0 collective-permute-done.14.refs_7_
  61.3 3.8 %shard_map.101.a_ref = bf16[384,768]{1,0:T(8,128)(2,1)S(1)} custom-call(bf16[384,640]{1,0:T(8,128)(2,1)S(1)} %pad_maximum_fusion.q_ref, bf16[384,640]{1,0:T(8,128)(2,1)S(1)} %get-tuple-element.28.refs_0_.same, bf16[384,640]{1,0:T(8,128)(2,1)S(1)} %slice.47.refs_1_.other, bf16[384,640]{1,0:T(8,128)(2,1)S(1)} %collective-permute-done.6.refs_2_.refs_0_, ...), custom_call_target="tpu_custom_call" | custom-call | flops 1509949440 | bytes 4194304 | tf_op jit(solution)/shard_map/pallas_call | solution.py:258
  65.2 0.0 copy-start.5
  65.2 0.6 collective-permute-done.15.c_ref
  65.8 0.8 shard_map.103
  66.6 0.6 collective-permute-start.16
  67.3 0.8 shard_map.102.a_ref
  68.1 0.3 collective-permute-done.16.b_ref
  68.4 1.7 %shard_map.104 = (bf16[96,1536]{1,0:T(8,128)(2,1)S(1)}, bf16[96,1536]{1,0:T(8,128)(2,1)S(1)}) custom-call(s32[1]{0:T(128)} %bitcast.1.core_ref, bf16[192,640]{1,0:T(8,128)(2,1)S(1)} %shard_map.102.a_ref, bf16[192,640]{1,0:T(8,128)(2,1)S(1)} %collective-permute-done.16.b_ref, bf16[1280,5120]{1,0:T(8,128)(2,1)S(1)} %bitcast.11, f32[1,5120]{1,0:T(1,128)S(1)} %copy-done.5), custom_call_target="tpu_custom_call" | custom-call | flops 754974720 | bytes 3932160 | tf_op jit(solution)/shard_map/pallas_call | solution.py:318
  70.2 1.1 %collective-permute-start.17 = (bf16[96,1536]{1,0:T(8,128)(2,1)S(1)}, bf16[96,1536]{1,0:T(8,128)(2,1)S(1)}, u32[]{:S(2)}, u32[]{:S(2)}) collective-permute-start(bf16[96,1536]{1,0:T(8,128)(2,1)S(1)} %get-tuple-element.39), channel_id=1, source_target_pairs={{0,64},{1,65},{64,0},{65,1},{2,66},{3,67},{66,2},{67,3},{4,68},{5,... | collective-permute-start | bytes 884744 | tf_op jit(solution)/shard_map/ppermute | solution.py:53
  71.2 2.1 %collective-permute-start.18 = (bf16[96,1536]{1,0:T(8,128)(2,1)S(1)}, bf16[96,1536]{1,0:T(8,128)(2,1)S(1)}, u32[]{:S(2)}, u32[]{:S(2)}) collective-permute-start(bf16[96,1536]{1,0:T(8,128)(2,1)S(1)} %get-tuple-element.40), channel_id=1, source_target_pairs={{0,65},{1,64},{64,1},{65,0},{2,67},{3,66},{66,3},{67,2},{4,69},{5,... | collective-permute-start | bytes 884744 | tf_op jit(solution)/shard_map/ppermute | solution.py:53
  73.4 3.8 %shard_map.105 = (bf16[96,3584]{1,0:T(8,128)(2,1)S(1)}, bf16[96,3584]{1,0:T(8,128)(2,1)S(1)}) custom-call(s32[1]{0:T(128)} %bitcast.1.core_ref, bf16[192,640]{1,0:T(8,128)(2,1)S(1)} %shard_map.102.a_ref, bf16[192,640]{1,0:T(8,128)(2,1)S(1)} %collective-permute-done.16.b_ref, bf16[1280,5120]{1,0:T(8,128)(2,1)S(1)} %bitcast.12, f32[1,5120]{1,0:T(1,128)S(1)} %copy-done.5), custom_call_target="tpu_custom_call" | custom-call | flops 1761607680 | bytes 9175040 | tf_op jit(solution)/shard_map/pallas_call | solution.py:318
  77.2 0.8 collective-permute-start.19
  78.0 0.8 collective-permute-start.20
  78.8 1.5 %shard_map.99 = (bf16[192,1280]{1,0:T(8,128)(2,1)}, bf16[192,1280]{1,0:T(8,128)(2,1)}) custom-call(s32[2]{0:T(128)S(1)} %pad_add_fusion.table_ref, bf16[96,2560]{1,0:T(8,128)(2,1)S(1)} %bitcast.15, bf16[96,2560]{1,0:T(8,128)(2,1)S(1)} %bitcast.18, bf16[192,1280]{1,0:T(8,128)(2,1)S(1)} %collective-permute-done.5.got_ref), custom_call_target="tpu_custom_call" | custom-call | tf_op jit(solution)/shard_map/pallas_call | solution.py:169
  80.4 0.0 collective-permute-done.17
  80.4 0.8 collective-permute-done.18
  81.2 0.1 add_convert_fusion.1
  81.3 13.0 %collective-permute-done.19 = bf16[96,3584]{1,0:T(8,128)(2,1)S(1)} collective-permute-done((bf16[96,3584]{1,0:T(8,128)(2,1)S(1)}, bf16[96,3584]{1,0:T(8,128)(2,1)S(1)}, u32[]{:S(2)}, u32[]{:S(2)}) %collective-permute-start.19) | collective-permute-done | bytes 688160 | tf_op jit(solution)/shard_map/ppermute | solution.py:53
  94.3 1.7 %collective-permute-done.20 = bf16[96,3584]{1,0:T(8,128)(2,1)S(1)} collective-permute-done((bf16[96,3584]{1,0:T(8,128)(2,1)S(1)}, bf16[96,3584]{1,0:T(8,128)(2,1)S(1)}, u32[]{:S(2)}, u32[]{:S(2)}) %collective-permute-start.20) | collective-permute-done | bytes 688160 | tf_op jit(solution)/shard_map/ppermute | solution.py:53
  95.9 0.2 add_convert_fusion
  96.1 1.0 %maximum_bitcast_fusion = bf16[1,96,5120]{2,1,0:T(8,128)(2,1)} fusion(bf16[96,3584]{1,0:T(8,128)(2,1)S(1)} %add_convert_fusion, bf16[96,1536]{1,0:T(8,128)(2,1)S(1)} %add_convert_fusion.1), kind=kLoop, calls=%fused_computation.1 | loop fusion | flops 1966080 | bytes 1966080 | tf_op jit(solution)/shard_map/broadcast_in_dim | solution.py:386
  (27 shorter events, 0.4 us)
Async XLA Ops:
  0.7 1.0 %copy-start.2 = (bf16[1,192,1280]{2,1,0:T(8,128)(2,1)S(1)}, bf16[1,192,1280]{2,1,0:T(8,128)(2,1)}, u32[]{:S(2)}) copy-start(bf16[1,192,1280]{2,1,0:T(8,128)(2,1)} %k_ref.1) | copy-start | bytes 1474564
  1.7 1.0 %copy-start.3 = (bf16[1,192,1280]{2,1,0:T(8,128)(2,1)S(1)}, bf16[1,192,1280]{2,1,0:T(8,128)(2,1)}, u32[]{:S(2)}) copy-start(bf16[1,192,1280]{2,1,0:T(8,128)(2,1)} %v_ref.1) | copy-start | bytes 1474564
  2.8 1.0 %copy-start.4 = (bf16[1,96,2560]{2,1,0:T(8,128)(2,1)S(1)}, bf16[1,96,2560]{2,1,0:T(8,128)(2,1)}, u32[]{:S(2)}) copy-start(bf16[1,96,2560]{2,1,0:T(8,128)(2,1)} %q_ref.1) | copy-start | bytes 1474564
  4.6 3.4 %collective-permute-start = (bf16[576,640]{1,0:T(8,128)(2,1)S(1)}, bf16[576,640]{1,0:T(8,128)(2,1)S(1)}, u32[]{:S(2)}, u32[]{:S(2)}) collective-permute-start(bf16[576,640]{1,0:T(8,128)(2,1)S(1)} %get-tuple-element.23), channel_id=1, source_target_pairs={{0,2},{2,0},{4,6},{6,4},{8,10},{10,8},{12,14},{14,12},{16,18},{18,... | collective-permute-start | bytes 2211848 | tf_op jit(solution)/shard_map/ppermute | solution.py:41
  4.7 10.1 %collective-permute-start.6 = (bf16[384,640]{1,0:T(8,128)(2,1)S(1)}, bf16[384,640]{1,0:T(8,128)(2,1)S(1)}, u32[]{:S(2)}, u32[]{:S(2)}) collective-permute-start(bf16[384,640]{1,0:T(8,128)(2,1)S(1)} %get-tuple-element.28.refs_0_.same), channel_id=1, source_target_pairs={{0,4},{2,18},{4,8},{6,22},{8,12},{10,26},{12,0},{14,30},{16,20},{1... | collective-permute-start | bytes 1474568 | tf_op jit(solution)/shard_map/ppermute | solution.py:29
  6.4 8.8 %collective-permute-start.7 = (bf16[384,640]{1,0:T(8,128)(2,1)S(1)}, bf16[384,640]{1,0:T(8,128)(2,1)S(1)}, u32[]{:S(2)}, u32[]{:S(2)}) collective-permute-start(bf16[384,640]{1,0:T(8,128)(2,1)S(1)} %get-tuple-element.28.refs_0_.same), channel_id=1, source_target_pairs={{0,12},{2,50},{4,0},{6,54},{8,4},{10,58},{12,8},{14,62},{16,28},{1... | collective-permute-start | bytes 1474568 | tf_op jit(solution)/shard_map/ppermute | solution.py:29
  8.1 10.3 %collective-permute-start.3 = (bf16[192,640]{1,0:T(8,128)(2,1)S(1)}, bf16[192,640]{1,0:T(8,128)(2,1)S(1)}, u32[]{:S(2)}, u32[]{:S(2)}) collective-permute-start(bf16[192,640]{1,0:T(8,128)(2,1)S(1)} %pad_maximum_fusion.3), channel_id=1, source_target_pairs={{0,1},{1,0},{2,3},{3,2},{4,5},{5,4},{6,7},{7,6},{8,9},{9,8},{10,11... | collective-permute-start | bytes 737288 | tf_op jit(solution)/shard_map/ppermute | solution.py:48
  11.3 10.1 %collective-permute-start.1 = (bf16[384,640]{1,0:T(8,128)(2,1)S(1)}, bf16[384,640]{1,0:T(8,128)(2,1)S(1)}, u32[]{:S(2)}, u32[]{:S(2)}) collective-permute-start(bf16[384,640]{1,0:T(8,128)(2,1)S(1)} %slice.47.refs_1_.other), channel_id=1, source_target_pairs={{0,4},{2,18},{4,8},{6,22},{8,12},{10,26},{12,0},{14,30},{16,20},{1... | collective-permute-start | bytes 1474568 | tf_op jit(solution)/shard_map/ppermute | solution.py:29
  11.8 11.3 %collective-permute-start.2 = (bf16[384,640]{1,0:T(8,128)(2,1)S(1)}, bf16[384,640]{1,0:T(8,128)(2,1)S(1)}, u32[]{:S(2)}, u32[]{:S(2)}) collective-permute-start(bf16[384,640]{1,0:T(8,128)(2,1)S(1)} %slice.47.refs_1_.other), channel_id=1, source_target_pairs={{0,12},{2,50},{4,0},{6,54},{8,4},{10,58},{12,8},{14,62},{16,28},{1... | collective-permute-start | bytes 1474568 | tf_op jit(solution)/shard_map/ppermute | solution.py:29
  18.5 14.7 %copy-start = (bf16[1,96,2560]{2,1,0:T(8,128)(2,1)S(1)}, bf16[1,96,2560]{2,1,0:T(8,128)(2,1)}, u32[]{:S(2)}) copy-start(bf16[1,96,2560]{2,1,0:T(8,128)(2,1)} %param.8) | copy-start | bytes 1474564
  18.5 14.7 %copy-start.1 = (bf16[1,96,2560]{2,1,0:T(8,128)(2,1)S(1)}, bf16[1,96,2560]{2,1,0:T(8,128)(2,1)}, u32[]{:S(2)}) copy-start(bf16[1,96,2560]{2,1,0:T(8,128)(2,1)} %param.9) | copy-start | bytes 1474564
  18.6 14.6 %collective-permute-start.4 = (bf16[384,640]{1,0:T(8,128)(2,1)S(1)}, bf16[384,640]{1,0:T(8,128)(2,1)S(1)}, u32[]{:S(2)}, u32[]{:S(2)}) collective-permute-start(bf16[384,640]{1,0:T(8,128)(2,1)S(1)} %pad_maximum_fusion.q_ref), channel_id=1, source_target_pairs={{0,32},{2,10},{4,36},{6,14},{8,40},{10,2},{12,44},{14,6},{16,48},{... | collective-permute-start | bytes 1474568 | tf_op jit(solution)/shard_map/ppermute | solution.py:29
  20.7 18.4 %collective-permute-start.11 = (bf16[384,640]{1,0:T(8,128)(2,1)S(1)}, bf16[384,640]{1,0:T(8,128)(2,1)S(1)}, u32[]{:S(2)}, u32[]{:S(2)}) collective-permute-start(bf16[384,640]{1,0:T(8,128)(2,1)S(1)} %pad_maximum_fusion.q_ref), channel_id=1, source_target_pairs={{0,48},{2,14},{4,52},{6,2},{8,56},{10,6},{12,60},{14,10},{16,0},{1... | collective-permute-start | bytes 1474568 | tf_op jit(solution)/shard_map/ppermute | solution.py:29
  21.5 17.5 %collective-permute-start.8 = (bf16[384,640]{1,0:T(8,128)(2,1)S(1)}, bf16[384,640]{1,0:T(8,128)(2,1)S(1)}, u32[]{:S(2)}, u32[]{:S(2)}) collective-permute-start(bf16[384,640]{1,0:T(8,128)(2,1)S(1)} %pad_maximum_fusion.1), channel_id=1, source_target_pairs={{0,4},{2,18},{4,8},{6,22},{8,12},{10,26},{12,0},{14,30},{16,20},{1... | collective-permute-start | bytes 1474568 | tf_op jit(solution)/shard_map/ppermute | solution.py:29
  23.2 15.8 %collective-permute-start.9 = (bf16[384,640]{1,0:T(8,128)(2,1)S(1)}, bf16[384,640]{1,0:T(8,128)(2,1)S(1)}, u32[]{:S(2)}, u32[]{:S(2)}) collective-permute-start(bf16[384,640]{1,0:T(8,128)(2,1)S(1)} %pad_maximum_fusion.2), channel_id=1, source_target_pairs={{0,12},{2,50},{4,0},{6,54},{8,4},{10,58},{12,8},{14,62},{16,28},{1... | collective-permute-start | bytes 1474568 | tf_op jit(solution)/shard_map/ppermute | solution.py:29
  29.8 21.2 %collective-permute-start.10 = (bf16[384,640]{1,0:T(8,128)(2,1)S(1)}, bf16[384,640]{1,0:T(8,128)(2,1)S(1)}, u32[]{:S(2)}, u32[]{:S(2)}) collective-permute-start(bf16[384,640]{1,0:T(8,128)(2,1)S(1)} %pad_maximum_fusion.q_ref), channel_id=1, source_target_pairs={{0,16},{2,6},{4,20},{6,10},{8,24},{10,14},{12,28},{14,2},{16,32},{... | collective-permute-start | bytes 1474568 | tf_op jit(solution)/shard_map/ppermute | solution.py:29
  33.2 21.6 %collective-permute-start.5 = (bf16[192,1280]{1,0:T(8,128)(2,1)S(1)}, bf16[192,1280]{1,0:T(8,128)(2,1)S(1)}, u32[]{:S(2)}, u32[]{:S(2)}) collective-permute-start(bf16[192,1280]{1,0:T(8,128)(2,1)S(1)} %shard_map.95), channel_id=1, source_target_pairs={{0,1},{1,0},{2,3},{3,2},{4,5},{5,4},{6,7},{7,6},{8,9},{9,8},{10,11... | collective-permute-start | bytes 1474568 | tf_op jit(solution)/shard_map/ppermute | solution.py:48
  39.0 29.4 %slice-start = ((s8[13107200]{0:T(1024)(128)(4,1)}), s8[4194304]{0:T(1024)(128)(4,1)S(1)}, s32[]{:S(2)}) async-start(s8[13107200]{0:T(1024)(128)(4,1)} %bitcast.9), calls=%async_computation | async-start | bytes 8388608
  42.8 25.6 %slice-start.1 = ((s8[13107200]{0:T(1024)(128)(4,1)}), s8[4194304]{0:T(1024)(128)(4,1)S(1)}, s32[]{:S(2)}) async-start(s8[13107200]{0:T(1024)(128)(4,1)} %bitcast.9), calls=%async_computation.1 | async-start | bytes 8388608
  42.8 15.4 %collective-permute-start.13 = (bf16[384,768]{1,0:T(8,128)(2,1)S(1)}, bf16[384,768]{1,0:T(8,128)(2,1)S(1)}, u32[]{:S(2)}, u32[]{:S(2)}) collective-permute-start(bf16[384,768]{1,0:T(8,128)(2,1)S(1)} %shard_map.98), channel_id=1, source_target_pairs={{0,16},{2,6},{4,20},{6,10},{8,24},{10,14},{12,28},{14,2},{16,32},{... | collective-permute-start | bytes 1769480 | tf_op jit(solution)/shard_map/ppermute | solution.py:29
  47.3 21.1 %slice-start.2 = ((s8[13107200]{0:T(1024)(128)(4,1)}), s8[4194304]{0:T(1024)(128)(4,1)S(1)}, s32[]{:S(2)}) async-start(s8[13107200]{0:T(1024)(128)(4,1)} %bitcast.9), calls=%async_computation.2 | async-start | bytes 8388608
  47.3 14.0 %collective-permute-start.12 = (bf16[384,768]{1,0:T(8,128)(2,1)S(1)}, bf16[384,768]{1,0:T(8,128)(2,1)S(1)}, u32[]{:S(2)}, u32[]{:S(2)}) collective-permute-start(bf16[384,768]{1,0:T(8,128)(2,1)S(1)} %shard_map.96), channel_id=1, source_target_pairs={{0,32},{2,10},{4,36},{6,14},{8,40},{10,2},{12,44},{14,6},{16,48},{... | collective-permute-start | bytes 1769480 | tf_op jit(solution)/shard_map/ppermute | solution.py:29
  55.5 5.8 %collective-permute-start.14 = (bf16[384,640]{1,0:T(8,128)(2,1)S(1)}, bf16[384,640]{1,0:T(8,128)(2,1)S(1)}, u32[]{:S(2)}, u32[]{:S(2)}) collective-permute-start(bf16[384,640]{1,0:T(8,128)(2,1)S(1)} %get-tuple-element.36), channel_id=1, source_target_pairs={{0,2},{2,0},{4,6},{6,4},{8,10},{10,8},{12,14},{14,12},{16,18},{18,... | collective-permute-start | bytes 1474568 | tf_op jit(solution)/shard_map/ppermute | solution.py:41
  55.6 10.2 %collective-permute-start.15 = (bf16[384,768]{1,0:T(8,128)(2,1)S(1)}, bf16[384,768]{1,0:T(8,128)(2,1)S(1)}, u32[]{:S(2)}, u32[]{:S(2)}) collective-permute-start(bf16[384,768]{1,0:T(8,128)(2,1)S(1)} %shard_map.97), channel_id=1, source_target_pairs={{0,48},{2,14},{4,52},{6,2},{8,56},{10,6},{12,60},{14,10},{16,0},{1... | collective-permute-start | bytes 1769480 | tf_op jit(solution)/shard_map/ppermute | solution.py:29
  61.3 7.1 %slice-start.3 = ((s8[13107200]{0:T(1024)(128)(4,1)}), s8[524288]{0:T(1024)(128)(4,1)S(1)}, s32[]{:S(2)}) async-start(s8[13107200]{0:T(1024)(128)(4,1)} %bitcast.9), calls=%async_computation.3 | async-start | bytes 1048576
  65.2 3.3 %copy-start.5 = (f32[1,5120]{1,0:T(1,128)S(1)}, f32[1,5120]{1,0:T(1,128)}, u32[]{:S(2)}) copy-start(f32[1,5120]{1,0:T(1,128)} %g_ref.3) | copy-start | bytes 61444
  66.6 1.8 %collective-permute-start.16 = (bf16[192,640]{1,0:T(8,128)(2,1)S(1)}, bf16[192,640]{1,0:T(8,128)(2,1)S(1)}, u32[]{:S(2)}, u32[]{:S(2)}) collective-permute-start(bf16[192,640]{1,0:T(8,128)(2,1)S(1)} %shard_map.103), channel_id=1, source_target_pairs={{0,2},{2,0},{4,6},{6,4},{8,10},{10,8},{12,14},{14,12},{16,18},{18,... | collective-permute-start | bytes 737288 | tf_op jit(solution)/shard_map/ppermute | solution.py:41
  70.2 10.2 %collective-permute-start.17 = (bf16[96,1536]{1,0:T(8,128)(2,1)S(1)}, bf16[96,1536]{1,0:T(8,128)(2,1)S(1)}, u32[]{:S(2)}, u32[]{:S(2)}) collective-permute-start(bf16[96,1536]{1,0:T(8,128)(2,1)S(1)} %get-tuple-element.39), channel_id=1, source_target_pairs={{0,64},{1,65},{64,0},{65,1},{2,66},{3,67},{66,2},{67,3},{4,68},{5,... | collective-permute-start | bytes 884744 | tf_op jit(solution)/shard_map/ppermute | solution.py:53
  71.2 10.0 %collective-permute-start.18 = (bf16[96,1536]{1,0:T(8,128)(2,1)S(1)}, bf16[96,1536]{1,0:T(8,128)(2,1)S(1)}, u32[]{:S(2)}, u32[]{:S(2)}) collective-permute-start(bf16[96,1536]{1,0:T(8,128)(2,1)S(1)} %get-tuple-element.40), channel_id=1, source_target_pairs={{0,65},{1,64},{64,1},{65,0},{2,67},{3,66},{66,3},{67,2},{4,69},{5,... | collective-permute-start | bytes 884744 | tf_op jit(solution)/shard_map/ppermute | solution.py:53
  77.2 17.1 %collective-permute-start.19 = (bf16[96,3584]{1,0:T(8,128)(2,1)S(1)}, bf16[96,3584]{1,0:T(8,128)(2,1)S(1)}, u32[]{:S(2)}, u32[]{:S(2)}) collective-permute-start(bf16[96,3584]{1,0:T(8,128)(2,1)S(1)} %get-tuple-element.41), channel_id=1, source_target_pairs={{0,64},{1,65},{64,0},{65,1},{2,66},{3,67},{66,2},{67,3},{4,68},{5,... | collective-permute-start | bytes 2064392 | tf_op jit(solution)/shard_map/ppermute | solution.py:53
  78.0 17.9 %collective-permute-start.20 = (bf16[96,3584]{1,0:T(8,128)(2,1)S(1)}, bf16[96,3584]{1,0:T(8,128)(2,1)S(1)}, u32[]{:S(2)}, u32[]{:S(2)}) collective-permute-start(bf16[96,3584]{1,0:T(8,128)(2,1)S(1)} %get-tuple-element.42), channel_id=1, source_target_pairs={{0,65},{1,64},{64,1},{65,0},{2,67},{3,66},{66,3},{67,2},{4,69},{5,... | collective-permute-start | bytes 2064392 | tf_op jit(solution)/shard_map/ppermute | solution.py:53

commit v5 on v4

--- a/solution.py
+++ b/solution.py
@@ -358,8 +358,8 @@
     k_far = keys_along(jnp.concatenate([up_same[:patch], up_other[:patch]], axis=0), 1)
     v_far = keys_along(jnp.concatenate([down_same[patch:], down_other[patch:]], axis=0), -1)
 
-    fresh_keys, fresh_values, up_other, down_other, q_far = lax.optimization_barrier(
-        (fresh_keys, fresh_values, up_other, down_other, q_far)
+    fresh_keys, fresh_values, up_other, down_other, q_up, q_down = lax.optimization_barrier(
+        (fresh_keys, fresh_values, up_other, down_other, q_up, q_down)
     )
     got = other_half(outgoing_fresh(head_table, fresh_keys[0], fresh_values[0]), 0, 1)
     blocks = [same, other, up_same, up_other, down_same, down_other, k_far, v_far]

time: 97.4 us -> 97.3 us (level)
    ppermute x2, starting transfers between devices: 5.2 us -> 7.51 us  [other_half(): return lax.ppermute(value, ('patch', 'head'), pairs)]
    ppermute x12, starting transfers between devices: 28 us -> 26.4 us  [along(): return lax.ppermute(value, 'patch', pairs)]
where the time goes in v5:
time: 97.3 us; the launch traced here: 97 us
  starting transfers between devices  39 us (40%)
  waiting for transfers between devices  26.9 us (28%)
  Pallas kernels  25.4 us (26%)
  local copies, waits for them, and re-layouts  3.33 us (3%)
  other arithmetic  1.49 us (2%)
    ppermute x12, starting transfers between devices, along(): return lax.ppermute(value, 'patch', pairs)  26.4 us
    pallas_call x4, Pallas kernels, attention(): pl.pallas_call(kernel, out_shape=jax.ShapeDtypeStruct((rows, width + HEAD...  15.1 us
    ppermute x4, waiting for transfers between devices, onward_to(): return lax.ppermute(value, ('pipe', 'head'), pairs)  14.9 us
    ppermute x12, waiting for transfers between devices, along(): return lax.ppermute(value, 'patch', pairs)  8.13 us
    ppermute x2, starting transfers between devices, other_half(): return lax.ppermute(value, ('patch', 'head'), pairs)  7.51 us
    pallas_call x2, Pallas kernels, project(): pl.pallas_call(project_kernel, grid_spec=pltpu.PrefetchScalarGridSpec(num...  5.54 us
    ppermute x4, starting transfers between devices, onward_to(): return lax.ppermute(value, ('pipe', 'head'), pairs)  4.82 us
    ppermute x2, waiting for transfers between devices, other_half(): return lax.ppermute(value, ('patch', 'head'), pairs)  3.17 us
  transfers between devices with their start and end apart: 21, of which 11 were waited for; matrix products, arithmetic and copies ran while one was open for 0% of the time, Pallas kernels for 23%

profile of v5, /device:TPU:0, one launch (start us, length us, event | category | flops | bytes accessed | tf_op | source)
XLA Modules:
  0.0 97.0 jit_solution(12315676651047440673)
XLA Ops:
  0.6 0.1 pad_add_fusion.table_ref
  0.7 1.0 %copy-done.2 = bf16[1,192,1280]{2,1,0:T(8,128)(2,1)S(1)} copy-done((bf16[1,192,1280]{2,1,0:T(8,128)(2,1)S(1)}, bf16[1,192,1280]{2,1,0:T(8,128)(2,1)}, u32[]{:S(2)}) %copy-start.2) | copy-done | bytes 491544
  1.8 1.0 %copy-done.3 = bf16[1,192,1280]{2,1,0:T(8,128)(2,1)S(1)} copy-done((bf16[1,192,1280]{2,1,0:T(8,128)(2,1)S(1)}, bf16[1,192,1280]{2,1,0:T(8,128)(2,1)}, u32[]{:S(2)}) %copy-start.3) | copy-done | bytes 491544
  2.8 1.0 %copy-done.4 = bf16[1,96,2560]{2,1,0:T(8,128)(2,1)S(1)} copy-done((bf16[1,96,2560]{2,1,0:T(8,128)(2,1)S(1)}, bf16[1,96,2560]{2,1,0:T(8,128)(2,1)}, u32[]{:S(2)}) %copy-start.4) | copy-done | bytes 491544
  3.8 0.8 shard_map.94
  4.6 0.1 collective-permute-start
  4.7 1.7 %collective-permute-start.8 = (bf16[384,640]{1,0:T(8,128)(2,1)S(1)}, bf16[384,640]{1,0:T(8,128)(2,1)S(1)}, u32[]{:S(2)}, u32[]{:S(2)}) collective-permute-start(bf16[384,640]{1,0:T(8,128)(2,1)S(1)} %get-tuple-element.28.refs_0_.same), channel_id=1, source_target_pairs={{0,4},{2,18},{4,8},{6,22},{8,12},{10,26},{12,0},{14,30},{16,20},{1... | collective-permute-start | bytes 1474568 | tf_op jit(solution)/shard_map/ppermute | solution.py:29
  6.4 1.6 %collective-permute-start.9 = (bf16[384,640]{1,0:T(8,128)(2,1)S(1)}, bf16[384,640]{1,0:T(8,128)(2,1)S(1)}, u32[]{:S(2)}, u32[]{:S(2)}) collective-permute-start(bf16[384,640]{1,0:T(8,128)(2,1)S(1)} %get-tuple-element.28.refs_0_.same), channel_id=1, source_target_pairs={{0,12},{2,50},{4,0},{6,54},{8,4},{10,58},{12,8},{14,62},{16,28},{1... | collective-permute-start | bytes 1474568 | tf_op jit(solution)/shard_map/ppermute | solution.py:29
  8.0 0.0 collective-permute-done
  8.1 3.2 %collective-permute-start.3 = (bf16[192,640]{1,0:T(8,128)(2,1)S(1)}, bf16[192,640]{1,0:T(8,128)(2,1)S(1)}, u32[]{:S(2)}, u32[]{:S(2)}) collective-permute-start(bf16[192,640]{1,0:T(8,128)(2,1)S(1)} %pad_maximum_fusion.3), channel_id=1, source_target_pairs={{0,1},{1,0},{2,3},{3,2},{4,5},{5,4},{6,7},{7,6},{8,9},{9,8},{10,11... | collective-permute-start | bytes 737288 | tf_op jit(solution)/shard_map/ppermute | solution.py:48
  11.3 0.5 collective-permute-start.1
  11.8 2.8 %collective-permute-start.2 = (bf16[384,640]{1,0:T(8,128)(2,1)S(1)}, bf16[384,640]{1,0:T(8,128)(2,1)S(1)}, u32[]{:S(2)}, u32[]{:S(2)}) collective-permute-start(bf16[384,640]{1,0:T(8,128)(2,1)S(1)} %slice.47.refs_1_.other), channel_id=1, source_target_pairs={{0,12},{2,50},{4,0},{6,54},{8,4},{10,58},{12,8},{14,62},{16,28},{1... | collective-permute-start | bytes 1474568 | tf_op jit(solution)/shard_map/ppermute | solution.py:29
  14.6 0.2 collective-permute-done.8.refs_2_.refs_0_
  14.8 0.4 collective-permute-done.9.refs_4_.refs_2_
  15.3 3.2 %collective-permute-done.3 = bf16[192,640]{1,0:T(8,128)(2,1)S(1)} collective-permute-done((bf16[192,640]{1,0:T(8,128)(2,1)S(1)}, bf16[192,640]{1,0:T(8,128)(2,1)S(1)}, u32[]{:S(2)}, u32[]{:S(2)}) %collective-permute-start.3) | collective-permute-done | bytes 245792 | tf_op jit(solution)/shard_map/ppermute | solution.py:48
  18.5 0.0 copy-start
  18.5 0.0 copy-start.1
  18.6 0.2 collective-permute-start.4
  18.7 3.2 %collective-permute-start.5 = (bf16[384,640]{1,0:T(8,128)(2,1)S(1)}, bf16[384,640]{1,0:T(8,128)(2,1)S(1)}, u32[]{:S(2)}, u32[]{:S(2)}) collective-permute-start(bf16[384,640]{1,0:T(8,128)(2,1)S(1)} %pad_maximum_fusion.q_ref), channel_id=1, source_target_pairs={{0,48},{2,14},{4,52},{6,2},{8,56},{10,6},{12,60},{14,10},{16,0},{1... | collective-permute-start | bytes 1474568 | tf_op jit(solution)/shard_map/ppermute | solution.py:29
  21.9 0.0 collective-permute-done.1.refs_3_.refs_1_
  21.9 0.7 collective-permute-start.10
  22.6 0.0 collective-permute-done.2.refs_5_.refs_3_
  22.7 2.7 %collective-permute-start.11 = (bf16[384,640]{1,0:T(8,128)(2,1)S(1)}, bf16[384,640]{1,0:T(8,128)(2,1)S(1)}, u32[]{:S(2)}, u32[]{:S(2)}) collective-permute-start(bf16[384,640]{1,0:T(8,128)(2,1)S(1)} %pad_maximum_fusion.2), channel_id=1, source_target_pairs={{0,12},{2,50},{4,0},{6,54},{8,4},{10,58},{12,8},{14,62},{16,28},{1... | collective-permute-start | bytes 1474568 | tf_op jit(solution)/shard_map/ppermute | solution.py:29
  25.4 4.9 %collective-permute-start.7 = (bf16[384,640]{1,0:T(8,128)(2,1)S(1)}, bf16[384,640]{1,0:T(8,128)(2,1)S(1)}, u32[]{:S(2)}, u32[]{:S(2)}) collective-permute-start(bf16[384,640]{1,0:T(8,128)(2,1)S(1)} %pad_maximum_fusion.q_ref), channel_id=1, source_target_pairs={{0,32},{2,10},{4,36},{6,14},{8,40},{10,2},{12,44},{14,6},{16,48},{... | collective-permute-start | bytes 1474568 | tf_op jit(solution)/shard_map/ppermute | solution.py:29
  30.3 1.6 %collective-permute-done.4.q_ref = bf16[384,640]{1,0:T(8,128)(2,1)S(1)} collective-permute-done((bf16[384,640]{1,0:T(8,128)(2,1)S(1)}, bf16[384,640]{1,0:T(8,128)(2,1)S(1)}, u32[]{:S(2)}, u32[]{:S(2)}) %collective-permute-start.4) | collective-permute-done | bytes 491552 | tf_op jit(solution)/shard_map/ppermute | solution.py:29
  31.9 0.0 collective-permute-done.5.q_ref
  31.9 4.3 %collective-permute-start.6 = (bf16[192,1280]{1,0:T(8,128)(2,1)S(1)}, bf16[192,1280]{1,0:T(8,128)(2,1)S(1)}, u32[]{:S(2)}, u32[]{:S(2)}) collective-permute-start(bf16[192,1280]{1,0:T(8,128)(2,1)S(1)} %shard_map.95), channel_id=1, source_target_pairs={{0,1},{1,0},{2,3},{3,2},{4,5},{5,4},{6,7},{7,6},{8,9},{9,8},{10,11... | collective-permute-start | bytes 1474568 | tf_op jit(solution)/shard_map/ppermute | solution.py:48
  36.3 1.3 %collective-permute-done.10.refs_6_.refs_4_ = bf16[384,640]{1,0:T(8,128)(2,1)S(1)} collective-permute-done((bf16[384,640]{1,0:T(8,128)(2,1)S(1)}, bf16[384,640]{1,0:T(8,128)(2,1)S(1)}, u32[]{:S(2)}, u32[]{:S(2)}) %collective-permute-start.10) | collective-permute-done | bytes 491552 | tf_op jit(solution)/shard_map/ppermute | solution.py:29
  37.6 0.0 collective-permute-done.11.refs_7_.refs_5_
  37.6 3.8 %shard_map.98 = bf16[384,768]{1,0:T(8,128)(2,1)S(1)} custom-call(bf16[384,640]{1,0:T(8,128)(2,1)S(1)} %collective-permute-done.5.q_ref, bf16[384,640]{1,0:T(8,128)(2,1)S(1)} %get-tuple-element.28.refs_0_.same, bf16[384,640]{1,0:T(8,128)(2,1)S(1)} %slice.47.refs_1_.other, bf16[384,640]{1,0:T(8,128)(2,1)S(1)} %collective-permute-done.8.refs_2_.refs_0_, ...), custom_call_target="tpu_custom_call" | custom-call | flops 1509949440 | bytes 4194304 | tf_op jit(solution)/shard_map/pallas_call | solution.py:258
  41.4 0.0 slice-start.1
  41.4 2.9 %collective-permute-start.13 = (bf16[384,768]{1,0:T(8,128)(2,1)S(1)}, bf16[384,768]{1,0:T(8,128)(2,1)S(1)}, u32[]{:S(2)}, u32[]{:S(2)}) collective-permute-start(bf16[384,768]{1,0:T(8,128)(2,1)S(1)} %shard_map.98), channel_id=1, source_target_pairs={{0,16},{2,6},{4,20},{6,10},{8,24},{10,14},{12,28},{14,2},{16,32},{... | collective-permute-start | bytes 1769480 | tf_op jit(solution)/shard_map/ppermute | solution.py:29
  44.3 0.0 collective-permute-done.7.q_ref
  44.3 3.8 %shard_map.96 = bf16[384,768]{1,0:T(8,128)(2,1)S(1)} custom-call(bf16[384,640]{1,0:T(8,128)(2,1)S(1)} %collective-permute-done.7.q_ref, bf16[384,640]{1,0:T(8,128)(2,1)S(1)} %get-tuple-element.28.refs_0_.same, bf16[384,640]{1,0:T(8,128)(2,1)S(1)} %slice.47.refs_1_.other, bf16[384,640]{1,0:T(8,128)(2,1)S(1)} %collective-permute-done.8.refs_2_.refs_0_, ...), custom_call_target="tpu_custom_call" | custom-call | flops 1509949440 | bytes 4194304 | tf_op jit(solution)/shard_map/pallas_call | solution.py:258
  48.0 0.0 slice-start.2
  48.0 3.7 %collective-permute-start.12 = (bf16[384,768]{1,0:T(8,128)(2,1)S(1)}, bf16[384,768]{1,0:T(8,128)(2,1)S(1)}, u32[]{:S(2)}, u32[]{:S(2)}) collective-permute-start(bf16[384,768]{1,0:T(8,128)(2,1)S(1)} %shard_map.96), channel_id=1, source_target_pairs={{0,32},{2,10},{4,36},{6,14},{8,40},{10,2},{12,44},{14,6},{16,48},{... | collective-permute-start | bytes 1769480 | tf_op jit(solution)/shard_map/ppermute | solution.py:29
  51.7 3.8 %shard_map.97 = bf16[384,768]{1,0:T(8,128)(2,1)S(1)} custom-call(bf16[384,640]{1,0:T(8,128)(2,1)S(1)} %collective-permute-done.4.q_ref, bf16[384,640]{1,0:T(8,128)(2,1)S(1)} %get-tuple-element.28.refs_0_.same, bf16[384,640]{1,0:T(8,128)(2,1)S(1)} %slice.47.refs_1_.other, bf16[384,640]{1,0:T(8,128)(2,1)S(1)} %collective-permute-done.8.refs_2_.refs_0_, ...), custom_call_target="tpu_custom_call" | custom-call | flops 1509949440 | bytes 4194304 | tf_op jit(solution)/shard_map/pallas_call | solution.py:258
  55.5 0.0 collective-permute-done.6.got_ref
  55.5 0.7 shard_map.100
  56.2 0.1 collective-permute-start.14
  56.3 1.7 %collective-permute-start.15 = (bf16[384,768]{1,0:T(8,128)(2,1)S(1)}, bf16[384,768]{1,0:T(8,128)(2,1)S(1)}, u32[]{:S(2)}, u32[]{:S(2)}) collective-permute-start(bf16[384,768]{1,0:T(8,128)(2,1)S(1)} %shard_map.97), channel_id=1, source_target_pairs={{0,48},{2,14},{4,52},{6,2},{8,56},{10,6},{12,60},{14,10},{16,0},{1... | collective-permute-start | bytes 1769480 | tf_op jit(solution)/shard_map/ppermute | solution.py:29
  58.0 4.0 %collective-permute-done.12.b_ref = bf16[384,768]{1,0:T(8,128)(2,1)S(1)} collective-permute-done((bf16[384,768]{1,0:T(8,128)(2,1)S(1)}, bf16[384,768]{1,0:T(8,128)(2,1)S(1)}, u32[]{:S(2)}, u32[]{:S(2)}) %collective-permute-start.12) | collective-permute-done | bytes 589856 | tf_op jit(solution)/shard_map/ppermute | solution.py:29
  62.0 0.0 collective-permute-done.14.refs_7_
  62.0 3.8 %shard_map.101.a_ref = bf16[384,768]{1,0:T(8,128)(2,1)S(1)} custom-call(bf16[384,640]{1,0:T(8,128)(2,1)S(1)} %pad_maximum_fusion.q_ref, bf16[384,640]{1,0:T(8,128)(2,1)S(1)} %get-tuple-element.28.refs_0_.same, bf16[384,640]{1,0:T(8,128)(2,1)S(1)} %slice.47.refs_1_.other, bf16[384,640]{1,0:T(8,128)(2,1)S(1)} %collective-permute-done.8.refs_2_.refs_0_, ...), custom_call_target="tpu_custom_call" | custom-call | flops 1509949440 | bytes 4194304 | tf_op jit(solution)/shard_map/pallas_call | solution.py:258
  65.9 0.0 copy-start.5
  65.9 0.6 collective-permute-done.15.c_ref
  66.5 0.8 shard_map.103
  67.3 0.1 collective-permute-start.16
  67.4 0.8 shard_map.102.a_ref
  68.3 0.7 collective-permute-done.16.b_ref
  69.0 1.7 %shard_map.104 = (bf16[96,1536]{1,0:T(8,128)(2,1)S(1)}, bf16[96,1536]{1,0:T(8,128)(2,1)S(1)}) custom-call(s32[1]{0:T(128)} %bitcast.1.core_ref, bf16[192,640]{1,0:T(8,128)(2,1)S(1)} %shard_map.102.a_ref, bf16[192,640]{1,0:T(8,128)(2,1)S(1)} %collective-permute-done.16.b_ref, bf16[1280,5120]{1,0:T(8,128)(2,1)S(1)} %bitcast.11, f32[1,5120]{1,0:T(1,128)S(1)} %copy-done.5), custom_call_target="tpu_custom_call" | custom-call | flops 754974720 | bytes 3932160 | tf_op jit(solution)/shard_map/pallas_call | solution.py:318
  70.7 0.3 collective-permute-start.17
  71.0 2.1 %collective-permute-start.18 = (bf16[96,1536]{1,0:T(8,128)(2,1)S(1)}, bf16[96,1536]{1,0:T(8,128)(2,1)S(1)}, u32[]{:S(2)}, u32[]{:S(2)}) collective-permute-start(bf16[96,1536]{1,0:T(8,128)(2,1)S(1)} %get-tuple-element.42), channel_id=1, source_target_pairs={{0,65},{1,64},{64,1},{65,0},{2,67},{3,66},{66,3},{67,2},{4,69},{5,... | collective-permute-start | bytes 884744 | tf_op jit(solution)/shard_map/ppermute | solution.py:53
  73.1 3.8 %shard_map.105 = (bf16[96,3584]{1,0:T(8,128)(2,1)S(1)}, bf16[96,3584]{1,0:T(8,128)(2,1)S(1)}) custom-call(s32[1]{0:T(128)} %bitcast.1.core_ref, bf16[192,640]{1,0:T(8,128)(2,1)S(1)} %shard_map.102.a_ref, bf16[192,640]{1,0:T(8,128)(2,1)S(1)} %collective-permute-done.16.b_ref, bf16[1280,5120]{1,0:T(8,128)(2,1)S(1)} %bitcast.12, f32[1,5120]{1,0:T(1,128)S(1)} %copy-done.5), custom_call_target="tpu_custom_call" | custom-call | flops 1761607680 | bytes 9175040 | tf_op jit(solution)/shard_map/pallas_call | solution.py:318
  77.0 0.8 collective-permute-start.19
  77.8 1.6 %collective-permute-start.20 = (bf16[96,3584]{1,0:T(8,128)(2,1)S(1)}, bf16[96,3584]{1,0:T(8,128)(2,1)S(1)}, u32[]{:S(2)}, u32[]{:S(2)}) collective-permute-start(bf16[96,3584]{1,0:T(8,128)(2,1)S(1)} %get-tuple-element.44), channel_id=1, source_target_pairs={{0,65},{1,64},{64,1},{65,0},{2,67},{3,66},{66,3},{67,2},{4,69},{5,... | collective-permute-start | bytes 2064392 | tf_op jit(solution)/shard_map/ppermute | solution.py:53
  79.3 1.5 %shard_map.99 = (bf16[192,1280]{1,0:T(8,128)(2,1)}, bf16[192,1280]{1,0:T(8,128)(2,1)}) custom-call(s32[2]{0:T(128)S(1)} %pad_add_fusion.table_ref, bf16[96,2560]{1,0:T(8,128)(2,1)S(1)} %bitcast.15, bf16[96,2560]{1,0:T(8,128)(2,1)S(1)} %bitcast.18, bf16[192,1280]{1,0:T(8,128)(2,1)S(1)} %collective-permute-done.6.got_ref), custom_call_target="tpu_custom_call" | custom-call | tf_op jit(solution)/shard_map/pallas_call | solution.py:169
  80.9 0.0 collective-permute-done.17
  80.9 0.4 collective-permute-done.18
  81.3 0.1 add_convert_fusion.1
  81.3 13.2 %collective-permute-done.19 = bf16[96,3584]{1,0:T(8,128)(2,1)S(1)} collective-permute-done((bf16[96,3584]{1,0:T(8,128)(2,1)S(1)}, bf16[96,3584]{1,0:T(8,128)(2,1)S(1)}, u32[]{:S(2)}, u32[]{:S(2)}) %collective-permute-start.19) | collective-permute-done | bytes 688160 | tf_op jit(solution)/shard_map/ppermute | solution.py:53
  94.5 1.3 %collective-permute-done.20 = bf16[96,3584]{1,0:T(8,128)(2,1)S(1)} collective-permute-done((bf16[96,3584]{1,0:T(8,128)(2,1)S(1)}, bf16[96,3584]{1,0:T(8,128)(2,1)S(1)}, u32[]{:S(2)}, u32[]{:S(2)}) %collective-permute-start.20) | collective-permute-done | bytes 688160 | tf_op jit(solution)/shard_map/ppermute | solution.py:53
  95.8 0.2 add_convert_fusion
  96.0 1.0 %maximum_bitcast_fusion = bf16[1,96,5120]{2,1,0:T(8,128)(2,1)} fusion(bf16[96,3584]{1,0:T(8,128)(2,1)S(1)} %add_convert_fusion, bf16[96,1536]{1,0:T(8,128)(2,1)S(1)} %add_convert_fusion.1), kind=kLoop, calls=%fused_computation.1 | loop fusion | flops 1966080 | bytes 1966080 | tf_op jit(solution)/shard_map/broadcast_in_dim | solution.py:386
  (27 shorter events, 0.4 us)
Async XLA Ops:
  0.7 1.0 %copy-start.2 = (bf16[1,192,1280]{2,1,0:T(8,128)(2,1)S(1)}, bf16[1,192,1280]{2,1,0:T(8,128)(2,1)}, u32[]{:S(2)}) copy-start(bf16[1,192,1280]{2,1,0:T(8,128)(2,1)} %k_ref.1) | copy-start | bytes 1474564
  1.7 1.0 %copy-start.3 = (bf16[1,192,1280]{2,1,0:T(8,128)(2,1)S(1)}, bf16[1,192,1280]{2,1,0:T(8,128)(2,1)}, u32[]{:S(2)}) copy-start(bf16[1,192,1280]{2,1,0:T(8,128)(2,1)} %v_ref.1) | copy-start | bytes 1474564
  2.8 1.0 %copy-start.4 = (bf16[1,96,2560]{2,1,0:T(8,128)(2,1)S(1)}, bf16[1,96,2560]{2,1,0:T(8,128)(2,1)}, u32[]{:S(2)}) copy-start(bf16[1,96,2560]{2,1,0:T(8,128)(2,1)} %q_ref.1) | copy-start | bytes 1474564
  4.6 3.4 %collective-permute-start = (bf16[576,640]{1,0:T(8,128)(2,1)S(1)}, bf16[576,640]{1,0:T(8,128)(2,1)S(1)}, u32[]{:S(2)}, u32[]{:S(2)}) collective-permute-start(bf16[576,640]{1,0:T(8,128)(2,1)S(1)} %get-tuple-element.24), channel_id=1, source_target_pairs={{0,2},{2,0},{4,6},{6,4},{8,10},{10,8},{12,14},{14,12},{16,18},{18,... | collective-permute-start | bytes 2211848 | tf_op jit(solution)/shard_map/ppermute | solution.py:41
  4.7 10.1 %collective-permute-start.8 = (bf16[384,640]{1,0:T(8,128)(2,1)S(1)}, bf16[384,640]{1,0:T(8,128)(2,1)S(1)}, u32[]{:S(2)}, u32[]{:S(2)}) collective-permute-start(bf16[384,640]{1,0:T(8,128)(2,1)S(1)} %get-tuple-element.28.refs_0_.same), channel_id=1, source_target_pairs={{0,4},{2,18},{4,8},{6,22},{8,12},{10,26},{12,0},{14,30},{16,20},{1... | collective-permute-start | bytes 1474568 | tf_op jit(solution)/shard_map/ppermute | solution.py:29
  6.4 8.8 %collective-permute-start.9 = (bf16[384,640]{1,0:T(8,128)(2,1)S(1)}, bf16[384,640]{1,0:T(8,128)(2,1)S(1)}, u32[]{:S(2)}, u32[]{:S(2)}) collective-permute-start(bf16[384,640]{1,0:T(8,128)(2,1)S(1)} %get-tuple-element.28.refs_0_.same), channel_id=1, source_target_pairs={{0,12},{2,50},{4,0},{6,54},{8,4},{10,58},{12,8},{14,62},{16,28},{1... | collective-permute-start | bytes 1474568 | tf_op jit(solution)/shard_map/ppermute | solution.py:29
  8.1 10.3 %collective-permute-start.3 = (bf16[192,640]{1,0:T(8,128)(2,1)S(1)}, bf16[192,640]{1,0:T(8,128)(2,1)S(1)}, u32[]{:S(2)}, u32[]{:S(2)}) collective-permute-start(bf16[192,640]{1,0:T(8,128)(2,1)S(1)} %pad_maximum_fusion.3), channel_id=1, source_target_pairs={{0,1},{1,0},{2,3},{3,2},{4,5},{5,4},{6,7},{7,6},{8,9},{9,8},{10,11... | collective-permute-start | bytes 737288 | tf_op jit(solution)/shard_map/ppermute | solution.py:48
  11.3 10.5 %collective-permute-start.1 = (bf16[384,640]{1,0:T(8,128)(2,1)S(1)}, bf16[384,640]{1,0:T(8,128)(2,1)S(1)}, u32[]{:S(2)}, u32[]{:S(2)}) collective-permute-start(bf16[384,640]{1,0:T(8,128)(2,1)S(1)} %slice.47.refs_1_.other), channel_id=1, source_target_pairs={{0,4},{2,18},{4,8},{6,22},{8,12},{10,26},{12,0},{14,30},{16,20},{1... | collective-permute-start | bytes 1474568 | tf_op jit(solution)/shard_map/ppermute | solution.py:29
  11.8 10.8 %collective-permute-start.2 = (bf16[384,640]{1,0:T(8,128)(2,1)S(1)}, bf16[384,640]{1,0:T(8,128)(2,1)S(1)}, u32[]{:S(2)}, u32[]{:S(2)}) collective-permute-start(bf16[384,640]{1,0:T(8,128)(2,1)S(1)} %slice.47.refs_1_.other), channel_id=1, source_target_pairs={{0,12},{2,50},{4,0},{6,54},{8,4},{10,58},{12,8},{14,62},{16,28},{1... | collective-permute-start | bytes 1474568 | tf_op jit(solution)/shard_map/ppermute | solution.py:29
  18.5 13.4 %copy-start = (bf16[1,96,2560]{2,1,0:T(8,128)(2,1)S(1)}, bf16[1,96,2560]{2,1,0:T(8,128)(2,1)}, u32[]{:S(2)}) copy-start(bf16[1,96,2560]{2,1,0:T(8,128)(2,1)} %param.8) | copy-start | bytes 1474564
  18.5 13.4 %copy-start.1 = (bf16[1,96,2560]{2,1,0:T(8,128)(2,1)S(1)}, bf16[1,96,2560]{2,1,0:T(8,128)(2,1)}, u32[]{:S(2)}) copy-start(bf16[1,96,2560]{2,1,0:T(8,128)(2,1)} %param.9) | copy-start | bytes 1474564
  18.6 13.3 %collective-permute-start.4 = (bf16[384,640]{1,0:T(8,128)(2,1)S(1)}, bf16[384,640]{1,0:T(8,128)(2,1)S(1)}, u32[]{:S(2)}, u32[]{:S(2)}) collective-permute-start(bf16[384,640]{1,0:T(8,128)(2,1)S(1)} %pad_maximum_fusion.q_ref), channel_id=1, source_target_pairs={{0,16},{2,6},{4,20},{6,10},{8,24},{10,14},{12,28},{14,2},{16,32},{... | collective-permute-start | bytes 1474568 | tf_op jit(solution)/shard_map/ppermute | solution.py:29
  18.7 13.2 %collective-permute-start.5 = (bf16[384,640]{1,0:T(8,128)(2,1)S(1)}, bf16[384,640]{1,0:T(8,128)(2,1)S(1)}, u32[]{:S(2)}, u32[]{:S(2)}) collective-permute-start(bf16[384,640]{1,0:T(8,128)(2,1)S(1)} %pad_maximum_fusion.q_ref), channel_id=1, source_target_pairs={{0,48},{2,14},{4,52},{6,2},{8,56},{10,6},{12,60},{14,10},{16,0},{1... | collective-permute-start | bytes 1474568 | tf_op jit(solution)/shard_map/ppermute | solution.py:29
  21.9 15.6 %collective-permute-start.10 = (bf16[384,640]{1,0:T(8,128)(2,1)S(1)}, bf16[384,640]{1,0:T(8,128)(2,1)S(1)}, u32[]{:S(2)}, u32[]{:S(2)}) collective-permute-start(bf16[384,640]{1,0:T(8,128)(2,1)S(1)} %pad_maximum_fusion.1), channel_id=1, source_target_pairs={{0,4},{2,18},{4,8},{6,22},{8,12},{10,26},{12,0},{14,30},{16,20},{1... | collective-permute-start | bytes 1474568 | tf_op jit(solution)/shard_map/ppermute | solution.py:29
  22.7 14.9 %collective-permute-start.11 = (bf16[384,640]{1,0:T(8,128)(2,1)S(1)}, bf16[384,640]{1,0:T(8,128)(2,1)S(1)}, u32[]{:S(2)}, u32[]{:S(2)}) collective-permute-start(bf16[384,640]{1,0:T(8,128)(2,1)S(1)} %pad_maximum_fusion.2), channel_id=1, source_target_pairs={{0,12},{2,50},{4,0},{6,54},{8,4},{10,58},{12,8},{14,62},{16,28},{1... | collective-permute-start | bytes 1474568 | tf_op jit(solution)/shard_map/ppermute | solution.py:29
  25.4 18.9 %collective-permute-start.7 = (bf16[384,640]{1,0:T(8,128)(2,1)S(1)}, bf16[384,640]{1,0:T(8,128)(2,1)S(1)}, u32[]{:S(2)}, u32[]{:S(2)}) collective-permute-start(bf16[384,640]{1,0:T(8,128)(2,1)S(1)} %pad_maximum_fusion.q_ref), channel_id=1, source_target_pairs={{0,32},{2,10},{4,36},{6,14},{8,40},{10,2},{12,44},{14,6},{16,48},{... | collective-permute-start | bytes 1474568 | tf_op jit(solution)/shard_map/ppermute | solution.py:29
  31.9 23.6 %collective-permute-start.6 = (bf16[192,1280]{1,0:T(8,128)(2,1)S(1)}, bf16[192,1280]{1,0:T(8,128)(2,1)S(1)}, u32[]{:S(2)}, u32[]{:S(2)}) collective-permute-start(bf16[192,1280]{1,0:T(8,128)(2,1)S(1)} %shard_map.95), channel_id=1, source_target_pairs={{0,1},{1,0},{2,3},{3,2},{4,5},{5,4},{6,7},{7,6},{8,9},{9,8},{10,11... | collective-permute-start | bytes 1474568 | tf_op jit(solution)/shard_map/ppermute | solution.py:48
  37.6 31.3 %slice-start = ((s8[13107200]{0:T(1024)(128)(4,1)}), s8[4194304]{0:T(1024)(128)(4,1)S(1)}, s32[]{:S(2)}) async-start(s8[13107200]{0:T(1024)(128)(4,1)} %bitcast.9), calls=%async_computation | async-start | bytes 8388608
  41.4 27.6 %slice-start.1 = ((s8[13107200]{0:T(1024)(128)(4,1)}), s8[4194304]{0:T(1024)(128)(4,1)S(1)}, s32[]{:S(2)}) async-start(s8[13107200]{0:T(1024)(128)(4,1)} %bitcast.9), calls=%async_computation.1 | async-start | bytes 8388608
  41.4 16.6 %collective-permute-start.13 = (bf16[384,768]{1,0:T(8,128)(2,1)S(1)}, bf16[384,768]{1,0:T(8,128)(2,1)S(1)}, u32[]{:S(2)}, u32[]{:S(2)}) collective-permute-start(bf16[384,768]{1,0:T(8,128)(2,1)S(1)} %shard_map.98), channel_id=1, source_target_pairs={{0,16},{2,6},{4,20},{6,10},{8,24},{10,14},{12,28},{14,2},{16,32},{... | collective-permute-start | bytes 1769480 | tf_op jit(solution)/shard_map/ppermute | solution.py:29
  48.0 20.9 %slice-start.2 = ((s8[13107200]{0:T(1024)(128)(4,1)}), s8[4194304]{0:T(1024)(128)(4,1)S(1)}, s32[]{:S(2)}) async-start(s8[13107200]{0:T(1024)(128)(4,1)} %bitcast.9), calls=%async_computation.2 | async-start | bytes 8388608
  48.0 14.0 %collective-permute-start.12 = (bf16[384,768]{1,0:T(8,128)(2,1)S(1)}, bf16[384,768]{1,0:T(8,128)(2,1)S(1)}, u32[]{:S(2)}, u32[]{:S(2)}) collective-permute-start(bf16[384,768]{1,0:T(8,128)(2,1)S(1)} %shard_map.96), channel_id=1, source_target_pairs={{0,32},{2,10},{4,36},{6,14},{8,40},{10,2},{12,44},{14,6},{16,48},{... | collective-permute-start | bytes 1769480 | tf_op jit(solution)/shard_map/ppermute | solution.py:29
  56.2 5.8 %collective-permute-start.14 = (bf16[384,640]{1,0:T(8,128)(2,1)S(1)}, bf16[384,640]{1,0:T(8,128)(2,1)S(1)}, u32[]{:S(2)}, u32[]{:S(2)}) collective-permute-start(bf16[384,640]{1,0:T(8,128)(2,1)S(1)} %get-tuple-element.38), channel_id=1, source_target_pairs={{0,2},{2,0},{4,6},{6,4},{8,10},{10,8},{12,14},{14,12},{16,18},{18,... | collective-permute-start | bytes 1474568 | tf_op jit(solution)/shard_map/ppermute | solution.py:41
  56.3 10.2 %collective-permute-start.15 = (bf16[384,768]{1,0:T(8,128)(2,1)S(1)}, bf16[384,768]{1,0:T(8,128)(2,1)S(1)}, u32[]{:S(2)}, u32[]{:S(2)}) collective-permute-start(bf16[384,768]{1,0:T(8,128)(2,1)S(1)} %shard_map.97), channel_id=1, source_target_pairs={{0,48},{2,14},{4,52},{6,2},{8,56},{10,6},{12,60},{14,10},{16,0},{1... | collective-permute-start | bytes 1769480 | tf_op jit(solution)/shard_map/ppermute | solution.py:29
  62.0 6.9 %slice-start.3 = ((s8[13107200]{0:T(1024)(128)(4,1)}), s8[524288]{0:T(1024)(128)(4,1)S(1)}, s32[]{:S(2)}) async-start(s8[13107200]{0:T(1024)(128)(4,1)} %bitcast.9), calls=%async_computation.3 | async-start | bytes 1048576
  65.9 3.1 %copy-start.5 = (f32[1,5120]{1,0:T(1,128)S(1)}, f32[1,5120]{1,0:T(1,128)}, u32[]{:S(2)}) copy-start(f32[1,5120]{1,0:T(1,128)} %g_ref.3) | copy-start | bytes 61444
  67.3 1.6 %collective-permute-start.16 = (bf16[192,640]{1,0:T(8,128)(2,1)S(1)}, bf16[192,640]{1,0:T(8,128)(2,1)S(1)}, u32[]{:S(2)}, u32[]{:S(2)}) collective-permute-start(bf16[192,640]{1,0:T(8,128)(2,1)S(1)} %shard_map.103), channel_id=1, source_target_pairs={{0,2},{2,0},{4,6},{6,4},{8,10},{10,8},{12,14},{14,12},{16,18},{18,... | collective-permute-start | bytes 737288 | tf_op jit(solution)/shard_map/ppermute | solution.py:41
  70.7 10.2 %collective-permute-start.17 = (bf16[96,1536]{1,0:T(8,128)(2,1)S(1)}, bf16[96,1536]{1,0:T(8,128)(2,1)S(1)}, u32[]{:S(2)}, u32[]{:S(2)}) collective-permute-start(bf16[96,1536]{1,0:T(8,128)(2,1)S(1)} %get-tuple-element.41), channel_id=1, source_target_pairs={{0,64},{1,65},{64,0},{65,1},{2,66},{3,67},{66,2},{67,3},{4,68},{5,... | collective-permute-start | bytes 884744 | tf_op jit(solution)/shard_map/ppermute | solution.py:53
  71.0 10.3 %collective-permute-start.18 = (bf16[96,1536]{1,0:T(8,128)(2,1)S(1)}, bf16[96,1536]{1,0:T(8,128)(2,1)S(1)}, u32[]{:S(2)}, u32[]{:S(2)}) collective-permute-start(bf16[96,1536]{1,0:T(8,128)(2,1)S(1)} %get-tuple-element.42), channel_id=1, source_target_pairs={{0,65},{1,64},{64,1},{65,0},{2,67},{3,66},{66,3},{67,2},{4,69},{5,... | collective-permute-start | bytes 884744 | tf_op jit(solution)/shard_map/ppermute | solution.py:53
  77.0 17.6 %collective-permute-start.19 = (bf16[96,3584]{1,0:T(8,128)(2,1)S(1)}, bf16[96,3584]{1,0:T(8,128)(2,1)S(1)}, u32[]{:S(2)}, u32[]{:S(2)}) collective-permute-start(bf16[96,3584]{1,0:T(8,128)(2,1)S(1)} %get-tuple-element.43), channel_id=1, source_target_pairs={{0,64},{1,65},{64,0},{65,1},{2,66},{3,67},{66,2},{67,3},{4,68},{5,... | collective-permute-start | bytes 2064392 | tf_op jit(solution)/shard_map/ppermute | solution.py:53
  77.8 18.1 %collective-permute-start.20 = (bf16[96,3584]{1,0:T(8,128)(2,1)S(1)}, bf16[96,3584]{1,0:T(8,128)(2,1)S(1)}, u32[]{:S(2)}, u32[]{:S(2)}) collective-permute-start(bf16[96,3584]{1,0:T(8,128)(2,1)S(1)} %get-tuple-element.44), channel_id=1, source_target_pairs={{0,65},{1,64},{64,1},{65,0},{2,67},{3,66},{66,3},{67,2},{4,69},{5,... | collective-permute-start | bytes 2064392 | tf_op jit(solution)/shard_map/ppermute | solution.py:53
